TPU v7x, 128 devices: a whole 4x4x4 slice. The times are simulated.
128 devices in a mesh: dp: 32 (over x, z, core), fsdp: 4 (over y).
Axes of the slice: x: 4, y: 4, z: 4, core: 2. Of those that a mesh axis runs over, the one named last changes fastest.
Arguments:
- tokens: bfloat16 [16384, 1024], P(('dp', 'fsdp')), may hold values from -6 to 6
- seq_lengths: int32 [256], replicated, may hold values from 1 to 127, as said below
- seq_owner: int32 [256], replicated, may hold values from 0 to 127, as said below
- input_norm: bfloat16 [1, 1024], P(None, ('dp', 'fsdp')), may hold values from 0.5 to 1.5
- gate_proj: bfloat16 [1, 1024, 1536], P(None, ('dp', 'fsdp')), may hold values from -0.1875 to 0.1875
- inner_proj: bfloat16 [1, 1024, 1792], P(None, ('dp', 'fsdp')), may hold values from -0.1875 to 0.1875
- step_proj: bfloat16 [1, 1024, 24], P(None, ('dp', 'fsdp')), may hold values from -0.1875 to 0.1875
- conv_weight: bfloat16 [1, 4, 1792], P(None, None, ('dp', 'fsdp')), may hold values from -0.5 to 0.5
- conv_bias: bfloat16 [1, 1792], P(None, ('dp', 'fsdp')), may hold values from -0.5 to 0.5
- step_bias: bfloat16 [1, 24], replicated, may hold values from -5 to -1
- decay_log: bfloat16 [1, 24], replicated, may hold values from 0 to 2.765625
- skip_gain: bfloat16 [1, 24], replicated, may hold values from 0.5 to 1.5
- mixer_norm: bfloat16 [1, 1536], P(None, ('dp', 'fsdp')), may hold values from 0.5 to 1.5
- mixer_out: bfloat16 [1, 1536, 1024], P(None, None, ('dp', 'fsdp')), may hold values from -0.15625 to 0.15625
- query_proj: bfloat16 [1, 1024, 512], P(None, ('dp', 'fsdp')), may hold values from -0.1875 to 0.1875
- keyval_proj: bfloat16 [1, 1024, 256], P(None, ('dp', 'fsdp')), may hold values from -0.1875 to 0.1875
- attn_out: bfloat16 [1, 512, 1024], P(None, None, ('dp', 'fsdp')), may hold values from -1.5 to 1.5
- ffn_norm: bfloat16 [1, 1024], P(None, ('dp', 'fsdp')), may hold values from 0.5 to 1.5
- gateup_proj: bfloat16 [1, 1024, 4096], P(None, ('dp', 'fsdp')), may hold values from -0.1875 to 0.1875
- down_proj: bfloat16 [1, 2048, 1024], P(None, None, ('dp', 'fsdp')), may hold values from -0.125 to 0.125
- out_grad: bfloat16 [16384, 1024], P(('dp', 'fsdp')), may hold values from -6 to 6
Outputs:
- result: bfloat16 [16384, 1024], P(('dp', 'fsdp'))
- tokens_grad: float32 [16384, 1024], P(('dp', 'fsdp'))
- input_norm_grad: float32 [1, 1024], P(None, ('dp', 'fsdp'))
- gate_proj_grad: float32 [1, 1024, 1536], P(None, ('dp', 'fsdp'))
- inner_proj_grad: float32 [1, 1024, 1792], P(None, ('dp', 'fsdp'))
- step_proj_grad: float32 [1, 1024, 24], P(None, ('dp', 'fsdp'))
- conv_weight_grad: float32 [1, 4, 1792], P(None, None, ('dp', 'fsdp'))
- conv_bias_grad: float32 [1, 1792], P(None, ('dp', 'fsdp'))
- step_bias_grad: float32 [1, 24], replicated
- decay_log_grad: float32 [1, 24], replicated
- skip_gain_grad: float32 [1, 24], replicated
- mixer_norm_grad: float32 [1, 1536], P(None, ('dp', 'fsdp'))
- mixer_out_grad: float32 [1, 1536, 1024], P(None, None, ('dp', 'fsdp'))
- query_proj_grad: float32 [1, 1024, 512], P(None, ('dp', 'fsdp'))
- keyval_proj_grad: float32 [1, 1024, 256], P(None, ('dp', 'fsdp'))
- attn_out_grad: float32 [1, 512, 1024], P(None, None, ('dp', 'fsdp'))
- ffn_norm_grad: float32 [1, 1024], P(None, ('dp', 'fsdp'))
- gateup_proj_grad: float32 [1, 1024, 4096], P(None, ('dp', 'fsdp'))
- down_proj_grad: float32 [1, 2048, 1024], P(None, None, ('dp', 'fsdp'))
Inputs may be any that keep to these rules, and one draw needn't show every extreme that they name: `seq_lengths`: the two sequences of a device hold at least 64 and at most 128 tokens together; some device holds exactly 128. `seq_owner`: every device owns exactly two sequences.
All inputs are finite; a program needn't handle non-finite values.
Results may differ from a plain program's by a relative error of at most 0.012.
Values may be sent and summed in bfloat16 or wider, within the bound.
A program may use at most 192 MiB of HBM per device.

v0:
```python
import math

import jax
import jax.numpy as jnp
from jax import lax
from jax.sharding import Mesh
from jax.sharding import PartitionSpec as P

QH = 8
KVH = 2
DP = ("dp_0", "dp_1", "dp_2")
DP_FSDP = ("dp_0", "dp_1", "dp_2", "fsdp")


EPSILON = 1e-05
ROPE_BASE = 100000000000.0


def in_one_piece(arrays, axis, dim, along):
    columns = [a.reshape(*a.shape[:along], -1) for a in arrays]
    both = jnp.concatenate(columns, axis=along)
    result, at, done = (lax.all_gather(both, axis, axis=dim, tiled=True), 0, [])
    for a, column in zip(arrays, columns):
        piece = result[..., at : at + column.shape[along]]
        done.append(piece.reshape(*piece.shape[:along], *a.shape[along:]))
        at += column.shape[along]
    return tuple(done)


def sent_together(arrays, axis, dim, along):
    widths = [a.shape[along] for a in arrays]
    both = jnp.concatenate(arrays, axis=along)
    result = lax.all_gather(both, axis, axis=dim, tiled=True)
    return tuple(jnp.split(result, [sum(widths[:k]) for k in range(1, len(widths))], axis=along))


def sent_together_2(arrays, axis, dim, along):
    columns = [a.reshape(*a.shape[:along], -1) for a in arrays]
    both = jnp.concatenate(columns, axis=along)
    result, at, done = (lax.psum_scatter(both, axis, scatter_dimension=dim, tiled=True), 0, [])
    for a, column in zip(arrays, columns):
        piece = result[..., at : at + column.shape[along]]
        done.append(piece.reshape(*piece.shape[:along], *a.shape[along:]))
        at += column.shape[along]
    return tuple(done)


def in_one_piece_2(arrays, axis, dim, along):
    ends, at = ([], 0)
    for a in arrays[:-1]:
        at += a.shape[along]
        ends.append(at)
    both = jnp.concatenate(arrays, axis=along)
    return tuple(
        jnp.split(lax.psum_scatter(both, axis, scatter_dimension=dim, tiled=True), ends, axis=along)
    )


def in_blocks(value, dim, length):
    dims = value.shape
    pieces = value.reshape(*dims[:dim], length, dims[dim] // length, *dims[dim + 1 :])
    return jnp.moveaxis(pieces, dim, 0)


def sum_at_owner(value, axis, dim):
    length = lax.axis_size(axis)
    pieces = lax.all_to_all(in_blocks(value, dim, length), axis, 0, 0, tiled=True)
    return jnp.sum(pieces, axis=0)


def side_by_side(arrays, axis, dim, along):
    columns = [a.reshape(*a.shape[:along], -1) for a in arrays]
    both = jnp.concatenate(columns, axis=along)
    result, at, done = (sum_at_owner(both, axis, dim), 0, [])
    for a, column in zip(arrays, columns):
        piece = result[..., at : at + column.shape[along]]
        done.append(piece.reshape(*piece.shape[:along], *a.shape[along:]))
        at += column.shape[along]
    return tuple(done)


def side_by_side_2(arrays, axis, dim, along):
    widths = [a.shape[along] for a in arrays]
    both = jnp.concatenate(arrays, axis=along)
    result = sum_at_owner(both, axis, dim)
    return tuple(jnp.split(result, [sum(widths[:k]) for k in range(1, len(widths))], axis=along))


def by_axis(value, axes):
    for axis in axes:
        value = lax.psum(value, axis)
    return value


def matmul_high(left_side, right_side):
    return jnp.dot(
        left_side, right_side, preferred_element_type=jnp.float32, precision=lax.Precision.HIGHEST
    )


def product_of(left_side, right_side):
    return jnp.dot(left_side, right_side, preferred_element_type=jnp.float32)


def across_rows(left_side, right_side):
    return lax.dot_general(
        left_side, right_side, (((0,), (0,)), ((), ())), preferred_element_type=jnp.float32
    )


def against_rows(left_side, right_side):
    return lax.dot_general(
        left_side, right_side, (((1,), (1,)), ((), ())), preferred_element_type=jnp.float32
    )


def rms_scale(values, gain):
    return values * lax.rsqrt(jnp.mean(values * values, axis=-1, keepdims=True) + EPSILON) * gain


def layout(device, seq_lengths, seq_owner, slot_count):
    owned = seq_owner == device
    own_lengths = jnp.where(owned, seq_lengths, 0)
    finish = jnp.cumsum(own_lengths, dtype=jnp.int32)
    slot_ids = jnp.arange(slot_count, dtype=jnp.int32)
    closed = owned[None, :] & (finish[None, :] <= slot_ids[:, None])
    segment = jnp.sum(closed.astype(jnp.int32), axis=1, dtype=jnp.int32)
    begins = jnp.max(jnp.where(closed, finish[None, :], 0), axis=1)
    active = slot_ids < jnp.sum(own_lengths, dtype=jnp.int32)
    return (segment, slot_ids - begins, active)


def rotate(values, position, head_count):
    row_count = values.shape[0]
    model_width = values.shape[1] // head_count
    half_width = model_width // 2
    ladder = jnp.arange(half_width, dtype=jnp.float32) * (2.0 / model_width)
    speeds = jnp.exp(-math.log(ROPE_BASE) * ladder)
    angles = position.astype(jnp.float32)[:, None] * speeds[None, :]
    cosine = jnp.cos(angles)[:, None, :]
    sine_part = jnp.sin(angles)[:, None, :]
    pieces = values.reshape(row_count, head_count, model_width)
    former = pieces[..., :half_width]
    latter = pieces[..., half_width:]
    turned = jnp.concatenate(
        [former * cosine - latter * sine_part, latter * cosine + former * sine_part], axis=-1
    )
    return turned.reshape(row_count, head_count * model_width)


def attend(queries, keys, values, segment):
    row_count = queries.shape[0]
    group_size = QH // KVH
    model_width = keys.shape[1] // KVH
    query_rank_four = queries.reshape(row_count, KVH, group_size, model_width)
    key_rank_three = keys.reshape(row_count, KVH, model_width)
    value_rank_three = values.reshape(row_count, KVH, model_width)
    attention_scores = jnp.einsum(
        "owhp,xwp->whox", query_rank_four, key_rank_three, precision=lax.Precision.HIGHEST
    ) * (1.0 / math.sqrt(model_width))
    slot_ids = jnp.arange(row_count)
    allowed = (segment[:, None] == segment[None, :]) & (slot_ids[:, None] >= slot_ids[None, :])
    attention_scores = jnp.where(allowed, attention_scores, -1e30)
    highest = jnp.max(attention_scores, axis=-1, keepdims=True)
    attention_weights = jnp.exp(attention_scores - highest)
    attention_weights = attention_weights / jnp.sum(attention_weights, axis=-1, keepdims=True)
    mixed_values = jnp.einsum(
        "qmaz,zqc->aqmc", attention_weights, value_rank_three, precision=lax.Precision.HIGHEST
    )
    return mixed_values.reshape(row_count, KVH * group_size * model_width)


def mamba_core(
    gate_in,
    conv_in,
    step_in,
    conv_taps,
    conv_shift,
    step_shift,
    decay_logs,
    skip_coef,
    gain,
    segment,
    position,
):
    row_count = conv_in.shape[0]
    inner = gate_in.shape[1]
    head_count = step_in.shape[1]
    state_size = (conv_in.shape[1] - inner) // 2
    kernel = conv_taps.shape[0]
    summed = conv_in * conv_taps[kernel - 1]
    for offset in range(1, kernel):
        moved = jnp.pad(conv_in, ((offset, 0), (0, 0)))[:row_count]
        summed = (
            summed
            + jnp.where((position >= offset)[:, None], moved, 0.0) * conv_taps[kernel - 1 - offset]
        )
    convolved = jax.nn.silu(summed + conv_shift)
    inputs_heads = convolved[:, :inner].reshape(row_count, head_count, inner // head_count)
    b_matrix = convolved[:, inner : inner + state_size]
    c_matrix = convolved[:, inner + state_size :]
    delta = jax.nn.softplus(step_in + step_shift)
    level = jnp.cumsum(delta * -jnp.exp(decay_logs), axis=0)
    slot_ids = jnp.arange(row_count)
    allowed = ((segment[:, None] == segment[None, :]) & (slot_ids[:, None] >= slot_ids[None, :]))[
        None
    ]
    spread = level.T[:, :, None] - level.T[:, None, :]
    decay = jnp.where(allowed, jnp.exp(jnp.where(allowed, spread, 0.0)), 0.0)
    intersection = matmul_high(c_matrix, b_matrix.T)
    mixing = decay * intersection[None] * delta.T[:, None, :]
    heads_out = jnp.einsum("hts,shp->thp", mixing, inputs_heads, precision=lax.Precision.HIGHEST)
    heads_out = heads_out + skip_coef[None, :, None] * inputs_heads
    gated = heads_out.reshape(row_count, inner) * jax.nn.silu(gate_in)
    return rms_scale(gated, gain)


def swiglu(joined):
    half_width = joined.shape[1] // 2
    return jax.nn.silu(joined[:, :half_width]) * joined[:, half_width:]


def fetch_forward(pieces):
    partial_set = (
        *in_one_piece((pieces[0], pieces[1], pieces[2], pieces[3]), "fsdp", 0, 1),
        lax.all_gather(pieces[4], "fsdp", axis=1, tiled=True),
        lax.all_gather(pieces[5], "fsdp", axis=0, tiled=True),
        lax.all_gather(pieces[6], "fsdp", axis=0, tiled=True),
        lax.all_gather(pieces[7], "fsdp", axis=1, tiled=True),
        *sent_together((pieces[8], pieces[9]), "fsdp", 0, 1),
        lax.all_gather(pieces[10], "fsdp", axis=1, tiled=True),
        *in_one_piece((pieces[11], pieces[12]), "fsdp", 0, 1),
        lax.all_gather(pieces[13], "fsdp", axis=1, tiled=True),
    )
    full = (
        *in_one_piece((partial_set[0], partial_set[1], partial_set[2], partial_set[3]), DP, 0, 1),
        lax.all_gather(partial_set[4], DP, axis=1, tiled=True),
        lax.all_gather(partial_set[5], DP, axis=0, tiled=True),
        lax.all_gather(partial_set[6], DP, axis=0, tiled=True),
        lax.all_gather(partial_set[7], DP, axis=1, tiled=True),
        *sent_together((partial_set[8], partial_set[9]), DP, 0, 1),
        lax.all_gather(partial_set[10], DP, axis=1, tiled=True),
        *in_one_piece((partial_set[11], partial_set[12]), DP, 0, 1),
        lax.all_gather(partial_set[13], DP, axis=1, tiled=True),
    )
    return full


def reduce_grads(terms):
    group_sums = (
        *sent_together_2((terms[0], terms[1], terms[2], terms[3]), DP, 0, 1),
        lax.psum_scatter(terms[4], DP, scatter_dimension=1, tiled=True),
        lax.psum_scatter(terms[5], DP, scatter_dimension=0, tiled=True),
        lax.psum_scatter(terms[6], DP, scatter_dimension=0, tiled=True),
        lax.psum_scatter(terms[7], DP, scatter_dimension=1, tiled=True),
        *in_one_piece_2((terms[8], terms[9]), DP, 0, 1),
        lax.psum_scatter(terms[10], DP, scatter_dimension=1, tiled=True),
        *sent_together_2((terms[11], terms[12]), DP, 0, 1),
        lax.psum_scatter(terms[13], DP, scatter_dimension=1, tiled=True),
    )
    shares = (
        *side_by_side((group_sums[0], group_sums[1], group_sums[2], group_sums[3]), "fsdp", 0, 1),
        sum_at_owner(group_sums[4], "fsdp", 1),
        sum_at_owner(group_sums[5], "fsdp", 0),
        sum_at_owner(group_sums[6], "fsdp", 0),
        sum_at_owner(group_sums[7], "fsdp", 1),
        *side_by_side_2((group_sums[8], group_sums[9]), "fsdp", 0, 1),
        sum_at_owner(group_sums[10], "fsdp", 1),
        *side_by_side((group_sums[11], group_sums[12]), "fsdp", 0, 1),
        sum_at_owner(group_sums[13], "fsdp", 1),
    )
    return shares


def forward_layer(stream, full, head_params, segment, position):
    (
        in_gain,
        gate_w,
        inner_w,
        step_w,
        conv_taps,
        conv_shift,
        mix_gain,
        mix_out_w,
        query_w,
        keyval_w,
        attn_w,
        ffn_gain,
        gateup_w,
        down_w,
    ) = full
    normed = rms_scale(stream, in_gain.astype(jnp.float32)).astype(jnp.bfloat16)
    mixer_inputs = (
        product_of(normed, gate_w),
        product_of(normed, inner_w),
        product_of(normed, step_w),
        conv_taps.astype(jnp.float32),
        conv_shift.astype(jnp.float32),
        head_params[0],
        head_params[1],
        head_params[2],
        mix_gain.astype(jnp.float32),
    )
    mixer_normed = mamba_core(*mixer_inputs, segment, position).astype(jnp.bfloat16)
    queries = product_of(normed, query_w)
    keyvals = product_of(normed, keyval_w)
    key_width = keyvals.shape[1] // 2
    query_turned = rotate(queries, position, QH).astype(jnp.bfloat16)
    key_turned = rotate(keyvals[:, :key_width], position, KVH).astype(jnp.bfloat16)
    value_low = keyvals[:, key_width:].astype(jnp.bfloat16)
    attended = attend(
        query_turned.astype(jnp.float32),
        key_turned.astype(jnp.float32),
        value_low.astype(jnp.float32),
        segment,
    ).astype(jnp.bfloat16)
    middle = stream + product_of(mixer_normed, mix_out_w) + product_of(attended, attn_w)
    ffn_in = rms_scale(middle, ffn_gain.astype(jnp.float32)).astype(jnp.bfloat16)
    gateup = product_of(ffn_in, gateup_w)
    activated = swiglu(gateup).astype(jnp.bfloat16)
    output = middle + product_of(activated, down_w)
    record = (
        stream,
        normed,
        mixer_inputs,
        mixer_normed,
        queries,
        keyvals,
        query_turned,
        key_turned,
        value_low,
        attended,
        middle,
        ffn_in,
        gateup,
        activated,
    )
    return (output, record)


def backward_layer(grad_out, record, full, segment, position):
    (
        stream,
        normed,
        mixer_inputs,
        mixer_normed,
        queries,
        keyvals,
        query_turned,
        key_turned,
        value_low,
        attended,
        middle,
        ffn_in,
        gateup,
        activated,
    ) = record
    (
        in_gain,
        gate_w,
        inner_w,
        step_w,
        conv_taps,
        conv_shift,
        mix_gain,
        mix_out_w,
        query_w,
        keyval_w,
        attn_w,
        ffn_gain,
        gateup_w,
        down_w,
    ) = full
    grad_low = grad_out.astype(jnp.bfloat16)
    down_grad = across_rows(activated, grad_low)
    act_grad = against_rows(grad_low, down_w)
    gateup_low = jax.vjp(swiglu, gateup)[1](act_grad)[0].astype(jnp.bfloat16)
    gateup_grad = across_rows(ffn_in, gateup_low)
    ffn_in_grad = against_rows(gateup_low, gateup_w)
    middle_part, ffn_gain_grad = jax.vjp(rms_scale, middle, ffn_gain.astype(jnp.float32))[1](
        ffn_in_grad
    )
    middle_grad = grad_out + middle_part
    branch_low = middle_grad.astype(jnp.bfloat16)
    attn_grad = across_rows(attended, branch_low)
    attended_grad = against_rows(branch_low, attn_w)

    def attention_only(query_in, key_in, value_in):
        return attend(query_in, key_in, value_in, segment)

    turned_query_grad, turned_key_grad, value_grad = jax.vjp(
        attention_only,
        query_turned.astype(jnp.float32),
        key_turned.astype(jnp.float32),
        value_low.astype(jnp.float32),
    )[1](attended_grad)
    key_width = keyvals.shape[1] // 2

    def turn_queries(inside):
        return rotate(inside, position, QH)

    def turn_keys(inside):
        return rotate(inside, position, KVH)

    query_low = jax.vjp(turn_queries, queries)[1](turned_query_grad)[0].astype(jnp.bfloat16)
    key_grad = jax.vjp(turn_keys, keyvals[:, :key_width])[1](turned_key_grad)[0]
    keyval_low = jnp.concatenate([key_grad, value_grad], axis=1).astype(jnp.bfloat16)
    mix_out_grad = across_rows(mixer_normed, branch_low)
    mixer_normed_grad = against_rows(branch_low, mix_out_w)

    def mixer_only(*inputs):
        return mamba_core(*inputs, segment, position)

    (
        gate_part,
        conv_part,
        step_part,
        taps_grad,
        shift_grad,
        bias_grad,
        decay_grad,
        skip_grad,
        mix_gain_grad,
    ) = jax.vjp(mixer_only, *mixer_inputs)[1](mixer_normed_grad)
    gate_low = gate_part.astype(jnp.bfloat16)
    conv_low = conv_part.astype(jnp.bfloat16)
    step_low = step_part.astype(jnp.bfloat16)
    normed_grad = (
        against_rows(gate_low, gate_w)
        + against_rows(conv_low, inner_w)
        + against_rows(step_low, step_w)
    )
    normed_grad = (
        normed_grad + against_rows(query_low, query_w) + against_rows(keyval_low, keyval_w)
    )
    stream_part, in_gain_grad = jax.vjp(rms_scale, stream, in_gain.astype(jnp.float32))[1](
        normed_grad
    )
    weight_terms = (
        in_gain_grad,
        across_rows(normed, gate_low),
        across_rows(normed, conv_low),
        across_rows(normed, step_low),
        taps_grad,
        shift_grad,
        mix_gain_grad,
        mix_out_grad,
        across_rows(normed, query_low),
        across_rows(normed, keyval_low),
        attn_grad,
        ffn_gain_grad,
        gateup_grad,
        down_grad,
    )
    return (middle_grad + stream_part, weight_terms, (bias_grad, decay_grad, skip_grad))


def body(
    tokens,
    seq_lengths,
    seq_owner,
    input_norm,
    gate_proj,
    inner_proj,
    step_proj,
    conv_weight,
    conv_bias,
    step_bias,
    decay_log,
    skip_gain,
    mixer_norm,
    mixer_out,
    query_proj,
    keyval_proj,
    attn_out,
    ffn_norm,
    gateup_proj,
    down_proj,
    out_grad,
):
    device = lax.axis_index(DP_FSDP)
    segment, position, active = layout(device, seq_lengths, seq_owner, tokens.shape[0])
    shards = (
        input_norm,
        gate_proj,
        inner_proj,
        step_proj,
        conv_weight,
        conv_bias,
        mixer_norm,
        mixer_out,
        query_proj,
        keyval_proj,
        attn_out,
        ffn_norm,
        gateup_proj,
        down_proj,
    )
    head_tables = (
        step_bias.astype(jnp.float32),
        decay_log.astype(jnp.float32),
        skip_gain.astype(jnp.float32),
    )
    layer_count = input_norm.shape[0]
    stream = tokens.astype(jnp.float32)
    layer = 0
    full = fetch_forward(tuple((member[layer] for member in shards)))
    head_params = tuple((member[layer] for member in head_tables))
    stream, record = forward_layer(stream, full, head_params, segment, position)
    records = [record]
    weights_kept = [full]
    result = stream.astype(jnp.bfloat16)
    grad_stream = out_grad.astype(jnp.float32) * active[:, None].astype(jnp.float32)
    shard_grads = [None] * layer_count
    head_grads = [None] * layer_count
    for layer in reversed(range(layer_count)):
        full = weights_kept[layer]
        grad_stream, weight_terms, head_terms = backward_layer(
            grad_stream, records[layer], full, segment, position
        )
        shard_grads[layer] = reduce_grads(weight_terms)
        head_grads[layer] = head_terms
    bias_total, decay_total, skip_total = (
        by_axis(jnp.stack([entry[0] for entry in head_grads]), DP_FSDP),
        by_axis(jnp.stack([entry[1] for entry in head_grads]), DP_FSDP),
        by_axis(jnp.stack([entry[2] for entry in head_grads]), DP_FSDP),
    )
    stacked = [jnp.stack([shard_grads[0][number]]) for number in range(14)]
    return (
        result,
        grad_stream,
        stacked[0],
        stacked[1],
        stacked[2],
        stacked[3],
        stacked[4],
        stacked[5],
        bias_total,
        decay_total,
        skip_total,
        stacked[6],
        stacked[7],
        stacked[8],
        stacked[9],
        stacked[10],
        stacked[11],
        stacked[12],
        stacked[13],
    )


def solution(mesh):
    split = Mesh(
        mesh.devices.reshape(4, 4, 2, mesh.shape["fsdp"]), ("dp_0", "dp_1", "dp_2", "fsdp")
    )
    in_specs = (
        P(DP_FSDP, None),
        P(),
        P(),
        P(None, DP_FSDP),
        P(None, DP_FSDP, None),
        P(None, DP_FSDP, None),
        P(None, DP_FSDP, None),
        P(None, None, DP_FSDP),
        P(None, DP_FSDP),
        P(),
        P(),
        P(),
        P(None, DP_FSDP),
        P(None, None, DP_FSDP),
        P(None, DP_FSDP, None),
        P(None, DP_FSDP, None),
        P(None, None, DP_FSDP),
        P(None, DP_FSDP),
        P(None, DP_FSDP, None),
        P(None, None, DP_FSDP),
        P(DP_FSDP, None),
    )
    out_specs = (
        P(DP_FSDP, None),
        P(DP_FSDP, None),
        P(None, DP_FSDP),
        P(None, DP_FSDP, None),
        P(None, DP_FSDP, None),
        P(None, DP_FSDP, None),
        P(None, None, DP_FSDP),
        P(None, DP_FSDP),
        P(),
        P(),
        P(),
        P(None, DP_FSDP),
        P(None, None, DP_FSDP),
        P(None, DP_FSDP, None),
        P(None, DP_FSDP, None),
        P(None, None, DP_FSDP),
        P(None, DP_FSDP),
        P(None, DP_FSDP, None),
        P(None, None, DP_FSDP),
    )
    return jax.shard_map(body, mesh=split, in_specs=in_specs, out_specs=out_specs, check_vma=False)
```

profile of v0, /device:TPU:0, one launch (start us, length us, event | category | flops | bytes accessed | tf_op | source)
XLA Modules:
  0.0 932.3 jit_solution(13423787492248796579)
XLA Ops:
  8.9 13.5 %all_gather.54 = bf16[32,3353]{1,0:T(8,128)(2,1)} all-gather(bf16[8,3353]{1,0:T(8,128)(2,1)S(1)} %concatenate.38), channel_id=1, replica_groups=mesh['dp_0'=4,'dp_1'=4,'dp_2'=2,'fsdp'=4] {'fsdp'}, dimensions={0}, use_global_device_ids=true | all-gather | bytes 268240 | tf_op jit(solution)/shard_map/all_gather | solution.py:22
  23.2 12.6 %all_gather.64 = bf16[32,768]{1,0:T(8,128)(2,1)} all-gather(bf16[8,768]{1,0:T(8,128)(2,1)S(1)} %pad_maximum_fusion.7), channel_id=1, replica_groups=mesh['dp_0'=4,'dp_1'=4,'dp_2'=2,'fsdp'=4] {'fsdp'}, dimensions={0}, use_global_device_ids=true | all-gather | bytes 61440 | tf_op jit(solution)/shard_map/all_gather | solution.py:33
  35.9 13.6 %all-gather.6 = bf16[1,1536,32]{1,2,0:T(8,128)(2,1)} all-gather(bf16[1,1536,8]{1,2,0:T(8,128)(2,1)} %param.34), channel_id=8, replica_groups=mesh['dp_0'=4,'dp_1'=4,'dp_2'=2,'fsdp'=4] {'fsdp'}, dimensions={2}, use_global_device_ids=true | all-gather | bytes 122880 | tf_op jit(solution)/shard_map/all_gather | solution.py:229
  49.6 12.9 %all-gather.8 = bf16[1,512,32]{1,2,0:T(8,128)(2,1)} all-gather(bf16[1,512,8]{1,2,0:T(8,128)(2,1)} %param.37), channel_id=10, replica_groups=mesh['dp_0'=4,'dp_1'=4,'dp_2'=2,'fsdp'=4] {'fsdp'}, dimensions={2}, use_global_device_ids=true | all-gather | bytes 40960 | tf_op jit(solution)/shard_map/all_gather | solution.py:231
  64.2 13.0 %all_gather.68 = bf16[32,4097]{1,0:T(8,128)(2,1)} all-gather(bf16[8,4097]{1,0:T(8,128)(2,1)S(1)} %pad_maximum_fusion.3), channel_id=1, replica_groups=mesh['dp_0'=4,'dp_1'=4,'dp_2'=2,'fsdp'=4] {'fsdp'}, dimensions={0}, use_global_device_ids=true | all-gather | bytes 327760 | tf_op jit(solution)/shard_map/all_gather | solution.py:22
  77.3 12.9 %all-gather.10 = bf16[1,2048,32]{1,2,0:T(8,128)(2,1)} all-gather(bf16[1,2048,8]{1,2,0:T(8,128)(2,1)} %param.40), channel_id=12, replica_groups=mesh['dp_0'=4,'dp_1'=4,'dp_2'=2,'fsdp'=4] {'fsdp'}, dimensions={2}, use_global_device_ids=true | all-gather | bytes 163840 | tf_op jit(solution)/shard_map/all_gather | solution.py:233
  99.1 9.5 %all-reduce.32 = (bf16[56]{0:T(256)(128)(2,1)S(1)}, bf16[48]{0:T(256)(128)(2,1)S(1)}) all-reduce(bf16[56]{0:T(256)(128)(2,1)S(1)} %dynamic-update-slice, bf16[48]{0:T(256)(128)(2,1)S(1)} %dynamic-update-slice.2), channel_id=4, replica_groups=mesh['dp_0'=4,'dp_1'=4,'dp_2'=2,'fsdp'=4] {'fsdp'}, use_global_device_ids=true, to_apply=%add.19 | all-reduce | flops 104 | bytes 416
  111.8 64.9 %all-reduce.31 = (bf16[1792]{0:T(1024)(128)(2,1)S(1)}, bf16[1536]{0:T(1024)(128)(2,1)S(1)}) all-reduce(bf16[1792]{0:T(1024)(128)(2,1)S(1)} %dynamic-update-slice.1, bf16[1536]{0:T(1024)(128)(2,1)S(1)} %dynamic-update-slice.3), channel_id=5, replica_groups=mesh['dp_0'=4,'dp_1'=4,'dp_2'=2,'fsdp'=4] {'dp_0','dp_1','dp_2'}, use_global_device_ids=true, to_apply=%add.20 | all-reduce | flops 3328 | bytes 13312
  177.4 11.9 %all-gather = bf16[1,4,56]{1,0,2:T(2,128)(2,1)S(1)} all-gather(bf16[1,4,14]{1,0,2:T(2,128)(2,1)S(1)} %copy.148), channel_id=2, replica_groups=mesh['dp_0'=4,'dp_1'=4,'dp_2'=2,'fsdp'=4] {'fsdp'}, dimensions={2}, use_global_device_ids=true | all-gather | bytes 560 | tf_op jit(solution)/shard_map/all_gather | solution.py:226
  189.4 22.0 %all-gather.1 = bf16[1,4,1792]{1,0,2:T(2,128)(2,1)S(1)} all-gather(bf16[1,4,56]{1,0,2:T(2,128)(2,1)S(1)} %all-gather), channel_id=3, replica_groups=mesh['dp_0'=4,'dp_1'=4,'dp_2'=2,'fsdp'=4] {'dp_0','dp_1','dp_2'}, dimensions={2}, use_global_device_ids=true | all-gather | bytes 14784 | tf_op jit(solution)/shard_map/all_gather | solution.py:237
  214.2 38.0 %slice_reduce_fusion.3 = (f32[1792]{0:T(1024)S(1)}, f32[1792]{0:T(1024)S(1)}, f32[1792]{0:T(1024)S(1)}, f32[1792]{0:T(1024)S(1)}) fusion(f32[1,4,1792]{1,0,2:T(1,128)S(1)} %convert_element_type.174), kind=kLoop, calls=%fused_computation.87 | loop fusion | bytes 57344 | tf_op jit(solution)/shard_map/slice | solution.py:191
  254.9 3.6 fusion.10
  265.2 5.6 fusion.36
  274.6 4.3 multiply_reduce_fusion.9
  287.3 7.7 fusion.2
  295.0 19.3 %all-gather.29.cloned.1.call-done = bf16[1,2048,1024]{1,2,0:T(8,128)(2,1)} async-done(((bf16[1,2048,32]{1,2,0:T(8,128)(2,1)}), bf16[1,2048,1024]{1,2,0:T(8,128)(2,1)}) %all-gather.29.cloned.1.call-update) | async-done | bytes 4194320 | tf_op jit(solution)/shard_map/all_gather | solution.py:244
  314.2 4.8 fusion.116
  319.1 8.5 multiply_reduce_fusion.10
  338.7 3.5 copy.186
  342.9 3.6 fusion.157
  347.6 5.3 fusion.117
  364.6 5.2 fusion.73
  376.4 4.0 fusion.8
  380.4 3.6 fusion.39
  386.6 3.8 fusion.164
  390.4 4.2 fusion.162
  394.6 17.4 %concatenate.44 = f32[1024,3353]{1,0:T(8,128)} concatenate(f32[1024,1]{1,0:T(8,128)S(1)} %copy.167, f32[1024,1536]{1,0:T(8,128)} %fusion.164, f32[1024,1792]{1,0:T(8,128)} %fusion.162, f32[1024,24]{1,0:T(8,128)S(1)} %fusion.140), dimensions={1} | concatenate | bytes 27467776 | tf_op jit(solution)/shard_map/concatenate | solution.py:39
  412.9 4.0 fusion.113
  416.9 7.7 pad_maximum_fusion
  426.1 126.7 %all-reduce.26 = (f32[4,1792]{1,0:T(4,128)S(1)}, f32[1792]{0:T(1024)S(1)}, f32[1536]{0:T(1024)S(1)}) all-reduce(f32[4,1792]{1,0:T(4,128)S(1)} %pad_add_fusion, f32[1792]{0:T(1024)S(1)} %get-tuple-element.31, f32[1536]{0:T(1024)S(1)} %get-tuple-element.27), channel_id=15, replica_groups=mesh['dp_0'=4,'dp_1'=4,'dp_2'=2,'fsdp'=4] {'dp_0','dp_1','dp_2'}, use_global_device_ids=true, to_apply=%region_29.30.clone | all-reduce | flops 10496 | bytes 83968
  553.6 4.3 all-to-all-start.3
  558.6 4.4 all-to-all-done.3
  566.4 5.0 all-to-all-done.2
  571.4 7.6 all_to_all.53
  582.5 4.5 fusion.49
  588.1 3.6 all-to-all-start.5
  591.9 7.7 all-reduce.29
  599.7 7.7 all-reduce.28
  609.9 11.4 %all-reduce.27 = (f32[1,24]{1,0:T(1,128)}, f32[1,24]{1,0:T(1,128)}, f32[1,24]{1,0:T(1,128)}) all-reduce(f32[1,24]{1,0:T(1,128)S(1)} %get-tuple-element.54, f32[1,24]{1,0:T(1,128)S(1)} %get-tuple-element.55, f32[1,24]{1,0:T(1,128)S(1)} %get-tuple-element.56), channel_id=1, replica_groups=mesh['dp_0'=4,'dp_1'=4,'dp_2'=2,'fsdp'=4] {'fsdp'}, use_global_device_ids=true, to_apply=%region_38.39 | all-reduce | flops 72 | bytes 576 | tf_op jit(solution)/shard_map/psum | solution.py:91
  624.7 6.3 all-to-all-done.4
  631.0 47.5 %reduce-scatter.18.cloned.1.call-done = f32[2048,32]{0,1:T(8,128)} async-done(((f32[2048,1024]{0,1:T(8,128)}), f32[2048,32]{0,1:T(8,128)}) %reduce-scatter.18.cloned.1.call-update) | async-done | bytes 262160 | tf_op jit(solution)/shard_map/reduce_scatter | solution.py:259
  678.5 4.3 all-to-all-start.8
  689.5 101.3 %reduce-scatter.10.cloned.1.call-done = f32[32,3353]{1,0:T(8,128)} async-done(((f32[1024,3353]{1,0:T(8,128)}), f32[32,3353]{1,0:T(8,128)}) %reduce-scatter.10.cloned.1.call-update) | async-done | bytes 429200 | tf_op jit(solution)/shard_map/reduce_scatter | solution.py:40
  790.7 4.3 all-to-all-start
  797.5 5.2 all-to-all-done
  804.6 106.5 %reduce-scatter.16.cloned.1.call-done = f32[32,4097]{1,0:T(8,128)} async-done(((f32[1024,4097]{1,0:T(8,128)}), f32[32,4097]{1,0:T(8,128)}) %reduce-scatter.16.cloned.1.call-update) | async-done | bytes 524432 | tf_op jit(solution)/shard_map/reduce_scatter | solution.py:40
  911.1 4.3 all-to-all-start.7
  916.1 7.8 all-to-all-done.7
  (379 shorter events, 100.9 us)
Async XLA Ops:
  7.2 206.8 %copy-start.88 = (bf16[1,24]{1,0:T(2,128)(2,1)S(1)}, bf16[1,24]{1,0:T(2,128)(2,1)}, u32[]{:S(2)}) copy-start(bf16[1,24]{1,0:T(2,128)(2,1)} %param.30) | copy-start | bytes 148
  7.2 206.8 %copy-start.90 = (bf16[1,24]{1,0:T(2,128)(2,1)S(1)}, bf16[1,24]{1,0:T(2,128)(2,1)}, u32[]{:S(2)}) copy-start(bf16[1,24]{1,0:T(2,128)(2,1)} %param.31) | copy-start | bytes 148
  7.2 206.8 %copy-start.89 = (bf16[1,24]{1,0:T(2,128)(2,1)S(1)}, bf16[1,24]{1,0:T(2,128)(2,1)}, u32[]{:S(2)}) copy-start(bf16[1,24]{1,0:T(2,128)(2,1)} %param.32) | copy-start | bytes 148
  7.2 245.1 %all-gather.19.cloned.1.call-start = ((), (), s32[]{:S(2)}) async-start(), calls=%async_computation.15 | async-start | bytes 7299072 | tf_op jit(solution)/shard_map/all_gather | solution.py:22
  22.4 231.0 %all-gather.21.cloned.1.call-start = ((), (), s32[]{:S(2)}) async-start(), calls=%async_computation.16 | async-start | bytes 1622016 | tf_op jit(solution)/shard_map/all_gather | solution.py:33
  35.8 244.2 %all-gather.25.cloned.1.call-start = ((), (), s32[]{:S(2)}) async-start(), calls=%async_computation.23 | async-start | bytes 3244032 | tf_op jit(solution)/shard_map/all_gather | solution.py:240
  49.5 233.6 %all-gather.27.cloned.1.call-start = ((), (), s32[]{:S(2)}) async-start(), calls=%async_computation.24 | async-start | bytes 1081344 | tf_op jit(solution)/shard_map/all_gather | solution.py:242
  62.4 223.7 %all-gather.23.cloned.1.call-start = ((), (), s32[]{:S(2)}) async-start(), calls=%async_computation.17 | async-start | bytes 8921088 | tf_op jit(solution)/shard_map/all_gather | solution.py:22
  77.2 237.0 %all-gather.29.cloned.1.call-start = ((), (), s32[]{:S(2)}) async-start(), calls=%async_computation.25 | async-start | bytes 4325376 | tf_op jit(solution)/shard_map/all_gather | solution.py:244
  90.2 488.8 %reduce-scatter.14.cloned.1.call-start = ((), (), s32[]{:S(2)}) async-start(), calls=%async_computation.20 | async-start | bytes 2162688 | tf_op jit(solution)/shard_map/reduce_scatter | solution.py:257
  94.0 180.6 %copy-start.62 = (f32[128]{0:T(128)}, f32[128]{0:T(128)S(1)}, u32[]{:S(2)}) copy-start(f32[128]{0:T(128)S(1)} %fusion.143) | copy-start | bytes 1540
  97.5 167.7 %copy-start.58 = (pred[128,128]{1,0:T(8,128)(4,1)}, pred[128,128]{1,0:T(8,128)(4,1)S(1)}, u32[]{:S(2)}) copy-start(pred[128,128]{1,0:T(8,128)(4,1)S(1)} %get-tuple-element.97) | copy-start | bytes 49156
  211.4 42.1 %copy-start = (bf16[128,1024]{1,0:T(8,128)(2,1)S(1)}, bf16[128,1024]{1,0:T(8,128)(2,1)}, u32[]{:S(2)}) copy-start(bf16[128,1024]{1,0:T(8,128)(2,1)} %param.21) | copy-start | bytes 786436
  212.8 66.2 %copy-start.21 = (pred[128,128]{0,1:T(8,128)(4,1)}, pred[128,128]{0,1:T(8,128)(4,1)S(1)}, u32[]{:S(2)}) copy-start(pred[128,128]{0,1:T(8,128)(4,1)S(1)} %copy.155) | copy-start | bytes 49156
  214.0 50.0 %copy-start.82 = (f32[24]{0:T(128)}, f32[24]{0:T(128)S(1)}, u32[]{:S(2)}) copy-start(f32[24]{0:T(128)S(1)} %negate_bitcast_fusion) | copy-start | bytes 292
  214.0 51.2 %copy-start.94 = (f32[24]{0:T(128)}, f32[24]{0:T(128)S(1)}, u32[]{:S(2)}) copy-start(f32[24]{0:T(128)S(1)} %bitcast_convert_fusion) | copy-start | bytes 292
  214.0 44.5 %copy-start.71 = (pred[128]{0:T(512)(128)(4,1)}, pred[128]{0:T(512)(128)(4,1)S(1)}, u32[]{:S(2)}) copy-start(pred[128]{0:T(512)(128)(4,1)S(1)} %get-tuple-element.98) | copy-start | bytes 388
  214.0 44.5 %copy-start.73 = (pred[128]{0:T(512)(128)(4,1)}, pred[128]{0:T(512)(128)(4,1)S(1)}, u32[]{:S(2)}) copy-start(pred[128]{0:T(512)(128)(4,1)S(1)} %get-tuple-element.99) | copy-start | bytes 388
  214.1 44.5 %copy-start.75 = (pred[128]{0:T(512)(128)(4,1)}, pred[128]{0:T(512)(128)(4,1)S(1)}, u32[]{:S(2)}) copy-start(pred[128]{0:T(512)(128)(4,1)S(1)} %get-tuple-element.100) | copy-start | bytes 388
  214.2 59.9 %copy-start.24 = (f32[128,32]{0,1:T(8,128)}, f32[128,32]{0,1:T(8,128)S(1)}, u32[]{:S(2)}) copy-start(f32[128,32]{0,1:T(8,128)S(1)} %get-tuple-element.92) | copy-start | bytes 49156
  214.2 59.9 %copy-start.27 = (f32[128,32]{0,1:T(8,128)}, f32[128,32]{0,1:T(8,128)S(1)}, u32[]{:S(2)}) copy-start(f32[128,32]{0,1:T(8,128)S(1)} %get-tuple-element.93) | copy-start | bytes 49156
  262.5 10.8 %slice-start = ((f32[128,256]{1,0:T(8,128)}), f32[128,128]{1,0:T(8,128)S(1)}, s32[]{:S(2)}) async-start(f32[128,256]{1,0:T(8,128)} %copy-done.32), calls=%async_computation.27 | async-start | bytes 131072 | tf_op jit(solution)/shard_map/slice | solution.py:309
  262.5 10.9 %copy-start.8 = (bf16[1024,768]{1,0:T(8,128)(2,1)S(1)}, bf16[1024,768]{1,0:T(8,128)(2,1)}, u32[]{:S(2)}) copy-start(bf16[1024,768]{1,0:T(8,128)(2,1)} %all-gather.21.cloned.1.call-done) | copy-start | bytes 4718596
  264.0 10.0 %copy-start.96 = (f32[24,128]{1,0:T(8,128)}, f32[24,128]{1,0:T(8,128)S(1)}, u32[]{:S(2)}) copy-start(f32[24,128]{1,0:T(8,128)S(1)} %get-tuple-element.101) | copy-start | bytes 36868
  264.9 9.1 copy-start.69
  274.6 10.9 %copy-start.52 = (f32[2,4,128]{2,1,0:T(4,128)}, f32[2,4,128]{2,1,0:T(4,128)S(1)}, u32[]{:S(2)}) copy-start(f32[2,4,128]{2,1,0:T(4,128)S(1)} %fusion.112) | copy-start | bytes 12292
  285.5 33.5 %copy-start.77 = (f32[128]{0:T(128)}, f32[128]{0:T(128)S(1)}, u32[]{:S(2)}) copy-start(f32[128]{0:T(128)S(1)} %fusion.145) | copy-start | bytes 1540
  287.2 27.0 %copy-start.16 = (bf16[128,1024]{1,0:T(8,128)(2,1)S(1)}, bf16[128,1024]{1,0:T(8,128)(2,1)}, u32[]{:S(2)}) copy-start(bf16[128,1024]{1,0:T(8,128)(2,1)} %param.41) | copy-start | bytes 786436
  287.3 27.0 %copy-start.80 = (f32[128]{0:T(128)S(1)}, f32[128]{0:T(128)}, u32[]{:S(2)}) copy-start(f32[128]{0:T(128)} %compare_convert_fusion) | copy-start | bytes 1540
  319.1 10.2 %copy-start.20 = (bf16[2,64,4,128]{3,1,2,0:T(8,128)(2,1)S(1)}, bf16[2,64,4,128]{3,1,2,0:T(8,128)(2,1)}, u32[]{:S(2)}) copy-start(bf16[2,64,4,128]{3,1,2,0:T(8,128)(2,1)} %convolution_convert_fusion) | copy-start | bytes 393220
  331.2 256.9 %reduce-scatter.20.cloned.1.call-start = ((), (), s32[]{:S(2)}) async-start(), calls=%async_computation.26 | async-start | bytes 3244032 | tf_op jit(solution)/shard_map/reduce_scatter | solution.py:55
  342.3 279.0 %reduce-scatter.12.cloned.1.call-start = ((), (), s32[]{:S(2)}) async-start(), calls=%async_computation.19 | async-start | bytes 6488064 | tf_op jit(solution)/shard_map/reduce_scatter | solution.py:255
  346.6 331.9 %reduce-scatter.18.cloned.1.call-start = ((), (), s32[]{:S(2)}) async-start(), calls=%async_computation.22 | async-start | bytes 8650752 | tf_op jit(solution)/shard_map/reduce_scatter | solution.py:259
  352.9 437.8 %reduce-scatter.10.cloned.1.call-start = ((), (), s32[]{:S(2)}) async-start(), calls=%async_computation.18 | async-start | bytes 14598144 | tf_op jit(solution)/shard_map/reduce_scatter | solution.py:40
  364.5 8.6 copy-start.2
  412.0 499.1 %reduce-scatter.16.cloned.1.call-start = ((), (), s32[]{:S(2)}) async-start(), calls=%async_computation.21 | async-start | bytes 17842176 | tf_op jit(solution)/shard_map/reduce_scatter | solution.py:40
  424.6 157.9 %copy-start.6 = (bf16[128,2048]{1,0:T(8,128)(2,1)S(1)}, bf16[128,2048]{1,0:T(8,128)(2,1)}, u32[]{:S(2)}) copy-start(bf16[128,2048]{1,0:T(8,128)(2,1)} %get-tuple-element.77) | copy-start | bytes 1572868
  424.6 167.1 %copy-start.91 = (bf16[1,24]{1,0:T(2,128)(2,1)S(1)}, bf16[1,24]{1,0:T(2,128)(2,1)}, u32[]{:S(2)}) copy-start(bf16[1,24]{1,0:T(2,128)(2,1)} %param.31) | copy-start | bytes 148
  553.6 9.5 %all-to-all-start.3 = ((f32[4,1,12]{2,1,0:T(1,128)}), f32[4,1,12]{2,1,0:T(1,128)S(1)}, u32[]{:S(2)}, u32[]{:S(2)}) async-start(f32[4,1,12]{2,1,0:T(1,128)} %bitcast.81), calls=%async_computation.4 | async-start | bytes 4096 | tf_op jit(solution)/shard_map/all_to_all | solution.py:67
  563.0 8.4 all-to-all-start.2
  579.1 45.6 %copy-start.85 = (f32[128]{0:T(128)S(1)}, f32[128]{0:T(128)}, u32[]{:S(2)}) copy-start(f32[128]{0:T(128)} %copy-done.84) | copy-start | bytes 1540
  579.1 9.0 all-to-all-start.6
  582.5 100.3 %copy-start.7 = (f32[128,1024]{1,0:T(8,128)S(1)}, f32[128,1024]{1,0:T(8,128)}, u32[]{:S(2)}) copy-start(f32[128,1024]{1,0:T(8,128)} %get-tuple-element.67) | copy-start | bytes 1572868
  588.1 33.2 %all-to-all-start.5 = ((f32[4,8,768]{2,1,0:T(8,128)}), f32[4,8,768]{2,1,0:T(8,128)S(1)}, u32[]{:S(2)}, u32[]{:S(2)}) async-start(f32[4,8,768]{2,1,0:T(8,128)} %bitcast.274), calls=%async_computation.7 | async-start | bytes 196608 | tf_op jit(solution)/shard_map/all_to_all | solution.py:67
  621.3 9.7 %all-to-all-start.4 = ((f32[4,1536,8]{1,2,0:T(8,128)}), f32[4,1536,8]{1,2,0:T(8,128)S(1)}, u32[]{:S(2)}, u32[]{:S(2)}) async-start(f32[4,1536,8]{1,2,0:T(8,128)} %bitcast.268), calls=%async_computation.6 | async-start | bytes 393216 | tf_op jit(solution)/shard_map/all_to_all | solution.py:67
  678.5 11.0 %all-to-all-start.8 = ((f32[4,2048,8]{1,2,0:T(8,128)}), f32[4,2048,8]{1,2,0:T(8,128)S(1)}, u32[]{:S(2)}, u32[]{:S(2)}) async-start(f32[4,2048,8]{1,2,0:T(8,128)} %bitcast.264), calls=%async_computation.13 | async-start | bytes 524288 | tf_op jit(solution)/shard_map/all_to_all | solution.py:67
  790.7 11.9 %all-to-all-start = ((f32[4,8,3353]{2,1,0:T(8,128)}), f32[4,8,3353]{2,1,0:T(8,128)S(1)}, u32[]{:S(2)}, u32[]{:S(2)}) async-start(f32[4,8,3353]{2,1,0:T(8,128)} %bitcast.261), calls=%async_computation.1 | async-start | bytes 884736 | tf_op jit(solution)/shard_map/all_to_all | solution.py:67
  911.1 12.8 %all-to-all-start.7 = ((f32[4,8,4097]{2,1,0:T(8,128)}), f32[4,8,4097]{2,1,0:T(8,128)S(1)}, u32[]{:S(2)}, u32[]{:S(2)}) async-start(f32[4,8,4097]{2,1,0:T(8,128)} %bitcast.258), calls=%async_computation.11 | async-start | bytes 1081344 | tf_op jit(solution)/shard_map/all_to_all | solution.py:67
  (71 other events, 286.5 us)
Sparse Core Ops, SparseCore 0:
  22.6 52.3 all-gather.18
  77.2 42.3 all-gather.20
  121.8 44.3 all-gather.24
  168.4 42.8 all-gather.26
  213.3 52.8 all-gather.22
  268.3 45.8 all-gather.28
  331.3 78.2 reduce-scatter.13
  413.2 79.7 reduce-scatter.19
  497.2 85.5 reduce-scatter.11
  586.4 92.0 reduce-scatter.17
  682.9 107.7 reduce-scatter.9
  794.5 116.5 reduce-scatter.15
where the time goes:
time: 939 us; the launch traced here: 932 us
  blocking collectives  351 us (37%)
  waiting for transfers between devices  308 us (33%)
  matrix products  98.7 us (11%)
  local copies, waits for them, and re-layouts  87.2 us (9%)
  other arithmetic  36.2 us (4%)
  starting transfers between devices  31.5 us (3%)
  between operations  20 us (2%)
    reduce_scatter x2, waiting for transfers between devices, sent_together_2(): lax.psum_scatter(both, axis, scatter_dimension=dim, tiled=True)  208 us
    unnamed x3, blocking collectives  201 us
    reduce_scatter x1, waiting for transfers between devices, reduce_grads(): lax.psum_scatter(terms[13], DP, scatter_dimension=1, tiled=True)  47.5 us
    slice x1, local copies, waits for them, and re-layouts, mamba_core(): summed = conv_in * conv_taps[kernel - 1]  38 us
    all_to_all x8, waiting for transfers between devices, sum_at_owner(): lax.all_to_all(in_blocks(value, dim, length), axis, 0, 0, tiled=True)  33.1 us
    all_to_all x8, starting transfers between devices, sum_at_owner(): lax.all_to_all(in_blocks(value, dim, length), axis, 0, 0, tiled=True)  30.8 us
    psum x4, blocking collectives, by_axis(): value = lax.psum(value, axis)  29.4 us
    dot_general x9, matrix products, against_rows(): lax.dot_general(left_side, right_side, (((1,), (1,)), ((), ())), preferre...  28.7 us
  transfers between devices with their start and end apart: 20, of which 11 were waited for; matrix products, arithmetic and copies ran while one was open for 21% of the time, Pallas kernels for 0%

commit v1 on v0

v1 whole, which is shorter than its diff:
```python
import functools
import math

import jax
import jax.numpy as jnp
from jax import lax
from jax.experimental import pallas as pl
from jax.experimental.pallas import tpu as pltpu
from jax.sharding import Mesh
from jax.sharding import PartitionSpec as P

EPSILON = 1e-05
ROPE_BASE = 100000000000.0
DP_FSDP = ("dp_0", "dp_1", "dp_2", "fsdp")
AX, AZ, AC, AY = "dp_0", "dp_1", "dp_2", "fsdp"
ORDERS = ((AX, AY, AZ), (AY, AZ, AX), (AZ, AX, AY))
MESH = pl.DeviceIdType.MESH


def places():
    return {a: lax.axis_index(a) for a in (AX, AZ, AC, AY)}


def greet(at):
    barrier = pltpu.get_barrier_semaphore()
    for a in (AX, AZ, AY):
        for d in (1, 3):
            pl.semaphore_signal(barrier, inc=1, device_id={a: lax.rem(at[a] + d, 4)}, device_id_type=MESH)
    pl.semaphore_signal(barrier, inc=1, device_id={AC: 1 - at[AC]}, device_id_type=MESH)
    pl.semaphore_wait(barrier, 7)


def cut3(cols, start=0):
    tiles = cols // 128
    sizes = [tiles // 3 + (1 if k < tiles % 3 else 0) for k in range(3)]
    parts, at = [], start
    for n in sizes:
        lo = (n + 1) // 2 * 128
        parts.append((at, lo, n * 128 - lo))
        at += n * 128
    return parts


def gather_kernel(parts, shard, out, send, recv, sib_send, sib_recv, own_sem):
    at = places()
    greet(at)
    whole = slice(None)
    core = at[AC]

    def block(sel, c0, n):
        return out.at[sel[AX], sel[AZ], core, sel[AY], :, pl.ds(c0, n)]

    own = pltpu.make_async_copy(shard, out.at[at[AX], at[AZ], core, at[AY]], own_sem)
    own.start()
    pending_sib, sent = [], []

    def to_sibling(part, k, sel, c0, n):
        ref = block(sel, c0, n)
        c = pltpu.make_async_remote_copy(ref, ref, sib_send.at[part, k], sib_recv.at[part, k],
                                         device_id={AC: 1 - core}, device_id_type=MESH)
        c.start()
        pending_sib.append(c)

    for phase in range(3):
        state = []
        for part, (c0, lo, hi) in enumerate(parts):
            order = ORDERS[part]
            a = order[phase]
            p = at[a]
            nxt, prv, opp = lax.rem(p + 1, 4), lax.rem(p + 3, 4), lax.rem(p + 2, 4)
            base = {b: at[b] for b in (AX, AZ, AY)}
            for b in order[:phase]:
                base[b] = whole

            def mk(kind, q, cc, n, to, part=part, a=a, base=base):
                dst = block({**base, a: q}, cc, n)
                src = shard.at[:, pl.ds(cc, n)] if (phase == 0 and kind < 4) else dst
                return pltpu.make_async_remote_copy(src, dst, send.at[part, phase, kind], recv.at[part, phase, kind],
                                                    device_id={a: to}, device_id_type=MESH)
            r_lo, l_hi = mk(0, p, c0, lo, nxt), mk(1, p, c0 + lo, hi, prv)
            r_hi, l_lo = mk(2, p, c0 + lo, hi, nxt), mk(3, p, c0, lo, prv)
            for c in (r_lo, l_hi, r_hi, l_lo):
                c.start()
            sent += [r_lo, l_hi, r_hi, l_lo]
            if phase == 2:
                to_sibling(part, 0, {**base}, c0, lo + hi)
            state.append((r_lo, l_hi, r_hi, l_lo, mk, nxt, prv, opp, base, a, c0, lo, hi))
        fwd = []
        for s in state:
            r_lo, l_hi, r_hi, l_lo, mk, nxt, prv, opp, base, a, c0, lo, hi = s
            r_lo.wait_recv()
            fr = mk(4, prv, c0, lo, nxt)
            fr.start()
            l_hi.wait_recv()
            fl = mk(5, nxt, c0 + lo, hi, prv)
            fl.start()
            fwd.append((fr, fl))
            sent += [fr, fl]
        for part, s in enumerate(state):
            r_lo, l_hi, r_hi, l_lo, mk, nxt, prv, opp, base, a, c0, lo, hi = s
            r_hi.wait_recv()
            if phase == 2:
                to_sibling(part, 1, {**base, a: prv}, c0, lo + hi)
            l_lo.wait_recv()
            if phase == 2:
                to_sibling(part, 2, {**base, a: nxt}, c0, lo + hi)
        for part, s in enumerate(state):
            r_lo, l_hi, r_hi, l_lo, mk, nxt, prv, opp, base, a, c0, lo, hi = s
            fr, fl = fwd[part]
            fr.wait_recv()
            if phase == 2:
                to_sibling(part, 3, {**base, a: opp}, c0, lo)
            fl.wait_recv()
            if phase == 2:
                to_sibling(part, 4, {**base, a: opp}, c0 + lo, hi)
        if phase == 0:
            own.wait()
    for c in sent:
        c.wait_send()
    for c in pending_sib:
        c.wait()


def gather(shard, space=pl.ANY, cid=0):
    cols = shard.shape[1]
    parts = cut3(cols)
    return pl.pallas_call(
        functools.partial(gather_kernel, parts),
        out_shape=jax.ShapeDtypeStruct((4, 4, 2, 4, 8, cols), jnp.bfloat16),
        in_specs=[pl.BlockSpec(memory_space=pltpu.VMEM)],
        out_specs=pl.BlockSpec(memory_space=space),
        scratch_shapes=[
            pltpu.SemaphoreType.DMA((3, 3, 6)), pltpu.SemaphoreType.DMA((3, 3, 6)),
            pltpu.SemaphoreType.DMA((3, 5)), pltpu.SemaphoreType.DMA((3, 5)), pltpu.SemaphoreType.DMA,
        ],
        compiler_params=pltpu.CompilerParams(collective_id=cid, has_side_effects=True, vmem_limit_bytes=60 << 20),
        name="gather",
    )(shard)


def shapes_of(phase, cols):
    return (4,) * (2 - phase) + (8, cols)


OFF = dict(gate=(0, 1536), inner=(1536, 1792), query=(3328, 512), keyval=(3840, 256), step=(4096, 128),
           mix=(4224, 1536), attn=(5760, 512), gateup=(6272, 4096), down=(10368, 2048))
COLS = 12416
FIRST = 4224
F32, BF16 = jnp.float32, jnp.bfloat16
HIGH = lax.Precision.HIGHEST


def nn(a, b, precision=None):
    return lax.dot_general(a, b, (((1,), (0,)), ((), ())), preferred_element_type=F32, precision=precision)


def nt(a, b, precision=None):
    return lax.dot_general(a, b, (((1,), (1,)), ((), ())), preferred_element_type=F32, precision=precision)


def tn(a, b, precision=None):
    return lax.dot_general(a, b, (((0,), (0,)), ((), ())), preferred_element_type=F32, precision=precision)


def sigmoid(v):
    return 1.0 / (1.0 + jnp.exp(-v))


def cols_of(i, n, start=0):
    return pl.ds(pl.multiple_of(start + i * n, 128), n)


def rms_back(values, scale, gain, grad):
    inner = grad * gain
    mean = jnp.mean(values * inner, axis=-1, keepdims=True)
    return scale * inner - values * (scale * scale * scale * mean), jnp.sum(grad * values * scale, axis=0, keepdims=True)


def row_scale(values):
    return lax.rsqrt(jnp.mean(values * values, axis=-1, keepdims=True) + EPSILON)


def layer_kernel(x_ref, og_ref, segc, segr, pos, act, cos, sin, w_hbm, gin, gffn, gmix, taps, cbias, sbias, dlog, skipx,
                 result, dx, rt, z, gin_g, gffn_g, gmix_g, taps_g, cbias_g, head_g, skip_g,
                 wv, proj, csum, conv, yfull, dec, soft, qr, x1_s, df_s, dm_s, do_s, dconv, ddt_s, wsem):
    groups = ((0, FIRST), (4224, 2048), (6272, 4096), (10368, 2048))
    loads = []
    for k, (c0, n) in enumerate(groups):
        c = pltpu.make_async_copy(w_hbm.at[:, pl.ds(c0, n)], wv.at[:, pl.ds(c0, n)], wsem.at[k])
        c.start()
        loads.append(c)

    lane = lax.broadcasted_iota(jnp.int32, (128, 128), 1)
    sub = lax.broadcasted_iota(jnp.int32, (128, 128), 0)
    low_lanes = lane < 64
    allowed = (segc[...] == segr[...]) & (sub >= lane)
    position = pos[...]

    def halves(v):
        return jnp.where(low_lanes, v, 0.0), jnp.where(low_lanes, 0.0, v)

    def stacked(v):
        lo, hi = halves(v)
        return jnp.concatenate([lo, hi], axis=0).astype(BF16)

    x = x_ref[...].astype(F32)
    h = (x * row_scale(x) * gin[...]).astype(BF16)
    rt[0:1024, :] = h.T
    g0 = og_ref[...].astype(F32) * act[...]
    glow = g0.astype(BF16)
    rt[3072:4096, :] = glow.T
    z_h = h
    loads[0].wait()

    def project(i, carry):
        proj[:, cols_of(i, 384)] = nn(z_h, wv[:, cols_of(i, 384)])
        return carry
    lax.fori_loop(0, 11, project, 0)

    def convolve(i, carry):
        cs = cols_of(i, 128)
        p = proj[:, cols_of(i, 128, 1536)]
        total = p * taps[3:4, cs]
        for j in (1, 2, 3):
            moved = jnp.where(position >= j, pltpu.roll(p, j, axis=0), 0.0)
            total = total + moved * taps[3 - j:4 - j, cs]
        total = total + cbias[:, cs]
        csum[:, cs] = total
        conv[:, cs] = total * sigmoid(total)
        return carry
    lax.fori_loop(0, 14, convolve, 0)

    step = proj[:, 4096:4224] + sbias[...]
    dt = jnp.maximum(step, 0.0) + jnp.log(1.0 + jnp.exp(-jnp.abs(step)))
    rate = -jnp.exp(dlog[...])
    lower = (sub >= lane).astype(F32)
    level = nn(lower, dt * rate, HIGH)
    dt_t = dt.T
    level_t = level.T
    b_mat = conv[:, 1536:1664]
    c_mat = conv[:, 1664:1792]
    inter = nt(c_mat, b_mat, HIGH)

    square = jnp.zeros((128, 1), F32)
    for t in range(12):
        cs = slice(128 * t, 128 * t + 128)
        mixes = []
        for n in (2 * t, 2 * t + 1):
            spread = jnp.where(allowed, level[:, n:n + 1] - level_t[n:n + 1, :], -1e30)
            decay = jnp.exp(spread)
            dec[n] = decay
            mixes.append((decay * inter * dt_t[n:n + 1, :]).astype(BF16))
        xs = conv[:, cs]
        y = nn(jnp.concatenate(mixes, axis=1), stacked(xs)) + skipx[:, cs] * xs
        yfull[:, cs] = y
        gate = proj[:, cs]
        gy = y * (gate * sigmoid(gate))
        square = square + jnp.sum(gy * gy, axis=1, keepdims=True)
    rmix = lax.rsqrt(square * (1.0 / 1536) + EPSILON)

    def mixer_norm(i, carry):
        cs = cols_of(i, 128)
        gate = proj[:, cs]
        gy = yfull[:, cs] * (gate * sigmoid(gate))
        z[:, cols_of(i, 128, 4224)] = (gy * rmix * gmix[:, cs]).astype(BF16)
        return carry
    lax.fori_loop(0, 12, mixer_norm, 0)

    cosine, sine = cos[...], sin[...]
    first = (lane % 64) < 32

    def turn(v, sign):
        side = jnp.where(first, -pltpu.roll(v, 96, axis=1), pltpu.roll(v, 32, axis=1))
        return v * cosine + sign * side * sine

    def dup(v, j):
        other = pltpu.roll(v, 64, axis=1)
        return jnp.where(low_lanes, v, other) if j == 0 else jnp.where(low_lanes, other, v)
    key_t = turn(proj[:, 3840:3968], 1.0).astype(BF16).astype(F32)
    val = proj[:, 3968:4096].astype(BF16).astype(F32)
    keys = [dup(key_t, j) for j in (0, 1)]
    vals = [dup(val, j) for j in (0, 1)]
    for t in range(4):
        cs = slice(128 * t, 128 * t + 128)
        q = turn(proj[:, 3328 + 128 * t:3456 + 128 * t], 1.0).astype(BF16).astype(F32)
        qr[:, cs] = q
        scores = nt(stacked(q), keys[t // 2].astype(BF16)) * 0.125
        weights = []
        for e in (0, 1):
            s = jnp.where(allowed, scores[128 * e:128 * e + 128], -1e30)
            w = jnp.exp(s - jnp.max(s, axis=1, keepdims=True))
            w = w / jnp.sum(w, axis=1, keepdims=True)
            soft[2 * t + e] = w
            weights.append(w.astype(BF16))
        z[:, 5760 + 128 * t:5888 + 128 * t] = nn(jnp.concatenate(weights, axis=1), stacked(vals[t // 2])).astype(BF16)

    loads[1].wait()
    for i in range(4):
        rows = slice(256 * i, 256 * i + 256)
        x1_s[:, rows] = x_ref[:, rows].astype(F32) + nt(z[:, 4224:6272], wv[rows, 4224:6272])
    x1 = x1_s[...]
    r1 = row_scale(x1)
    f = (x1 * r1 * gffn[...]).astype(BF16)
    rt[2048:3072, :] = f.T

    loads[2].wait()
    loads[3].wait()

    def feed(i, carry):
        g = nn(f, wv[:, cols_of(i, 256, 6272)])
        u = nn(f, wv[:, cols_of(i, 256, 8320)])
        da = nn(glow, wv[:, cols_of(i, 256, 10368)])
        s = sigmoid(g)
        gs = g * s
        z[:, cols_of(i, 256, 10368)] = (gs * u).astype(BF16)
        z[:, cols_of(i, 256, 6272)] = (da * u * (s + gs * (1.0 - s))).astype(BF16)
        z[:, cols_of(i, 256, 8320)] = (da * gs).astype(BF16)
        return carry
    lax.fori_loop(0, 8, feed, 0)
    for i in range(4):
        rows = slice(256 * i, 256 * i + 256)
        result[:, rows] = (x1_s[:, rows] + nt(z[:, 10368:12416], wv[rows, 10368:12416])).astype(BF16)
        df_s[:, rows] = nt(z[:, 6272:10368], wv[rows, 6272:10368])
    part, gain_grad = rms_back(x1, r1, gffn[...], df_s[...])
    gffn_g[...] = gain_grad
    dx1 = g0 + part
    x1_s[...] = dx1
    blow = dx1.astype(BF16)
    rt[1024:2048, :] = blow.T

    def back_branch(i, carry):
        dm_s[:, cols_of(i, 512)] = nn(blow, wv[:, cols_of(i, 512, 4224)])
        return carry
    lax.fori_loop(0, 3, back_branch, 0)
    do_s[...] = nn(blow, wv[:, 5760:6272])

    dks, dvs = [], []
    for t in range(4):
        cs = slice(128 * t, 128 * t + 128)
        do2 = stacked(do_s[:, cs])
        dp = nt(do2, vals[t // 2].astype(BF16))
        ds, ws = [], []
        for e in (0, 1):
            w = soft[2 * t + e]
            d = dp[128 * e:128 * e + 128]
            ds.append((w * (d - jnp.sum(d * w, axis=1, keepdims=True)) * 0.125).astype(BF16))
            ws.append(w.astype(BF16))
        dq = nn(jnp.concatenate(ds, axis=1), stacked(keys[t // 2]))
        z[:, 3328 + 128 * t:3456 + 128 * t] = turn(dq, -1.0).astype(BF16)
        dks.append(tn(jnp.concatenate(ds, axis=0), stacked(qr[:, cs])))
        dvs.append(tn(jnp.concatenate(ws, axis=0), do2))

    def fold(parts):
        a, b = parts[0] + parts[1], parts[2] + parts[3]
        return jnp.where(low_lanes, a + pltpu.roll(a, 64, axis=1), b + pltpu.roll(b, 64, axis=1))
    z[:, 3840:3968] = turn(fold(dks), -1.0).astype(BF16)
    z[:, 3968:4096] = fold(dvs).astype(BF16)

    dots = jnp.zeros((128, 1), F32)
    for t in range(12):
        cs = slice(128 * t, 128 * t + 128)
        gate = proj[:, cs]
        gy = yfull[:, cs] * (gate * sigmoid(gate))
        dm = dm_s[:, cs]
        gmix_g[:, cs] = jnp.sum(dm * gy * rmix, axis=0, keepdims=True)
        dots = dots + jnp.sum(gy * dm * gmix[:, cs], axis=1, keepdims=True)
    pull = rmix * rmix * rmix * dots * (1.0 / 1536)
    ddt_s[...] = jnp.zeros((128, 128), F32)
    dlevel = jnp.zeros((128, 128), F32)
    dinter = jnp.zeros((128, 128), F32)
    for t in range(12):
        cs = slice(128 * t, 128 * t + 128)
        gate = proj[:, cs]
        s = sigmoid(gate)
        gs = gate * s
        y = yfull[:, cs]
        dgy = rmix * (gmix[:, cs] * dm_s[:, cs]) - y * gs * pull
        z[:, cs] = (dgy * y * (s + gs * (1.0 - s))).astype(BF16)
        dy = dgy * gs
        xs = conv[:, cs]
        skip_g[:, cs] = jnp.sum(dy * xs, axis=0, keepdims=True)
        dy2 = stacked(dy)
        dmix = nt(dy2, xs.astype(BF16))
        mixes = []
        for e in (0, 1):
            n = 2 * t + e
            dt_row = dt_t[n:n + 1, :]
            decay = dec[n]
            mixed = decay * inter
            dm = dmix[128 * e:128 * e + 128]
            mixes.append((mixed * dt_row).astype(BF16))
            dd = dm * dt_row
            dinter = dinter + dd * decay
            ddt_s[n:n + 1, :] = jnp.sum(dm * mixed, axis=0, keepdims=True)
            dlevel = dlevel + jnp.where(lane == n, jnp.sum(dd * mixed, axis=1, keepdims=True), 0.0)
        dconv[:, cs] = tn(jnp.concatenate(mixes, axis=0), dy2) + skipx[:, cs] * dy
    dconv[:, 1536:1664] = tn(dinter, c_mat, HIGH)
    dconv[:, 1664:1792] = nn(dinter, b_mat, HIGH)
    ddt = ddt_s[...].T
    dlevel = dlevel - ddt * dt
    upper = (sub <= lane).astype(F32)
    drate = nn(upper, dlevel, HIGH)
    dstep = jnp.where(lane < 24, (ddt + drate * rate) * sigmoid(step), 0.0)
    z[:, 4096:4224] = dstep.astype(BF16)
    head_g[0:1, :] = jnp.sum(dstep, axis=0, keepdims=True)
    head_g[1:2, :] = jnp.sum(drate * dt * rate, axis=0, keepdims=True)

    def unconvolve(i, carry):
        cs = cols_of(i, 128)
        total = csum[:, cs]
        s = sigmoid(total)
        d = dconv[:, cs] * (s + total * s * (1.0 - s))
        p = proj[:, cols_of(i, 128, 1536)]
        cbias_g[:, cs] = jnp.sum(d, axis=0, keepdims=True)
        taps_g[3:4, cs] = jnp.sum(d * p, axis=0, keepdims=True)
        back = d * taps[3:4, cs]
        for j in (1, 2, 3):
            masked = jnp.where(position >= j, d, 0.0)
            taps_g[3 - j:4 - j, cs] = jnp.sum(masked * pltpu.roll(p, j, axis=0), axis=0, keepdims=True)
            back = back + pltpu.roll(masked, 128 - j, axis=0) * taps[3 - j:4 - j, cs]
        z[:, cols_of(i, 128, 1536)] = back.astype(BF16)
        return carry
    lax.fori_loop(0, 14, unconvolve, 0)

    for i in range(4):
        rows = slice(256 * i, 256 * i + 256)
        df_s[:, rows] = nt(z[:, 0:FIRST], wv[rows, 0:FIRST])
    x = x_ref[...].astype(F32)
    part, gain_grad = rms_back(x, row_scale(x), gin[...], df_s[...])
    gin_g[...] = gain_grad
    dx[...] = x1_s[...] + part


def layer_call(*args):
    def of(*s, t=F32):
        return jax.ShapeDtypeStruct(s, t)
    vm = pl.BlockSpec(memory_space=pltpu.VMEM)
    specs = [vm] * 17
    specs[8] = pl.BlockSpec(memory_space=pl.ANY)
    return pl.pallas_call(
        layer_kernel,
        out_shape=(of(128, 1024, t=BF16), of(128, 1024), of(4096, 128, t=BF16), of(128, COLS, t=BF16), of(1, 1024),
                   of(1, 1024), of(1, 1536), of(4, 1792), of(1, 1792), of(8, 128), of(1, 1536)),
        in_specs=specs,
        out_specs=[vm] * 11,
        scratch_shapes=[
            pltpu.VMEM((1024, COLS), BF16), pltpu.VMEM((128, FIRST), F32), pltpu.VMEM((128, 1792), F32),
            pltpu.VMEM((128, 1792), F32), pltpu.VMEM((128, 1536), F32), pltpu.VMEM((24, 128, 128), F32),
            pltpu.VMEM((8, 128, 128), F32), pltpu.VMEM((128, 512), F32), pltpu.VMEM((128, 1024), F32),
            pltpu.VMEM((128, 1024), F32), pltpu.VMEM((128, 1536), F32), pltpu.VMEM((128, 512), F32),
            pltpu.VMEM((128, 1792), F32), pltpu.VMEM((128, 128), F32), pltpu.SemaphoreType.DMA((4,)),
        ],
        compiler_params=pltpu.CompilerParams(vmem_limit_bytes=60 << 20),
        cost_estimate=pl.CostEstimate(flops=6_500_000_000, bytes_accessed=30_000_000, transcendentals=3_000_000),
        name="layer",
    )(*args)


def layout(device, seq_lengths, seq_owner, slot_count):
    owned = seq_owner == device
    own_lengths = jnp.where(owned, seq_lengths, 0)
    finish = jnp.cumsum(own_lengths, dtype=jnp.int32)
    slot_ids = jnp.arange(slot_count, dtype=jnp.int32)
    closed = owned[None, :] & (finish[None, :] <= slot_ids[:, None])
    segment = jnp.sum(closed.astype(jnp.int32), axis=1, dtype=jnp.int32)
    begins = jnp.max(jnp.where(closed, finish[None, :], 0), axis=1)
    active = slot_ids < jnp.sum(own_lengths, dtype=jnp.int32)
    return (segment, slot_ids - begins, active)


def turn_tables(position):
    ladder = jnp.arange(32, dtype=jnp.float32) * (2.0 / 64)
    speeds = jnp.exp(-math.log(ROPE_BASE) * ladder)
    angles = position.astype(jnp.float32)[:, None] * jnp.tile(speeds, 4)[None, :]
    return jnp.cos(angles), jnp.sin(angles)


def pack_smalls(mixer, taps, bias):
    k = mixer.shape[0]
    flat = jnp.concatenate([mixer, taps.reshape(k, 56), bias, jnp.zeros((k, 6), mixer.dtype)], axis=1)
    return flat.reshape(k * 8, 11)


def unpack_smalls(table):
    k = table.shape[0] // 8
    flat = table.reshape(k, 88)
    return flat[:, :12], flat[:, 12:68].reshape(k, 4, 14), flat[:, 68:82]


def row_of(values, width=128):
    return jnp.pad(values.astype(F32), ((0, 0), (0, width - values.shape[1])))


def layer_inputs(tokens, out_grad, segment, position, active, weights, step_bias, decay_log, skip_gain):
    smalls = weights[:, 4120:4133].astype(F32)
    mixer, taps, bias = unpack_smalls(smalls[:, 2:])
    cosine, sine = turn_tables(position)
    return (tokens, out_grad, segment[:, None], segment[None, :], position[:, None], active[:, None].astype(F32),
            cosine, sine, weights, smalls[:, 0][None], smalls[:, 1][None], mixer.reshape(1, 1536),
            jnp.moveaxis(taps, 1, 0).reshape(4, 1792), bias.reshape(1, 1792), row_of(step_bias), row_of(decay_log),
            jnp.repeat(skip_gain.astype(F32), 64, axis=1))


def small_table(gin_g, gffn_g, gmix_g, taps_g, cbias_g):
    smalls = pack_smalls(gmix_g.reshape(128, 12), jnp.moveaxis(taps_g.reshape(4, 128, 14), 0, 1), cbias_g.reshape(128, 14))
    return jnp.concatenate([jnp.zeros((1024, 24), F32), gin_g.reshape(1024, 1), gffn_g.reshape(1024, 1), smalls,
                            jnp.zeros((1024, 91), F32)], axis=1)


PIECES = (((0, 0, 4224, 384),), ((1, 4224, 2048, 256), (2, 6272, 2048, 256)), ((2, 8320, 2048, 256), (3, 10368, 2048, 256)))


def reduce_kernel(parts, rt, z, small, out, grad, z_sib, rt_sib, small_sib, *scratch):
    bufs, (send, recv, x_send, x_recv) = scratch[:-4], scratch[-4:]
    at = places()
    greet(at)
    whole = slice(None)
    core = at[AC]
    swaps = []

    def swap(k, src, dst):
        c = pltpu.make_async_remote_copy(src, dst, x_send.at[k], x_recv.at[k], device_id={AC: 1 - core}, device_id_type=MESH)
        c.start()
        swaps.append(c)
    swap(0, rt.at[:, :, 1 - core], rt_sib)
    for part, (c0, lo, hi) in enumerate(parts):
        swap(1 + part, z.at[:, pl.ds(c0, lo + hi)], z_sib.at[:, pl.ds(c0, lo + hi)])
        if part == 0:
            swap(4, small.at[:, 1 - core], small_sib)

    def products(part):
        for g, c0, n, width in PIECES[part]:
            left = jnp.concatenate([rt[g, :, core].reshape(512, 128), rt_sib[g].reshape(512, 128)], axis=1)

            def one(i, carry, c0=c0, width=width, left=left):
                cs = pl.ds(pl.multiple_of(c0 + i * width, 128), width)
                right = jnp.concatenate([z[:, cs], z_sib[:, cs]], axis=0)
                v = lax.dot_general(left, right, (((1,), (0,)), ((), ())), preferred_element_type=F32)
                grad[:, :, :, :, cs] = v.reshape(4, 4, 4, 8, width).astype(BF16)
                return carry
            lax.fori_loop(0, n // width, one, 0)

    sent = []
    for phase in range(3):
        state = []
        for part, (c0, lo, hi) in enumerate(parts):
            order = ORDERS[part][::-1]
            a = order[phase]
            p = at[a]
            nxt, prv, opp = lax.rem(p + 1, 4), lax.rem(p + 3, 4), lax.rem(p + 2, 4)
            base = {b: at[b] for b in (AX, AZ, AY)}
            for b in order[phase + 1:]:
                base[b] = whole
            el, er, fr, fl = bufs[(part * 3 + phase) * 4:(part * 3 + phase) * 4 + 4]

            def ref(q, cc, n, base=base, a=a):
                sel = {**base, a: q}
                return grad.at[sel[AX], sel[AZ], sel[AY], :, pl.ds(cc, n)]

            def mk(kind, q, cc, n, dst, to, part=part, a=a, ref=ref):
                return pltpu.make_async_remote_copy(ref(q, cc, n), dst, send.at[part, phase, kind],
                                                    recv.at[part, phase, kind], device_id={a: to}, device_id_type=MESH)
            if phase == 0:
                if part == 0:
                    swaps[0].wait_recv()
                    swaps[1].wait_recv()
                    swaps[2].wait_recv()
                else:
                    swaps[2 + part].wait_recv()
                products(part)
                if part == 0:
                    tile = grad.at[:, :, :, :, pl.ds(4096, 128)]
                    extra = small[:, core] + small_sib[...]
                    tile[...] = (tile[...].astype(F32) + extra.reshape(4, 4, 4, 8, 128)).astype(BF16)
            lead = (whole,) * (2 - phase) + (whole,)
            fr_lo, fr_hi = fr.at[lead + (pl.ds(0, lo),)], fr.at[lead + (pl.ds(lo, hi),)]
            fl_lo, fl_hi = fl.at[lead + (pl.ds(0, lo),)], fl.at[lead + (pl.ds(lo, hi),)]
            e_l = mk(0, opp, c0, lo, el, prv)
            e_r = mk(1, opp, c0 + lo, hi, er, nxt)
            d_l_hi = mk(2, prv, c0 + lo, hi, fr_hi, prv)
            d_r_lo = mk(3, nxt, c0, lo, fl_lo, nxt)
            for c in (e_l, e_r, d_l_hi, d_r_lo):
                c.start()
            d_l_lo = mk(4, prv, c0, lo, fr_lo, prv)
            d_r_hi = mk(5, nxt, c0 + lo, hi, fl_hi, nxt)
            sent += [e_l, e_r, d_l_hi, d_r_lo, d_l_lo, d_r_hi]
            state.append((e_l, e_r, d_l_hi, d_r_lo, d_l_lo, d_r_hi, ref, nxt, prv, p, c0, lo, hi, el, er, fr, fl))

        def each(fn):
            n = 2 - phase
            if n == 2:
                def outer(k, carry):
                    fn((k // 4, k % 4))
                    return carry
                lax.fori_loop(0, 16, outer, 0)
            elif n == 1:
                def outer(k, carry):
                    fn((k,))
                    return carry
                lax.fori_loop(0, 4, outer, 0)
            else:
                fn(())

        for s in state:
            e_l, e_r, d_l_hi, d_r_lo, d_l_lo, d_r_hi, ref, nxt, prv, p, c0, lo, hi, el, er, fr, fl = s
            e_l.wait_recv()

            def add_lo(ix, t=ref(prv, c0, lo), e=el):
                ix = ix + (whole, whole)
                t[ix] = t[ix] + e[ix]
            each(add_lo)
            d_l_lo.start()
            e_r.wait_recv()

            def add_hi(ix, t=ref(nxt, c0 + lo, hi), e=er):
                ix = ix + (whole, whole)
                t[ix] = t[ix] + e[ix]
            each(add_hi)
            d_r_hi.start()
        for part, s in enumerate(state):
            e_l, e_r, d_l_hi, d_r_lo, d_l_lo, d_r_hi, ref, nxt, prv, p, c0, lo, hi, el, er, fr, fl = s
            for c in (d_l_hi, d_r_lo, d_l_lo, d_r_hi):
                c.wait_recv()

            def total(ix, t=ref(p, c0, lo + hi), l=fl, r=fr):
                ix = ix + (whole, whole)
                v = t[ix].astype(F32) + l[ix].astype(F32) + r[ix].astype(F32)
                if phase == 2:
                    out[:, pl.ds(c0, lo + hi)] = v
                else:
                    t[ix] = v.astype(BF16)
            each(total)
    for c in sent:
        c.wait_send()
    for c in swaps:
        c.wait_send()


def shapes_of(phase, cols):
    return (4,) * (2 - phase) + (8, cols)


def reduce_call(rt, z, small):
    parts = cut3(COLS)
    bufs = []
    for c0, lo, hi in parts:
        for phase in range(3):
            for n in (lo, hi, lo + hi, lo + hi):
                bufs.append(pltpu.VMEM(shapes_of(phase, n), BF16))
    vm = pl.BlockSpec(memory_space=pltpu.VMEM)
    return pl.pallas_call(
        functools.partial(reduce_kernel, parts),
        out_shape=jax.ShapeDtypeStruct((8, COLS), F32),
        in_specs=[vm] * 3,
        out_specs=vm,
        scratch_shapes=[pltpu.VMEM((4, 4, 4, 8, COLS), BF16), pltpu.VMEM((128, COLS), BF16),
                        pltpu.VMEM((4, 16, 32, 128), BF16), pltpu.VMEM((16, 32, 128), F32)] + bufs + [
            pltpu.SemaphoreType.DMA((3, 3, 6)), pltpu.SemaphoreType.DMA((3, 3, 6)),
            pltpu.SemaphoreType.DMA((5,)), pltpu.SemaphoreType.DMA((5,))],
        compiler_params=pltpu.CompilerParams(collective_id=1, has_side_effects=True, vmem_limit_bytes=60 << 20),
        name="reduce",
    )(rt, z, small)


def body(tokens, seq_lengths, seq_owner, input_norm, gate_proj, inner_proj, step_proj, conv_weight, conv_bias, step_bias,
         decay_log, skip_gain, mixer_norm, mixer_out, query_proj, keyval_proj, attn_out, ffn_norm, gateup_proj, down_proj,
         out_grad):
    device = lax.axis_index(DP_FSDP)
    segment, position, active = layout(device, seq_lengths, seq_owner, tokens.shape[0])
    smalls = pack_smalls(mixer_norm, conv_weight, conv_bias)
    shard = jnp.concatenate(
        [gate_proj[0], inner_proj[0], query_proj[0], keyval_proj[0], step_proj[0], input_norm.reshape(8, 1),
         ffn_norm.reshape(8, 1), smalls, jnp.zeros((8, 91), BF16), mixer_out[0].T, attn_out[0].T, gateup_proj[0],
         down_proj[0].T], axis=1)
    weights = gather(shard).reshape(1024, COLS)
    inputs = layer_inputs(tokens, out_grad, segment, position, active, weights, step_bias, decay_log, skip_gain)
    result, dx, rt, z, gin_g, gffn_g, gmix_g, taps_g, cbias_g, head_g, skip_g = layer_call(*inputs)
    table = small_table(gin_g, gffn_g, gmix_g, taps_g, cbias_g)
    heads = jnp.concatenate([head_g[0, :24], head_g[1, :24], jnp.sum(skip_g.reshape(24, 64), axis=1)])
    heads = lax.psum(heads, DP_FSDP).reshape(3, 1, 24)
    grads = reduce_call(rt.reshape(4, 16, 2, 32, 128), z, table.reshape(16, 2, 32, 128))
    mixer_g, conv_g, bias_g = unpack_smalls(grads[:, 4122:4133])

    def cols(name):
        start, n = OFF[name]
        return grads[:, start:start + n]
    return (
        result, dx, grads[:, 4120].reshape(1, 8), cols("gate")[None], cols("inner")[None], grads[None, :, 4096:4120],
        conv_g, bias_g, heads[0], heads[1], heads[2], mixer_g, cols("mix").T[None], cols("query")[None],
        cols("keyval")[None], cols("attn").T[None], grads[:, 4121].reshape(1, 8), cols("gateup")[None],
        cols("down").T[None],
    )


def solution(mesh):
    split = Mesh(mesh.devices.reshape(4, 4, 2, mesh.shape["fsdp"]), DP_FSDP)
    rows, flat = P(DP_FSDP, None), P(None, DP_FSDP)
    weight, turned = P(None, DP_FSDP, None), P(None, None, DP_FSDP)
    in_specs = (rows, P(), P(), flat, weight, weight, weight, turned, flat, P(), P(), P(), flat, turned, weight, weight,
                turned, flat, weight, turned, rows)
    out_specs = (rows, rows, flat, weight, weight, weight, turned, flat, P(), P(), P(), flat, turned, weight, weight,
                 turned, flat, weight, turned)
    return jax.shard_map(body, mesh=split, in_specs=in_specs, out_specs=out_specs, check_vma=False)
```

time: 939 us -> 286 us (0.30)
  waiting for transfers between devices: 308 us -> 0 us
  blocking collectives: 351 us -> 65.6 us
  Pallas kernels: 0 us -> 176 us
  matrix products: 98.7 us -> 0 us
  local copies, waits for them, and re-layouts: 87.2 us -> 29.6 us
  starting transfers between devices: 31.5 us -> 0 us
  other arithmetic: 36.2 us -> 13 us
  between operations: 20 us -> 0.9 us
    reduce_scatter x6 -> x0, waiting for transfers between devices: 255 us -> none  [the longest x2 208 us: sent_together_2(): lax.psum_scatter(both, axis, scatter_dimension=dim, tiled=True)]
    unnamed x3 -> x0, blocking collectives: 201 us -> none
    pallas_call x0 -> x3, Pallas kernels: none -> 176 us  [the longest x1 74.8 us: reduce_call(): pl.pallas_call(functools.partial(reduce_kernel, parts), out_shape=jax.Sha...]
    all_gather x8 -> x0, blocking collectives: 113 us -> none  [the longest x2 26.6 us: in_one_piece(): result, at, done = (lax.all_gather(both, axis, axis=dim, tiled=True), 0, [])]
    dot_general x39 -> x0, matrix products: 98.7 us -> none  [the longest x9 28.7 us: against_rows(): lax.dot_general(left_side, right_side, (((1,), (1,)), ((), ())), preferre...]
    slice x11 -> x10, local copies, waits for them, and re-layouts: 40.8 us -> 4.45 us  [the longest x1 1.47 us: body(): grads[:, 4121].reshape(1, 8)]
    psum x4 -> x1, blocking collectives: 29.4 us -> 65.6 us  [body(): heads = lax.psum(heads, DP_FSDP).reshape(3, 1, 24)]
    all_to_all x8 -> x0, waiting for transfers between devices: 33.1 us -> none  [sum_at_owner(): lax.all_to_all(in_blocks(value, dim, length), axis, 0, 0, tiled=True)]
  transfers between devices with their start and end apart: 20 -> 0, of which waited for: 11 -> 0; matrix products, arithmetic and copies ran while one was open for 21% -> 0% of each run, Pallas kernels for 0% -> 0%
where the time goes in v1:
time: 286 us; the launch traced here: 285 us
  Pallas kernels  176 us (62%)
  blocking collectives  65.6 us (23%)
  local copies, waits for them, and re-layouts  29.6 us (10%)
  other arithmetic  13 us (5%)
    pallas_call x1, Pallas kernels, reduce_call(): pl.pallas_call(functools.partial(reduce_kernel, parts), out_shape=jax.Sha...  74.8 us
    pallas_call x1, Pallas kernels, gather(): pl.pallas_call(functools.partial(gather_kernel, parts), out_shape=jax.Sha...  68.4 us
    psum x1, blocking collectives, body(): heads = lax.psum(heads, DP_FSDP).reshape(3, 1, 24)  65.6 us
    pallas_call x1, Pallas kernels, layer_call(): pl.pallas_call(layer_kernel, out_shape=(of(128, 1024, t=BF16), of(128, 10...  32.4 us

profile of v1, /device:TPU:0, one launch (start us, length us, event | category | flops | bytes accessed | tf_op | source)
XLA Modules:
  0.0 284.6 jit_solution(3425584075436802790)
XLA Ops:
  0.7 1.3 select_reduce_fusion.1
  2.0 0.7 select_bitcast_fusion
  2.7 0.3 reduce-window.9
  3.6 1.0 multiply_sine_fusion
  4.7 0.6 iota_subtract_fusion.pos
  5.3 0.7 copy.63.segc
  6.0 1.3 fusion.1.act
  7.3 0.8 reshape.179
  8.1 0.8 fusion.2
  8.9 0.7 copy.59
  9.7 0.7 copy.60
  10.4 1.7 concatenate.23.shard
  12.1 68.4 %gather.1 = bf16[4,4,2,4,8,12416]{5,4,3,2,1,0:T(8,128)(2,1)} custom-call(bf16[8,12416]{1,0:T(8,128)(2,1)} %concatenate.23.shard), custom_call_target="tpu_custom_call" | custom-call | tf_op jit(solution)/shard_map/gather/pallas_call | solution.py:127
  80.5 1.1 slice_convert_fusion
  81.6 0.2 slice.123
  82.3 0.8 reshape.185.taps
  83.2 0.7 reshape.186.cbias
  83.9 0.7 reshape.183.gmix
  84.6 1.1 slice_reduce_fusion
  85.7 0.5 pad_convert_fusion
  86.3 0.7 broadcast_in_dim.77.skipx
  87.0 32.4 %layer.1 = (bf16[128,1024]{1,0:T(8,128)(2,1)}, f32[128,1024]{1,0:T(8,128)}, bf16[4096,128]{1,0:T(8,128)(2,1)}, bf16[128,12416]{1,0:T(8,128)(2,1)}, f32[1,1024]{1...) custom-call(bf16[128,1024]{1,0:T(8,128)(2,1)} %x_ref.1, ...), custom_call_target="tpu_custom_call" | custom-call | flops 6499999744 | bytes 30000000 | tf_op jit(solution)/shard_map/layer/pallas_call | solution.py:440
  119.4 0.7 reduce.11
  120.3 0.8 slice_bitcast_fusion.13
  121.2 65.6 %psum.7 = f32[72]{0:T(128)S(1)} all-reduce(f32[72]{0:T(128)S(1)} %pad_maximum_fusion), channel_id=1, replica_groups=mesh['dp_0'=4,'dp_1'=4,'dp_2'=2,'fsdp'=4] {'dp_0','dp_1','dp_2','fsdp'}, use_global_device_ids=true, to_apply=%region_6.7 | all-reduce | flops 72 | bytes 576 | tf_op jit(solution)/shard_map/psum | solution.py:680
  186.8 0.6 slice_bitcast_fusion.9
  187.4 1.0 reshape.189
  188.5 0.7 reduce.7
  189.4 0.7 reduce.8
  190.6 0.2 concatenate.27
  190.8 0.5 broadcast.56
  191.3 1.3 reduce.28
  192.6 0.3 concatenate.30
  193.0 1.3 reduce.29
  194.3 0.3 concatenate.31
  194.8 1.6 concatenate.28.small
  196.4 74.8 %reduce.30 = f32[8,12416]{1,0:T(8,128)} custom-call(bf16[4,16,2,32,128]{4,3,2,1,0:T(8,128)(2,1)} %bitcast.83, bf16[128,12416]{1,0:T(8,128)(2,1)} %get-tuple-element.33.z, f32[16,2,32,128]{3,2,1,0:T(8,128)} %concatenate.28.small), custom_call_target="tpu_custom_call" | custom-call | tf_op jit(solution)/shard_map/reduce/pallas_call | solution.py:651
  271.2 1.6 slice_bitcast_fusion
  272.7 1.5 slice_bitcast_fusion.3
  274.2 1.5 slice_bitcast_fusion.1
  275.7 1.4 slice_bitcast_fusion.2
  277.1 1.3 slice_bitcast_fusion.5
  278.5 1.3 slice_bitcast_fusion.7
  279.8 0.7 slice.104
  280.7 0.7 reshape.193
  281.3 0.6 slice.106
  281.9 1.3 slice_bitcast_fusion.8
  283.2 1.5 slice_reduce_fusion.2
  (48 shorter events, 2.7 us)
Async XLA Ops:
  0.7 85.1 %copy-start.3 = (bf16[1,24]{1,0:T(2,128)(2,1)S(1)}, bf16[1,24]{1,0:T(2,128)(2,1)}, u32[]{:S(2)}) copy-start(bf16[1,24]{1,0:T(2,128)(2,1)} %param.30) | copy-start | bytes 148
  0.7 85.1 %copy-start.2 = (bf16[1,24]{1,0:T(2,128)(2,1)S(1)}, bf16[1,24]{1,0:T(2,128)(2,1)}, u32[]{:S(2)}) copy-start(bf16[1,24]{1,0:T(2,128)(2,1)} %param.31) | copy-start | bytes 148
  0.7 85.6 %copy-start.4 = (bf16[1,24]{1,0:T(2,128)(2,1)S(1)}, bf16[1,24]{1,0:T(2,128)(2,1)}, u32[]{:S(2)}) copy-start(bf16[1,24]{1,0:T(2,128)(2,1)} %param.32) | copy-start | bytes 148
  3.5 83.6 %copy-start = (s32[128]{0:T(128)}, s32[128]{0:T(128)S(1)}, u32[]{:S(2)}) copy-start(s32[128]{0:T(128)S(1)} %get-tuple-element.46) | copy-start | bytes 1540
  280.6 4.1 %copy-start.1 = (f32[1,88]{1,0:T(1,128)}, f32[1,88]{1,0:T(1,128)S(1)}, u32[]{:S(2)}) copy-start(f32[1,88]{1,0:T(1,128)S(1)} %reshape.192) | copy-start | bytes 1060

commit v2 on v1

--- a/solution.py
+++ b/solution.py
@@ -12,6 +12,17 @@
 EPSILON = 1e-05
 ROPE_BASE = 100000000000.0
 DP_FSDP = ("dp_0", "dp_1", "dp_2", "fsdp")
+OFF = dict(gate=(0, 1536), inner=(1536, 1792), query=(3328, 512), keyval=(3840, 256), step=(4096, 128),
+           mix=(4224, 1536), attn=(5760, 512), gateup=(6272, 4096), down=(10368, 2048))
+COLS = 12416
+FIRST = 4224
+F32, BF16 = jnp.float32, jnp.bfloat16
+HIGH = lax.Precision.HIGHEST
+AT_IN, AT_FFN, AT_MIX, AT_BIAS, AT_TAPS = 24, 32, 40, 52, 66
+SMALLS = ((AT_IN, 8, 1024), (AT_FFN, 8, 1024), (AT_MIX, 12, 1536), (AT_BIAS, 14, 1792))
+INVERSE = {8: 8192, 12: 5462, 14: 4682}
+
+
 AX, AZ, AC, AY = "dp_0", "dp_1", "dp_2", "fsdp"
 ORDERS = ((AX, AY, AZ), (AY, AZ, AX), (AZ, AX, AY))
 MESH = pl.DeviceIdType.MESH
@@ -24,10 +35,10 @@
 def greet(at):
     barrier = pltpu.get_barrier_semaphore()
     for a in (AX, AZ, AY):
-        for d in (1, 3):
+        for d in (1, 2, 3):
             pl.semaphore_signal(barrier, inc=1, device_id={a: lax.rem(at[a] + d, 4)}, device_id_type=MESH)
     pl.semaphore_signal(barrier, inc=1, device_id={AC: 1 - at[AC]}, device_id_type=MESH)
-    pl.semaphore_wait(barrier, 7)
+    pl.semaphore_wait(barrier, 10)
 
 
 def cut3(cols, start=0):
@@ -41,8 +52,25 @@
     return parts
 
 
-def gather_kernel(parts, shard, out, send, recv, sib_send, sib_recv, own_sem):
+def assemble(pieces, shard, tile):
+    gate, inner, step, taps, cbias, mixer, mix, query, keyval, attn, gin, gffn, gateup, down = pieces
+    for ref, (c0, n) in ((gate, OFF["gate"]), (inner, OFF["inner"]), (query, OFF["query"]), (keyval, OFF["keyval"]),
+                         (mix, OFF["mix"]), (attn, OFF["attn"]), (gateup, OFF["gateup"]), (down, OFF["down"])):
+        shard[:, c0:c0 + n] = ref[...]
+    tile[...] = jnp.zeros((8, 128), F32)
+    tile[:, 0:24] = step[...].astype(F32)
+    tile[0:1, AT_IN:AT_IN + 8] = gin[...].astype(F32)
+    tile[0:1, AT_FFN:AT_FFN + 8] = gffn[...].astype(F32)
+    tile[0:1, AT_MIX:AT_MIX + 12] = mixer[...].astype(F32)
+    tile[0:1, AT_BIAS:AT_BIAS + 14] = cbias[...].astype(F32)
+    tile[0:4, AT_TAPS:AT_TAPS + 14] = taps[...].astype(F32)
+    shard[:, 4096:4224] = tile[...].astype(BF16)
+
+
+def gather_kernel(parts, *refs):
+    pieces, out, (shard, tile, send, recv, sib_send, sib_recv, own_sem) = refs[:14], refs[14], refs[15:]
     at = places()
+    assemble(pieces, shard, tile)
     greet(at)
     whole = slice(None)
     core = at[AC]
@@ -121,33 +149,22 @@
         c.wait()
 
 
-def gather(shard, space=pl.ANY, cid=0):
-    cols = shard.shape[1]
-    parts = cut3(cols)
+def gather(*pieces):
+    parts = cut3(COLS)
+    vm = pl.BlockSpec(memory_space=pltpu.VMEM)
     return pl.pallas_call(
         functools.partial(gather_kernel, parts),
-        out_shape=jax.ShapeDtypeStruct((4, 4, 2, 4, 8, cols), jnp.bfloat16),
-        in_specs=[pl.BlockSpec(memory_space=pltpu.VMEM)],
-        out_specs=pl.BlockSpec(memory_space=space),
+        out_shape=jax.ShapeDtypeStruct((4, 4, 2, 4, 8, COLS), BF16),
+        in_specs=[vm] * 14,
+        out_specs=pl.BlockSpec(memory_space=pl.ANY),
         scratch_shapes=[
+            pltpu.VMEM((8, COLS), BF16), pltpu.VMEM((8, 128), F32),
             pltpu.SemaphoreType.DMA((3, 3, 6)), pltpu.SemaphoreType.DMA((3, 3, 6)),
             pltpu.SemaphoreType.DMA((3, 5)), pltpu.SemaphoreType.DMA((3, 5)), pltpu.SemaphoreType.DMA,
         ],
-        compiler_params=pltpu.CompilerParams(collective_id=cid, has_side_effects=True, vmem_limit_bytes=60 << 20),
+        compiler_params=pltpu.CompilerParams(collective_id=0, has_side_effects=True, vmem_limit_bytes=60 << 20),
         name="gather",
-    )(shard)
-
-
-def shapes_of(phase, cols):
-    return (4,) * (2 - phase) + (8, cols)
-
-
-OFF = dict(gate=(0, 1536), inner=(1536, 1792), query=(3328, 512), keyval=(3840, 256), step=(4096, 128),
-           mix=(4224, 1536), attn=(5760, 512), gateup=(6272, 4096), down=(10368, 2048))
-COLS = 12416
-FIRST = 4224
-F32, BF16 = jnp.float32, jnp.bfloat16
-HIGH = lax.Precision.HIGHEST
+    )(*pieces)
 
 
 def nn(a, b, precision=None):
@@ -180,9 +197,33 @@
     return lax.rsqrt(jnp.mean(values * values, axis=-1, keepdims=True) + EPSILON)
 
 
-def layer_kernel(x_ref, og_ref, segc, segr, pos, act, cos, sin, w_hbm, gin, gffn, gmix, taps, cbias, sbias, dlog, skipx,
-                 result, dx, rt, z, gin_g, gffn_g, gmix_g, taps_g, cbias_g, head_g, skip_g,
-                 wv, proj, csum, conv, yfull, dec, soft, qr, x1_s, df_s, dm_s, do_s, dconv, ddt_s, wsem):
+def selectors(i, start, n):
+    d = lax.broadcasted_iota(jnp.int32, (128, 128), 1) + 128 * i
+    row = lax.broadcasted_iota(jnp.int32, (128, 128), 0)
+    owner = lax.shift_right_logical(d * INVERSE[n], 16)
+    return row == owner, row == start + d - n * owner
+
+
+def spread_row(table, start, n, width, dst, row=0):
+    for i in range(width // 128):
+        owned, lane = selectors(i, start, n)
+        v = nn(table, lane.astype(F32).astype(BF16))
+        dst[row:row + 1, 128 * i:128 * i + 128] = jnp.sum(jnp.where(owned, v, 0.0), axis=0, keepdims=True)
+
+
+def unspread_row(src, start, n, width, row=0):
+    total = jnp.zeros((128, 128), F32)
+    for i in range(width // 128):
+        owned, lane = selectors(i, start, n)
+        held = jnp.where(owned, src[row:row + 1, 128 * i:128 * i + 128], 0.0)
+        total = total + nt(held.astype(BF16), lane.astype(F32).astype(BF16))
+    return total
+
+
+def layer_kernel(x_ref, og_ref, lengths, owners, w_hbm, sbias_ref, dlog_ref, skip_ref,
+                 result, dx, rt, z, small, head_g,
+                 wv, proj, csum, conv, yfull, dec, soft, qr, x1_s, df_s, dm_s, do_s, dconv, ddt_s, wsem,
+                 gin, gffn, gmix, taps, cbias, skipx, rows_s, gin_g, gffn_g, gmix_g, taps_g, cbias_g, table):
     groups = ((0, FIRST), (4224, 2048), (6272, 4096), (10368, 2048))
     loads = []
     for k, (c0, n) in enumerate(groups):
@@ -193,8 +234,36 @@
     lane = lax.broadcasted_iota(jnp.int32, (128, 128), 1)
     sub = lax.broadcasted_iota(jnp.int32, (128, 128), 0)
     low_lanes = lane < 64
-    allowed = (segc[...] == segr[...]) & (sub >= lane)
-    position = pos[...]
+
+    at = places()
+    me = ((at[AX] * 4 + at[AZ]) * 2 + at[AC]) * 4 + at[AY]
+    owned = owners[...] == me
+    held = jnp.where(owned, lengths[...], 0).astype(F32)
+    before = lax.broadcasted_iota(jnp.int32, (256, 256), 0) <= lax.broadcasted_iota(jnp.int32, (256, 256), 1)
+    ends = nn(jnp.broadcast_to(held, (8, 256)).astype(BF16), before.astype(F32).astype(BF16))[0:1, :]
+    slot = lax.broadcasted_iota(jnp.int32, (128, 256), 0).astype(F32)
+    closed = jnp.broadcast_to(owned.astype(F32), (128, 256)) * (jnp.broadcast_to(ends, (128, 256)) <= slot).astype(F32)
+    segment = jnp.sum(closed, axis=1, keepdims=True)
+    begins = jnp.max(closed * ends, axis=1, keepdims=True)
+    used = jnp.max(ends, axis=1, keepdims=True)
+    slots = sub.astype(F32)
+    position = jnp.broadcast_to(slots[:, 0:1] - begins, (128, 128))
+    active = (slots[:, 0:1] < used).astype(F32)
+    segments = jnp.broadcast_to(segment, (128, 128))
+    allowed = (segments == segments.T) & (sub >= lane)
+    speeds = jnp.exp((lane % 32).astype(F32) * (-math.log(ROPE_BASE) * 2.0 / 64))
+    angles = position * speeds
+    cosine, sine = jnp.cos(angles), jnp.sin(angles)
+
+    rows_s[...] = jnp.zeros((8, 128), F32)
+    rows_s[0:1, 0:24] = sbias_ref[...].astype(F32)
+    rows_s[1:2, 0:24] = dlog_ref[...].astype(F32)
+    rows_s[2:3, 0:24] = skip_ref[...].astype(F32)
+    sbias, dlog = rows_s[0:1, :], rows_s[1:2, :]
+    heads_low = rows_s[...].astype(BF16)
+    for i in range(12):
+        of_head = (sub == 2 * i + lax.shift_right_logical(lane, 6)).astype(F32).astype(BF16)
+        skipx[:, 128 * i:128 * i + 128] = nn(heads_low, of_head)[2:3, :]
 
     def halves(v):
         return jnp.where(low_lanes, v, 0.0), jnp.where(low_lanes, 0.0, v)
@@ -203,14 +272,21 @@
         lo, hi = halves(v)
         return jnp.concatenate([lo, hi], axis=0).astype(BF16)
 
+    loads[0].wait()
+    table[...] = wv[:, 4096:4224].astype(F32)
+    tables = [table[pl.ds(r, 128, stride=8), :].astype(BF16) for r in range(4)]
+    for dst, (start, n, width) in zip((gin, gffn, gmix, cbias), SMALLS):
+        spread_row(tables[0], start, n, width, dst)
+    for r in range(4):
+        spread_row(tables[r], AT_TAPS, 14, 1792, taps, r)
+
     x = x_ref[...].astype(F32)
     h = (x * row_scale(x) * gin[...]).astype(BF16)
     rt[0:1024, :] = h.T
-    g0 = og_ref[...].astype(F32) * act[...]
+    g0 = og_ref[...].astype(F32) * active
     glow = g0.astype(BF16)
     rt[3072:4096, :] = glow.T
     z_h = h
-    loads[0].wait()
 
     def project(i, carry):
         proj[:, cols_of(i, 384)] = nn(z_h, wv[:, cols_of(i, 384)])
@@ -222,7 +298,7 @@
         p = proj[:, cols_of(i, 128, 1536)]
         total = p * taps[3:4, cs]
         for j in (1, 2, 3):
-            moved = jnp.where(position >= j, pltpu.roll(p, j, axis=0), 0.0)
+            moved = jnp.where(position >= float(j), pltpu.roll(p, j, axis=0), 0.0)
             total = total + moved * taps[3 - j:4 - j, cs]
         total = total + cbias[:, cs]
         csum[:, cs] = total
@@ -230,9 +306,9 @@
         return carry
     lax.fori_loop(0, 14, convolve, 0)
 
-    step = proj[:, 4096:4224] + sbias[...]
+    step = proj[:, 4096:4224] + sbias
     dt = jnp.maximum(step, 0.0) + jnp.log(1.0 + jnp.exp(-jnp.abs(step)))
-    rate = -jnp.exp(dlog[...])
+    rate = -jnp.exp(dlog)
     lower = (sub >= lane).astype(F32)
     level = nn(lower, dt * rate, HIGH)
     dt_t = dt.T
@@ -266,7 +342,6 @@
         return carry
     lax.fori_loop(0, 12, mixer_norm, 0)
 
-    cosine, sine = cos[...], sin[...]
     first = (lane % 64) < 32
 
     def turn(v, sign):
@@ -367,6 +442,8 @@
     pull = rmix * rmix * rmix * dots * (1.0 / 1536)
     ddt_s[...] = jnp.zeros((128, 128), F32)
     dlevel = jnp.zeros((128, 128), F32)
+    dskip = jnp.zeros((1, 128), F32)
+    lane_row = lane[0:1, :]
     dinter = jnp.zeros((128, 128), F32)
     for t in range(12):
         cs = slice(128 * t, 128 * t + 128)
@@ -378,7 +455,11 @@
         z[:, cs] = (dgy * y * (s + gs * (1.0 - s))).astype(BF16)
         dy = dgy * gs
         xs = conv[:, cs]
-        skip_g[:, cs] = jnp.sum(dy * xs, axis=0, keepdims=True)
+        skipped = jnp.sum(dy * xs, axis=0, keepdims=True)
+        for e in (0, 1):
+            in_head = (lane_row < 64) if e == 0 else (lane_row >= 64)
+            dskip = dskip + jnp.where(lane_row == 2 * t + e,
+                                      jnp.sum(jnp.where(in_head, skipped, 0.0), axis=1, keepdims=True), 0.0)
         dy2 = stacked(dy)
         dmix = nt(dy2, xs.astype(BF16))
         mixes = []
@@ -402,6 +483,8 @@
     drate = nn(upper, dlevel, HIGH)
     dstep = jnp.where(lane < 24, (ddt + drate * rate) * sigmoid(step), 0.0)
     z[:, 4096:4224] = dstep.astype(BF16)
+    head_g[...] = jnp.zeros((8, 128), F32)
+    head_g[2:3, :] = dskip
     head_g[0:1, :] = jnp.sum(dstep, axis=0, keepdims=True)
     head_g[1:2, :] = jnp.sum(drate * dt * rate, axis=0, keepdims=True)
 
@@ -415,7 +498,7 @@
         taps_g[3:4, cs] = jnp.sum(d * p, axis=0, keepdims=True)
         back = d * taps[3:4, cs]
         for j in (1, 2, 3):
-            masked = jnp.where(position >= j, d, 0.0)
+            masked = jnp.where(position >= float(j), d, 0.0)
             taps_g[3 - j:4 - j, cs] = jnp.sum(masked * pltpu.roll(p, j, axis=0), axis=0, keepdims=True)
             back = back + pltpu.roll(masked, 128 - j, axis=0) * taps[3 - j:4 - j, cs]
         z[:, cols_of(i, 128, 1536)] = back.astype(BF16)
@@ -430,25 +513,37 @@
     gin_g[...] = gain_grad
     dx[...] = x1_s[...] + part
 
+    small[...] = jnp.zeros((1024, 128), F32)
+    for r in range(4):
+        total = unspread_row(taps_g, AT_TAPS, 14, 1792, r)
+        if r == 0:
+            for src, (start, n, width) in zip((gin_g, gffn_g, gmix_g, cbias_g), SMALLS):
+                total = total + unspread_row(src, start, n, width)
+        small[pl.ds(r, 128, stride=8), :] = total
+
 
 def layer_call(*args):
     def of(*s, t=F32):
         return jax.ShapeDtypeStruct(s, t)
     vm = pl.BlockSpec(memory_space=pltpu.VMEM)
-    specs = [vm] * 17
-    specs[8] = pl.BlockSpec(memory_space=pl.ANY)
+    specs = [vm] * 8
+    specs[4] = pl.BlockSpec(memory_space=pl.ANY)
     return pl.pallas_call(
         layer_kernel,
-        out_shape=(of(128, 1024, t=BF16), of(128, 1024), of(4096, 128, t=BF16), of(128, COLS, t=BF16), of(1, 1024),
-                   of(1, 1024), of(1, 1536), of(4, 1792), of(1, 1792), of(8, 128), of(1, 1536)),
+        out_shape=(of(128, 1024, t=BF16), of(128, 1024), of(4096, 128, t=BF16), of(128, COLS, t=BF16), of(1024, 128),
+                   of(8, 128)),
         in_specs=specs,
-        out_specs=[vm] * 11,
+        out_specs=[vm] * 6,
         scratch_shapes=[
             pltpu.VMEM((1024, COLS), BF16), pltpu.VMEM((128, FIRST), F32), pltpu.VMEM((128, 1792), F32),
             pltpu.VMEM((128, 1792), F32), pltpu.VMEM((128, 1536), F32), pltpu.VMEM((24, 128, 128), F32),
             pltpu.VMEM((8, 128, 128), F32), pltpu.VMEM((128, 512), F32), pltpu.VMEM((128, 1024), F32),
             pltpu.VMEM((128, 1024), F32), pltpu.VMEM((128, 1536), F32), pltpu.VMEM((128, 512), F32),
             pltpu.VMEM((128, 1792), F32), pltpu.VMEM((128, 128), F32), pltpu.SemaphoreType.DMA((4,)),
+            pltpu.VMEM((1, 1024), F32), pltpu.VMEM((1, 1024), F32), pltpu.VMEM((1, 1536), F32), pltpu.VMEM((4, 1792), F32),
+            pltpu.VMEM((1, 1792), F32), pltpu.VMEM((1, 1536), F32), pltpu.VMEM((8, 128), F32),
+            pltpu.VMEM((1, 1024), F32), pltpu.VMEM((1, 1024), F32), pltpu.VMEM((1, 1536), F32), pltpu.VMEM((4, 1792), F32),
+            pltpu.VMEM((1, 1792), F32), pltpu.VMEM((1024, 128), F32),
         ],
         compiler_params=pltpu.CompilerParams(vmem_limit_bytes=60 << 20),
         cost_estimate=pl.CostEstimate(flops=6_500_000_000, bytes_accessed=30_000_000, transcendentals=3_000_000),
@@ -456,62 +551,11 @@
     )(*args)
 
 
-def layout(device, seq_lengths, seq_owner, slot_count):
-    owned = seq_owner == device
-    own_lengths = jnp.where(owned, seq_lengths, 0)
-    finish = jnp.cumsum(own_lengths, dtype=jnp.int32)
-    slot_ids = jnp.arange(slot_count, dtype=jnp.int32)
-    closed = owned[None, :] & (finish[None, :] <= slot_ids[:, None])
-    segment = jnp.sum(closed.astype(jnp.int32), axis=1, dtype=jnp.int32)
-    begins = jnp.max(jnp.where(closed, finish[None, :], 0), axis=1)
-    active = slot_ids < jnp.sum(own_lengths, dtype=jnp.int32)
-    return (segment, slot_ids - begins, active)
-
-
-def turn_tables(position):
-    ladder = jnp.arange(32, dtype=jnp.float32) * (2.0 / 64)
-    speeds = jnp.exp(-math.log(ROPE_BASE) * ladder)
-    angles = position.astype(jnp.float32)[:, None] * jnp.tile(speeds, 4)[None, :]
-    return jnp.cos(angles), jnp.sin(angles)
-
-
-def pack_smalls(mixer, taps, bias):
-    k = mixer.shape[0]
-    flat = jnp.concatenate([mixer, taps.reshape(k, 56), bias, jnp.zeros((k, 6), mixer.dtype)], axis=1)
-    return flat.reshape(k * 8, 11)
-
-
-def unpack_smalls(table):
-    k = table.shape[0] // 8
-    flat = table.reshape(k, 88)
-    return flat[:, :12], flat[:, 12:68].reshape(k, 4, 14), flat[:, 68:82]
-
-
-def row_of(values, width=128):
-    return jnp.pad(values.astype(F32), ((0, 0), (0, width - values.shape[1])))
-
-
-def layer_inputs(tokens, out_grad, segment, position, active, weights, step_bias, decay_log, skip_gain):
-    smalls = weights[:, 4120:4133].astype(F32)
-    mixer, taps, bias = unpack_smalls(smalls[:, 2:])
-    cosine, sine = turn_tables(position)
-    return (tokens, out_grad, segment[:, None], segment[None, :], position[:, None], active[:, None].astype(F32),
-            cosine, sine, weights, smalls[:, 0][None], smalls[:, 1][None], mixer.reshape(1, 1536),
-            jnp.moveaxis(taps, 1, 0).reshape(4, 1792), bias.reshape(1, 1792), row_of(step_bias), row_of(decay_log),
-            jnp.repeat(skip_gain.astype(F32), 64, axis=1))
-
-
-def small_table(gin_g, gffn_g, gmix_g, taps_g, cbias_g):
-    smalls = pack_smalls(gmix_g.reshape(128, 12), jnp.moveaxis(taps_g.reshape(4, 128, 14), 0, 1), cbias_g.reshape(128, 14))
-    return jnp.concatenate([jnp.zeros((1024, 24), F32), gin_g.reshape(1024, 1), gffn_g.reshape(1024, 1), smalls,
-                            jnp.zeros((1024, 91), F32)], axis=1)
-
-
 PIECES = (((0, 0, 4224, 384),), ((1, 4224, 2048, 256), (2, 6272, 2048, 256)), ((2, 8320, 2048, 256), (3, 10368, 2048, 256)))
 
 
-def reduce_kernel(parts, rt, z, small, out, grad, z_sib, rt_sib, small_sib, *scratch):
-    bufs, (send, recv, x_send, x_recv) = scratch[:-4], scratch[-4:]
+def reduce_kernel(parts, rt, z, small, head, out, head_out, grad, z_sib, rt_sib, small_sib, *scratch):
+    bufs, (send, recv, x_send, x_recv, hnow, hbuf, h_send, h_recv) = scratch[:-8], scratch[-8:]
     at = places()
     greet(at)
     whole = slice(None)
@@ -527,6 +571,7 @@
         swap(1 + part, z.at[:, pl.ds(c0, lo + hi)], z_sib.at[:, pl.ds(c0, lo + hi)])
         if part == 0:
             swap(4, small.at[:, 1 - core], small_sib)
+            swap(5, head, hnow.at[4])
 
     def products(part):
         for g, c0, n, width in PIECES[part]:
@@ -541,6 +586,26 @@
             lax.fori_loop(0, n // width, one, 0)
 
     sent = []
+    axes = (AX, AZ, AY)
+
+    def heads_out(k):
+        a = axes[k]
+        p = at[a]
+        hbuf[k, p] = hnow[k]
+        copies = []
+        for d in (1, 2, 3):
+            c = pltpu.make_async_remote_copy(hnow.at[k], hbuf.at[k, p], h_send.at[k, d - 1], h_recv.at[k, d - 1],
+                                             device_id={a: lax.rem(p + d, 4)}, device_id_type=MESH)
+            c.start()
+            copies.append(c)
+        sent.extend(copies)
+        return copies
+
+    def heads_in(k, copies):
+        for c in copies:
+            c.wait_recv()
+        return ((hbuf[k, 0] + hbuf[k, 1]) + hbuf[k, 2]) + hbuf[k, 3]
+    moving = None
     for phase in range(3):
         state = []
         for part, (c0, lo, hi) in enumerate(parts):
@@ -566,7 +631,7 @@
                     swaps[1].wait_recv()
                     swaps[2].wait_recv()
                 else:
-                    swaps[2 + part].wait_recv()
+                    swaps[3 + part].wait_recv()
                 products(part)
                 if part == 0:
                     tile = grad.at[:, :, :, :, pl.ds(4096, 128)]
@@ -586,6 +651,13 @@
             sent += [e_l, e_r, d_l_hi, d_r_lo, d_l_lo, d_r_hi]
             state.append((e_l, e_r, d_l_hi, d_r_lo, d_l_lo, d_r_hi, ref, nxt, prv, p, c0, lo, hi, el, er, fr, fl))
 
+        if phase == 0:
+            swaps[3].wait_recv()
+            hnow[0] = head[...] + hnow[4]
+        else:
+            hnow[phase] = heads_in(phase - 1, moving)
+        moving = heads_out(phase)
+
         def each(fn):
             n = 2 - phase
             if n == 2:
@@ -630,6 +702,7 @@
                 else:
                     t[ix] = v.astype(BF16)
             each(total)
+    head_out[...] = heads_in(2, moving)
     for c in sent:
         c.wait_send()
     for c in swaps:
@@ -640,7 +713,7 @@
     return (4,) * (2 - phase) + (8, cols)
 
 
-def reduce_call(rt, z, small):
+def reduce_call(rt, z, small, head):
     parts = cut3(COLS)
     bufs = []
     for c0, lo, hi in parts:
@@ -650,46 +723,66 @@
     vm = pl.BlockSpec(memory_space=pltpu.VMEM)
     return pl.pallas_call(
         functools.partial(reduce_kernel, parts),
-        out_shape=jax.ShapeDtypeStruct((8, COLS), F32),
-        in_specs=[vm] * 3,
-        out_specs=vm,
+        out_shape=(jax.ShapeDtypeStruct((8, COLS), F32), jax.ShapeDtypeStruct((8, 128), F32)),
+        in_specs=[vm] * 4,
+        out_specs=[vm] * 2,
         scratch_shapes=[pltpu.VMEM((4, 4, 4, 8, COLS), BF16), pltpu.VMEM((128, COLS), BF16),
                         pltpu.VMEM((4, 16, 32, 128), BF16), pltpu.VMEM((16, 32, 128), F32)] + bufs + [
             pltpu.SemaphoreType.DMA((3, 3, 6)), pltpu.SemaphoreType.DMA((3, 3, 6)),
-            pltpu.SemaphoreType.DMA((5,)), pltpu.SemaphoreType.DMA((5,))],
+            pltpu.SemaphoreType.DMA((6,)), pltpu.SemaphoreType.DMA((6,)),
+            pltpu.VMEM((5, 8, 128), F32), pltpu.VMEM((3, 4, 8, 128), F32),
+            pltpu.SemaphoreType.DMA((3, 3)), pltpu.SemaphoreType.DMA((3, 3))],
         compiler_params=pltpu.CompilerParams(collective_id=1, has_side_effects=True, vmem_limit_bytes=60 << 20),
         name="reduce",
-    )(rt, z, small)
+    )(rt, z, small, head)
+
+
+SPLIT = ("gate", "inner", "query", "keyval", "mix", "attn", "gateup", "down")
+
+
+def split_kernel(grads, head, *outs):
+    for name, dst in zip(SPLIT, outs[:8]):
+        start, n = OFF[name]
+        dst[...] = grads[:, start:start + n]
+    step, gin, gffn, gmix, cbias, taps, bias, decay, skip = outs[8:]
+    tile = grads[:, 4096:4224]
+    step[...] = tile[:, 0:24]
+    gin[...] = tile[0:1, AT_IN:AT_IN + 8]
+    gffn[...] = tile[0:1, AT_FFN:AT_FFN + 8]
+    gmix[...] = tile[0:1, AT_MIX:AT_MIX + 12]
+    cbias[...] = tile[0:1, AT_BIAS:AT_BIAS + 14]
+    taps[...] = tile[0:4, AT_TAPS:AT_TAPS + 14]
+    for r, dst in enumerate((bias, decay, skip)):
+        dst[...] = head[r:r + 1, 0:24]
+
+
+def split_call(grads, head):
+    def of(*s):
+        return jax.ShapeDtypeStruct(s, F32)
+    vm = pl.BlockSpec(memory_space=pltpu.VMEM)
+    return pl.pallas_call(
+        split_kernel,
+        out_shape=[of(8, OFF[k][1]) for k in SPLIT] + [of(8, 24), of(1, 8), of(1, 8), of(1, 12), of(1, 14), of(4, 14),
+                                                       of(1, 24), of(1, 24), of(1, 24)],
+        in_specs=[vm] * 2,
+        out_specs=[vm] * 17,
+        name="split",
+    )(grads, head)
 
 
 def body(tokens, seq_lengths, seq_owner, input_norm, gate_proj, inner_proj, step_proj, conv_weight, conv_bias, step_bias,
          decay_log, skip_gain, mixer_norm, mixer_out, query_proj, keyval_proj, attn_out, ffn_norm, gateup_proj, down_proj,
          out_grad):
-    device = lax.axis_index(DP_FSDP)
-    segment, position, active = layout(device, seq_lengths, seq_owner, tokens.shape[0])
-    smalls = pack_smalls(mixer_norm, conv_weight, conv_bias)
-    shard = jnp.concatenate(
-        [gate_proj[0], inner_proj[0], query_proj[0], keyval_proj[0], step_proj[0], input_norm.reshape(8, 1),
-         ffn_norm.reshape(8, 1), smalls, jnp.zeros((8, 91), BF16), mixer_out[0].T, attn_out[0].T, gateup_proj[0],
-         down_proj[0].T], axis=1)
-    weights = gather(shard).reshape(1024, COLS)
-    inputs = layer_inputs(tokens, out_grad, segment, position, active, weights, step_bias, decay_log, skip_gain)
-    result, dx, rt, z, gin_g, gffn_g, gmix_g, taps_g, cbias_g, head_g, skip_g = layer_call(*inputs)
-    table = small_table(gin_g, gffn_g, gmix_g, taps_g, cbias_g)
-    heads = jnp.concatenate([head_g[0, :24], head_g[1, :24], jnp.sum(skip_g.reshape(24, 64), axis=1)])
-    heads = lax.psum(heads, DP_FSDP).reshape(3, 1, 24)
-    grads = reduce_call(rt.reshape(4, 16, 2, 32, 128), z, table.reshape(16, 2, 32, 128))
-    mixer_g, conv_g, bias_g = unpack_smalls(grads[:, 4122:4133])
-
-    def cols(name):
-        start, n = OFF[name]
-        return grads[:, start:start + n]
-    return (
-        result, dx, grads[:, 4120].reshape(1, 8), cols("gate")[None], cols("inner")[None], grads[None, :, 4096:4120],
-        conv_g, bias_g, heads[0], heads[1], heads[2], mixer_g, cols("mix").T[None], cols("query")[None],
-        cols("keyval")[None], cols("attn").T[None], grads[:, 4121].reshape(1, 8), cols("gateup")[None],
-        cols("down").T[None],
-    )
+    weights = gather(gate_proj[0], inner_proj[0], step_proj[0], conv_weight[0], conv_bias, mixer_norm, mixer_out[0].T,
+                     query_proj[0], keyval_proj[0], attn_out[0].T, input_norm, ffn_norm, gateup_proj[0],
+                     down_proj[0].T).reshape(1024, COLS)
+    result, dx, rt, z, small, head = layer_call(tokens, out_grad, seq_lengths.reshape(1, 256), seq_owner.reshape(1, 256),
+                                                weights, step_bias, decay_log, skip_gain)
+    grads, heads = reduce_call(rt.reshape(4, 16, 2, 32, 128), z, small.reshape(16, 2, 32, 128), head)
+    (gate, inner, query, keyval, mix, attn, gateup, down, step, gin, gffn, gmix, cbias, taps, bias, decay,
+     skip) = split_call(grads, heads)
+    return (result, dx, gin, gate[None], inner[None], step[None], taps[None], cbias, bias, decay, skip, gmix, mix.T[None],
+            query[None], keyval[None], attn.T[None], gffn, gateup[None], down.T[None])
 
 
 def solution(mesh):

time: 286 us -> 185 us (0.65)
  blocking collectives: 65.6 us -> 0 us
  local copies, waits for them, and re-layouts: 29.6 us -> 0 us
  other arithmetic: 13 us -> 0 us
  Pallas kernels: 176 us -> 184 us
    psum x1 -> x0, blocking collectives: 65.6 us -> none  [body(): heads = lax.psum(heads, DP_FSDP).reshape(3, 1, 24)]
    broadcast_in_dim x14 -> x0, local copies, waits for them, and re-layouts: 11.4 us -> none  [the longest x1 1.57 us: body(): cols('gateup')[None]]
    reshape x18 -> x0, local copies, waits for them, and re-layouts: 6.96 us -> none  [the longest x1 0.98 us: small_table(): taps_g.reshape(4, 128, 14)]
    pallas_call x5 -> x0, other arithmetic: 4.85 us -> none  [layer_call(): pl.pallas_call(layer_kernel, out_shape=(of(128, 1024, t=BF16), of(128, 10...]
    slice x10 -> x0, local copies, waits for them, and re-layouts: 4.45 us -> none  [the longest x1 1.47 us: body(): grads[:, 4121].reshape(1, 8)]
    pallas_call x1 -> x2, Pallas kernels: 74.8 us -> 79.1 us  [the longest x1 77.4 us: reduce_call(): pl.pallas_call(functools.partial(reduce_kernel, parts), out_shape=(jax.Sh...]
    concatenate x7 -> x0, local copies, waits for them, and re-layouts: 4.29 us -> none  [the longest x4 2.44 us: small_table(): jnp.concatenate([jnp.zeros((1024, 24), F32), gin_g.reshape(1024, 1), gffn...]
where the time goes in v2:
time: 185 us
  Pallas kernels  184 us (99%)
    pallas_call x1, Pallas kernels, reduce_call(): pl.pallas_call(functools.partial(reduce_kernel, parts), out_shape=(jax.Sh...  77.4 us
    pallas_call x1, Pallas kernels, gather(): pl.pallas_call(functools.partial(gather_kernel, parts), out_shape=jax.Sha...  69.6 us
    pallas_call x1, Pallas kernels, layer_call(): pl.pallas_call(layer_kernel, out_shape=(of(128, 1024, t=BF16), of(128, 10...  35.2 us

profile of v2, /device:TPU:0, one launch (start us, length us, event | category | flops | bytes accessed | tf_op | source)
XLA Modules:
  0.0 184.8 jit_solution(14243339719226056716)
XLA Ops:
  0.7 69.6 %gather.1 = bf16[4,4,2,4,8,12416]{5,4,3,2,1,0:T(8,128)(2,1)} custom-call(bf16[8,1536]{1,0:T(8,128)(2,1)} %bitcast.43, bf16[8,1792]{1,0:T(8,128)(2,1)} %bitcast.42, bf16[8,24]{1,0:T(8,128)(2,1)} %bitcast.48, bf16[4,14]{1,0:T(4,128)(2,1)} %bitcast.49, bf16[1,14]{1,0:T(2,128)(2,1)} %refs_4_.1, bf16[1,12]{1,0:T(2,128)(2,1)} %refs_5_.1, ...), custom_call_target="tpu_custom_call" | custom-call | tf_op jit(solution)/shard_map/gather/pallas_call | solution.py:155
  70.3 35.2 %layer.1 = (bf16[128,1024]{1,0:T(8,128)(2,1)}, f32[128,1024]{1,0:T(8,128)}, bf16[4096,128]{1,0:T(8,128)(2,1)}, bf16[128,12416]{1,0:T(8,128)(2,1)}, f32[1024,128]{1,0:T(8,128)}, /*index=5*/f32[8,128]{1,0:T(8,128)}) custom-call(bf16[128,1024]{1,0:T(8,128)(2,1)} %x_ref.1, bf16[128,1024]{1,0:T(8,128)(2,1)} %og_ref.1, s32[1,256]{1,0:T(1,128)} %bitcast.50, ...), custom_call_target="tpu_custom_call" | custom-call | flops 6499999744 | bytes 30000000 | tf_op jit(solution)/shard_map/layer/pallas_call | solution.py:531
  105.5 77.4 %reduce.1 = (f32[8,12416]{1,0:T(8,128)}, f32[8,128]{1,0:T(8,128)}) custom-call(bf16[4,16,2,32,128]{4,3,2,1,0:T(8,128)(2,1)} %bitcast.38, bf16[128,12416]{1,0:T(8,128)(2,1)} %get-tuple-element.47.z, f32[16,2,32,128]{3,2,1,0:T(8,128)} %bitcast.39, f32[8,128]{1,0:T(8,128)} %get-tuple-element.49.head), custom_call_target="tpu_custom_call" | custom-call | tf_op jit(solution)/shard_map/reduce/pallas_call | solution.py:724
  182.9 1.8 split.1

commit v3 on v2

v3 whole, which is shorter than its diff:
```python
import functools
import math

import jax
import jax.numpy as jnp
from jax import lax
from jax.experimental import pallas as pl
from jax.experimental.pallas import tpu as pltpu
from jax.sharding import Mesh
from jax.sharding import PartitionSpec as P

EPSILON = 1e-05
ROPE_BASE = 100000000000.0
DP_FSDP = ("dp_0", "dp_1", "dp_2", "fsdp")
OFF = dict(gate=(0, 1536), inner=(1536, 1792), query=(3328, 512), keyval=(3840, 256), step=(4096, 128),
           mix=(4224, 1536), attn=(5760, 512), gateup=(6272, 4096), down=(10368, 2048))
COLS = 12416
FIRST = 4224
F32, BF16 = jnp.float32, jnp.bfloat16
HIGH = lax.Precision.HIGHEST
AT_IN, AT_FFN, AT_MIX, AT_BIAS, AT_TAPS = 24, 32, 40, 52, 66
SMALLS = ((AT_IN, 8, 1024), (AT_FFN, 8, 1024), (AT_MIX, 12, 1536), (AT_BIAS, 14, 1792))
INVERSE = {8: 8192, 12: 5462, 14: 4682}


AX, AZ, AC, AY = "dp_0", "dp_1", "dp_2", "fsdp"
ORDERS = ((AX, AY, AZ), (AY, AZ, AX), (AZ, AX, AY))
MESH = pl.DeviceIdType.MESH
WHOLE = slice(None)


def places():
    return {a: lax.axis_index(a) for a in (AX, AZ, AC, AY)}


def greet(at):
    barrier = pltpu.get_barrier_semaphore()
    for a in (AX, AZ, AY):
        for d in (1, 2, 3):
            pl.semaphore_signal(barrier, inc=1, device_id={a: lax.rem(at[a] + d, 4)}, device_id_type=MESH)
    pl.semaphore_signal(barrier, inc=1, device_id={AC: 1 - at[AC]}, device_id_type=MESH)
    pl.semaphore_wait(barrier, 10)


def cut3(cols, start=0):
    tiles = cols // 128
    sizes = [tiles // 3 + (1 if k < tiles % 3 else 0) for k in range(3)]
    parts, at = [], start
    for n in sizes:
        lo = (n + 1) // 2 * 128
        parts.append((at, lo, n * 128 - lo))
        at += n * 128
    return parts


class Gather:
    def __init__(self, at, parts, shard, out, send, recv, sib_send, sib_recv):
        self.at, self.parts, self.shard, self.out = at, parts, shard, out
        self.sems, self.sib_sems = (send, recv), (sib_send, sib_recv)
        self.sent, self.sib, self.state = [], [], {}

    def block(self, sel, c0, n):
        return self.out.at[sel[AX], sel[AZ], self.at[AC], sel[AY], :, pl.ds(c0, n)]

    def to_sibling(self, part, k, sel, c0, n):
        ref = self.block(sel, c0, n)
        send, recv = self.sib_sems
        c = pltpu.make_async_remote_copy(ref, ref, send.at[part, k], recv.at[part, k],
                                         device_id={AC: 1 - self.at[AC]}, device_id_type=MESH)
        c.start()
        self.sib.append(c)

    def start(self, phase):
        send, recv = self.sems
        state = []
        for part, (c0, lo, hi) in enumerate(self.parts):
            order = ORDERS[part]
            a = order[phase]
            p = self.at[a]
            nxt, prv, opp = lax.rem(p + 1, 4), lax.rem(p + 3, 4), lax.rem(p + 2, 4)
            base = {b: self.at[b] for b in (AX, AZ, AY)}
            for b in order[:phase]:
                base[b] = WHOLE

            def mk(kind, q, cc, n, to, part=part, a=a, base=base):
                dst = self.block({**base, a: q}, cc, n)
                src = self.shard.at[:, pl.ds(cc, n)] if (phase == 0 and kind < 4) else dst
                return pltpu.make_async_remote_copy(src, dst, send.at[part, phase, kind], recv.at[part, phase, kind],
                                                    device_id={a: to}, device_id_type=MESH)
            copies = [mk(0, p, c0, lo, nxt), mk(1, p, c0 + lo, hi, prv), mk(2, p, c0 + lo, hi, nxt), mk(3, p, c0, lo, prv)]
            for c in copies:
                c.start()
            self.sent += copies
            if phase == 2:
                self.to_sibling(part, 0, base, c0, lo + hi)
            state.append((copies, mk, nxt, prv, opp, base, a, c0, lo, hi))
        self.state[phase] = state

    def forward(self, phase):
        self.fwd = []
        for part, (copies, mk, nxt, prv, opp, base, a, c0, lo, hi) in enumerate(self.state[phase]):
            copies[0].wait_recv()
            fr = mk(4, prv, c0, lo, nxt)
            fr.start()
            copies[1].wait_recv()
            fl = mk(5, nxt, c0 + lo, hi, prv)
            fl.start()
            if phase == 2:
                self.to_sibling(part, 1, {**base, a: prv}, c0, lo)
                self.to_sibling(part, 2, {**base, a: nxt}, c0 + lo, hi)
            self.fwd.append((fr, fl))
            self.sent += [fr, fl]

    def sides(self, phase):
        for part, (copies, mk, nxt, prv, opp, base, a, c0, lo, hi) in enumerate(self.state[phase]):
            copies[2].wait_recv()
            if phase == 2:
                self.to_sibling(part, 3, {**base, a: prv}, c0 + lo, hi)
            copies[3].wait_recv()
            if phase == 2:
                self.to_sibling(part, 4, {**base, a: nxt}, c0, lo)

    def finish(self, phase):
        for part, (copies, mk, nxt, prv, opp, base, a, c0, lo, hi) in enumerate(self.state[phase]):
            fr, fl = self.fwd[part]
            fr.wait_recv()
            if phase == 2:
                self.to_sibling(part, 5, {**base, a: opp}, c0, lo)
            fl.wait_recv()
            if phase == 2:
                self.to_sibling(part, 6, {**base, a: opp}, c0 + lo, hi)

    def shared(self):
        for c in self.sib:
            c.wait_recv()

    def drain(self):
        for c in self.sent + self.sib:
            c.wait_send()


class Reduce:
    def __init__(self, at, parts, grad, first, out, bufs, send, recv):
        self.at, self.parts, self.grad, self.first, self.out, self.bufs = at, parts, grad, first, out, bufs
        self.sems, self.sent, self.state = (send, recv), [], {0: [], 1: [], 2: []}

    def start(self, phase, part):
        send, recv = self.sems
        c0, lo, hi = self.parts[part]
        order = ORDERS[part][::-1]
        a = order[phase]
        p = self.at[a]
        nxt, prv, opp = lax.rem(p + 1, 4), lax.rem(p + 3, 4), lax.rem(p + 2, 4)
        base = {b: self.at[b] for b in (AX, AZ, AY)}
        for b in order[phase + 1:]:
            base[b] = WHOLE
        el, er, fr, fl = self.bufs[(part * 3 + phase) * 4:(part * 3 + phase) * 4 + 4]

        def ref(q, cc, n):
            sel = {**base, a: q}
            return self.grad.at[sel[AX], sel[AZ], sel[AY], :, pl.ds(cc - self.first, n)]

        def mk(kind, q, cc, n, dst, to):
            return pltpu.make_async_remote_copy(ref(q, cc, n), dst, send.at[part, phase, kind],
                                                recv.at[part, phase, kind], device_id={a: to}, device_id_type=MESH)
        lead = (WHOLE,) * (3 - phase)
        fr_lo, fr_hi = fr.at[lead + (pl.ds(0, lo),)], fr.at[lead + (pl.ds(lo, hi),)]
        fl_lo, fl_hi = fl.at[lead + (pl.ds(0, lo),)], fl.at[lead + (pl.ds(lo, hi),)]
        now = [mk(0, opp, c0, lo, el, prv), mk(1, opp, c0 + lo, hi, er, nxt), mk(2, prv, c0 + lo, hi, fr_hi, prv),
               mk(3, nxt, c0, lo, fl_lo, nxt)]
        for c in now:
            c.start()
        later = [mk(4, prv, c0, lo, fr_lo, prv), mk(5, nxt, c0 + lo, hi, fl_hi, nxt)]
        self.sent += now + later
        self.state[phase].append((now, later, ref(prv, c0, lo), ref(nxt, c0 + lo, hi), ref(p, c0, lo + hi), el, er, fr, fl))

    def each(self, phase, fn):
        if phase == 2:
            fn((WHOLE, WHOLE))
            return

        def one(k, carry):
            fn(((k // 4, k % 4) if phase == 0 else (k,)) + (WHOLE, WHOLE))
            return carry
        lax.fori_loop(0, 16 if phase == 0 else 4, one, 0)

    def middle(self, phase):
        for now, later, left, right, own, el, er, fr, fl in self.state[phase]:
            for c, onward, target, come in ((now[0], later[0], left, el), (now[1], later[1], right, er)):
                c.wait_recv()

                def add(ix, target=target, come=come):
                    target[ix] = target[ix] + come[ix]
                self.each(phase, add)
                onward.start()

    def finish(self, phase, then=None):
        for part, (now, later, left, right, own, el, er, fr, fl) in enumerate(self.state[phase]):
            for c in (now[2], now[3], later[0], later[1]):
                c.wait_recv()
            c0, lo, hi = self.parts[part]

            def total(ix, own=own, fl=fl, fr=fr, c0=c0, n=lo + hi):
                v = own[ix].astype(F32) + fl[ix].astype(F32) + fr[ix].astype(F32)
                if phase == 2:
                    self.out[:, pl.ds(c0, n)] = v
                else:
                    own[ix] = v.astype(BF16)
            self.each(phase, total)
            if phase < 2:
                self.start(phase + 1, part)

    def drain(self):
        for c in self.sent:
            c.wait_send()


def assemble(pieces, shard, tile):
    gate, inner, step, taps, cbias, mixer, mix, query, keyval, attn, gin, gffn, gateup, down = pieces
    for ref, (c0, n) in ((gate, OFF["gate"]), (inner, OFF["inner"]), (query, OFF["query"]), (keyval, OFF["keyval"]),
                         (mix, OFF["mix"]), (attn, OFF["attn"]), (gateup, OFF["gateup"]), (down, OFF["down"])):
        shard[:, c0:c0 + n] = ref[...]
    tile[...] = jnp.zeros((8, 128), F32)
    tile[:, 0:24] = step[...].astype(F32)
    tile[0:1, AT_IN:AT_IN + 8] = gin[...].astype(F32)
    tile[0:1, AT_FFN:AT_FFN + 8] = gffn[...].astype(F32)
    tile[0:1, AT_MIX:AT_MIX + 12] = mixer[...].astype(F32)
    tile[0:1, AT_BIAS:AT_BIAS + 14] = cbias[...].astype(F32)
    tile[0:4, AT_TAPS:AT_TAPS + 14] = taps[...].astype(F32)
    shard[:, 4096:4224] = tile[...].astype(BF16)


def nn(a, b, precision=None):
    return lax.dot_general(a, b, (((1,), (0,)), ((), ())), preferred_element_type=F32, precision=precision)


def nt(a, b, precision=None):
    return lax.dot_general(a, b, (((1,), (1,)), ((), ())), preferred_element_type=F32, precision=precision)


def tn(a, b, precision=None):
    return lax.dot_general(a, b, (((0,), (0,)), ((), ())), preferred_element_type=F32, precision=precision)


def sigmoid(v):
    return 1.0 / (1.0 + jnp.exp(-v))


def cols_of(i, n, start=0):
    return pl.ds(pl.multiple_of(start + i * n, 128), n)


def rms_back(values, scale, gain, grad):
    inner = grad * gain
    mean = jnp.mean(values * inner, axis=-1, keepdims=True)
    return scale * inner - values * (scale * scale * scale * mean), jnp.sum(grad * values * scale, axis=0, keepdims=True)


def row_scale(values):
    return lax.rsqrt(jnp.mean(values * values, axis=-1, keepdims=True) + EPSILON)


def selectors(i, start, n):
    d = lax.broadcasted_iota(jnp.int32, (128, 128), 1) + 128 * i
    row = lax.broadcasted_iota(jnp.int32, (128, 128), 0)
    owner = lax.shift_right_logical(d * INVERSE[n], 16)
    return row == owner, row == start + d - n * owner


def spread_row(table, start, n, width, dst, row=0):
    for i in range(width // 128):
        owned, lane = selectors(i, start, n)
        v = nn(table, lane.astype(F32).astype(BF16))
        dst[row:row + 1, 128 * i:128 * i + 128] = jnp.sum(jnp.where(owned, v, 0.0), axis=0, keepdims=True)


def unspread_row(src, start, n, width, row=0):
    total = jnp.zeros((128, 128), F32)
    for i in range(width // 128):
        owned, lane = selectors(i, start, n)
        held = jnp.where(owned, src[row:row + 1, 128 * i:128 * i + 128], 0.0)
        total = total + nt(held.astype(BF16), lane.astype(F32).astype(BF16))
    return total


SAVED = (("proj", (128, FIRST)), ("csum", (128, 1792)), ("conv", (128, 1792)), ("yfull", (128, 1536)), ("dec", (24, 128, 128)),
         ("soft", (8, 128, 128)), ("qr", (128, 512)), ("misc", (9, 128, 128)))


def forward_kernel(*refs):
    pieces, (x_ref, og_ref, lengths, owners, sbias_ref, dlog_ref, skip_ref) = refs[:14], refs[14:21]
    w, result, rt, zb, x1_s, dm_s, do_s, gffn_g, gin, gmix, taps, skipx, rows_s = refs[21:34]
    kept, (proj, csum, conv, yfull, dec, soft, qr, misc) = refs[34:42], refs[42:50]
    wv, df_s, gffn, cbias, table, shard, tile, wsem, own_sem, keep_sem, a_sems, b_sems, a_sib, b_sib = refs[50:]
    at = places()
    assemble(pieces, shard, tile)
    greet(at)
    own = pltpu.make_async_copy(shard, w.at[at[AX], at[AZ], at[AC], at[AY]], own_sem)
    own.start()
    first_group = Gather(at, cut3(FIRST), shard, w, a_sems.at[0], a_sems.at[1], a_sib.at[0], a_sib.at[1])
    second_group = Gather(at, cut3(COLS - FIRST, FIRST), shard, w, b_sems.at[0], b_sems.at[1], b_sib.at[0], b_sib.at[1])
    first_group.start(0)
    second_group.start(0)
    lane = lax.broadcasted_iota(jnp.int32, (128, 128), 1)
    sub = lax.broadcasted_iota(jnp.int32, (128, 128), 0)
    low_lanes = lane < 64

    me = ((at[AX] * 4 + at[AZ]) * 2 + at[AC]) * 4 + at[AY]
    owned = owners[...] == me
    held = jnp.where(owned, lengths[...], 0).astype(F32)
    before = lax.broadcasted_iota(jnp.int32, (256, 256), 0) <= lax.broadcasted_iota(jnp.int32, (256, 256), 1)
    ends = nn(jnp.broadcast_to(held, (8, 256)).astype(BF16), before.astype(F32).astype(BF16))[0:1, :]
    slot = lax.broadcasted_iota(jnp.int32, (128, 256), 0).astype(F32)
    closed = jnp.broadcast_to(owned.astype(F32), (128, 256)) * (jnp.broadcast_to(ends, (128, 256)) <= slot).astype(F32)
    segment = jnp.sum(closed, axis=1, keepdims=True)
    begins = jnp.max(closed * ends, axis=1, keepdims=True)
    used = jnp.max(ends, axis=1, keepdims=True)
    slots = sub.astype(F32)
    position = jnp.broadcast_to(slots[:, 0:1] - begins, (128, 128))
    active = (slots[:, 0:1] < used).astype(F32)
    segments = jnp.broadcast_to(segment, (128, 128))
    allowed = (segments == segments.T) & (sub >= lane)
    speeds = jnp.exp((lane % 32).astype(F32) * (-math.log(ROPE_BASE) * 2.0 / 64))
    angles = position * speeds
    cosine, sine = jnp.cos(angles), jnp.sin(angles)

    rows_s[...] = jnp.zeros((8, 128), F32)
    rows_s[0:1, 0:24] = sbias_ref[...].astype(F32)
    rows_s[1:2, 0:24] = dlog_ref[...].astype(F32)
    rows_s[2:3, 0:24] = skip_ref[...].astype(F32)
    sbias, dlog = rows_s[0:1, :], rows_s[1:2, :]
    heads_low = rows_s[...].astype(BF16)
    for i in range(12):
        of_head = (sub == 2 * i + lax.shift_right_logical(lane, 6)).astype(F32).astype(BF16)
        skipx[:, 128 * i:128 * i + 128] = nn(heads_low, of_head)[2:3, :]

    def halves(v):
        return jnp.where(low_lanes, v, 0.0), jnp.where(low_lanes, 0.0, v)

    def stacked(v):
        lo, hi = halves(v)
        return jnp.concatenate([lo, hi], axis=0).astype(BF16)

    first_group.forward(0)
    second_group.forward(0)
    first_group.sides(0)
    first_group.finish(0)
    own.wait()
    first_group.start(1)
    second_group.sides(0)
    second_group.finish(0)
    second_group.start(1)
    first_group.forward(1)
    first_group.sides(1)
    second_group.forward(1)
    first_group.finish(1)
    first_group.start(2)
    first_group.forward(2)
    second_group.sides(1)
    second_group.finish(1)
    second_group.start(2)
    first_group.sides(2)
    first_group.finish(2)
    first_group.shared()
    rows_of_w = w.reshape(1024, COLS)

    def load(k, c0, n):
        c = pltpu.make_async_copy(rows_of_w.at[:, pl.ds(c0, n)], wv.at[:, pl.ds(c0, n)], wsem.at[k])
        c.start()
        return c
    load(0, 0, FIRST).wait()
    table[...] = wv[:, 4096:4224].astype(F32)
    tables = [table[pl.ds(r, 128, stride=8), :].astype(BF16) for r in range(4)]
    for dst, (start, n, width) in zip((gin, gffn, gmix, cbias), SMALLS):
        spread_row(tables[0], start, n, width, dst)
    for r in range(4):
        spread_row(tables[r], AT_TAPS, 14, 1792, taps, r)

    x = x_ref[...].astype(F32)
    h = (x * row_scale(x) * gin[...]).astype(BF16)
    rt[0:1024, :] = h.T
    g0 = og_ref[...].astype(F32) * active
    glow = g0.astype(BF16)
    rt[3072:4096, :] = glow.T
    z_h = h

    def project(i, carry):
        proj[:, cols_of(i, 384)] = nn(z_h, wv[:, cols_of(i, 384)])
        return carry
    lax.fori_loop(0, 11, project, 0)

    def convolve(i, carry):
        cs = cols_of(i, 128)
        p = proj[:, cols_of(i, 128, 1536)]
        total = p * taps[3:4, cs]
        for j in (1, 2, 3):
            moved = jnp.where(position >= float(j), pltpu.roll(p, j, axis=0), 0.0)
            total = total + moved * taps[3 - j:4 - j, cs]
        total = total + cbias[:, cs]
        csum[:, cs] = total
        conv[:, cs] = total * sigmoid(total)
        return carry
    lax.fori_loop(0, 14, convolve, 0)

    step = proj[:, 4096:4224] + sbias
    dt = jnp.maximum(step, 0.0) + jnp.log(1.0 + jnp.exp(-jnp.abs(step)))
    rate = -jnp.exp(dlog)
    lower = (sub >= lane).astype(F32)
    level = nn(lower, dt * rate, HIGH)
    dt_t = dt.T
    level_t = level.T
    b_mat = conv[:, 1536:1664]
    c_mat = conv[:, 1664:1792]
    inter = nt(c_mat, b_mat, HIGH)

    second_group.forward(2)
    square = jnp.zeros((128, 1), F32)
    for t in range(12):
        cs = slice(128 * t, 128 * t + 128)
        mixes = []
        for n in (2 * t, 2 * t + 1):
            spread = jnp.where(allowed, level[:, n:n + 1] - level_t[n:n + 1, :], -1e30)
            decay = jnp.exp(spread)
            dec[n] = decay
            mixes.append((decay * inter * dt_t[n:n + 1, :]).astype(BF16))
        xs = conv[:, cs]
        y = nn(jnp.concatenate(mixes, axis=1), stacked(xs)) + skipx[:, cs] * xs
        yfull[:, cs] = y
        gate = proj[:, cs]
        gy = y * (gate * sigmoid(gate))
        square = square + jnp.sum(gy * gy, axis=1, keepdims=True)
    rmix = lax.rsqrt(square * (1.0 / 1536) + EPSILON)

    def mixer_norm(i, carry):
        cs = cols_of(i, 128)
        gate = proj[:, cs]
        gy = yfull[:, cs] * (gate * sigmoid(gate))
        zb[:, cols_of(i, 128)] = (gy * rmix * gmix[:, cs]).astype(BF16)
        return carry
    lax.fori_loop(0, 12, mixer_norm, 0)

    second_group.sides(2)
    first = (lane % 64) < 32

    def turn(v, sign):
        side = jnp.where(first, -pltpu.roll(v, 96, axis=1), pltpu.roll(v, 32, axis=1))
        return v * cosine + sign * side * sine

    def dup(v, j):
        other = pltpu.roll(v, 64, axis=1)
        return jnp.where(low_lanes, v, other) if j == 0 else jnp.where(low_lanes, other, v)
    key_t = turn(proj[:, 3840:3968], 1.0).astype(BF16).astype(F32)
    val = proj[:, 3968:4096].astype(BF16).astype(F32)
    keys = [dup(key_t, j) for j in (0, 1)]
    vals = [dup(val, j) for j in (0, 1)]
    for t in range(4):
        cs = slice(128 * t, 128 * t + 128)
        q = turn(proj[:, 3328 + 128 * t:3456 + 128 * t], 1.0).astype(BF16).astype(F32)
        qr[:, cs] = q
        scores = nt(stacked(q), keys[t // 2].astype(BF16)) * 0.125
        weights = []
        for e in (0, 1):
            s = jnp.where(allowed, scores[128 * e:128 * e + 128], -1e30)
            w = jnp.exp(s - jnp.max(s, axis=1, keepdims=True))
            w = w / jnp.sum(w, axis=1, keepdims=True)
            soft[2 * t + e] = w
            weights.append(w.astype(BF16))
        zb[:, 1536 + 128 * t:1664 + 128 * t] = nn(jnp.concatenate(weights, axis=1), stacked(vals[t // 2])).astype(BF16)

    for k, v in enumerate((key_t, val, dt, step, inter, jnp.broadcast_to(rmix, (128, 128)), position, cosine, sine)):
        misc[k] = v
    keeps = []
    for k, (src, dst) in enumerate(zip((proj, csum, conv, yfull, dec, soft, qr, misc), kept)):
        c = pltpu.make_async_copy(src, dst, keep_sem.at[k])
        c.start()
        keeps.append(c)
    second_group.finish(2)
    second_group.shared()
    loads = [load(1, 4224, 2048), load(2, 6272, 4096), load(3, 10368, 2048)]
    loads[0].wait()
    for i in range(4):
        rows = slice(256 * i, 256 * i + 256)
        x1_s[:, rows] = x_ref[:, rows].astype(F32) + nt(zb[:, 0:2048], wv[rows, 4224:6272])
    x1 = x1_s[...]
    r1 = row_scale(x1)
    f = (x1 * r1 * gffn[...]).astype(BF16)
    rt[2048:3072, :] = f.T

    loads[1].wait()
    loads[2].wait()

    def feed(i, carry):
        g = nn(f, wv[:, cols_of(i, 256, 6272)])
        u = nn(f, wv[:, cols_of(i, 256, 8320)])
        da = nn(glow, wv[:, cols_of(i, 256, 10368)])
        s = sigmoid(g)
        gs = g * s
        zb[:, cols_of(i, 256, 6144)] = (gs * u).astype(BF16)
        zb[:, cols_of(i, 256, 2048)] = (da * u * (s + gs * (1.0 - s))).astype(BF16)
        zb[:, cols_of(i, 256, 4096)] = (da * gs).astype(BF16)
        return carry
    lax.fori_loop(0, 8, feed, 0)
    for i in range(4):
        rows = slice(256 * i, 256 * i + 256)
        result[:, rows] = (x1_s[:, rows] + nt(zb[:, 6144:8192], wv[rows, 10368:12416])).astype(BF16)
        df_s[:, rows] = nt(zb[:, 2048:6144], wv[rows, 6272:10368])
    part, gain_grad = rms_back(x1, r1, gffn[...], df_s[...])
    gffn_g[...] = gain_grad
    dx1 = g0 + part
    x1_s[...] = dx1
    blow = dx1.astype(BF16)
    rt[1024:2048, :] = blow.T

    def back_branch(i, carry):
        dm_s[:, cols_of(i, 512)] = nn(blow, wv[:, cols_of(i, 512, 4224)])
        return carry
    lax.fori_loop(0, 3, back_branch, 0)
    do_s[...] = nn(blow, wv[:, 5760:6272])

    first_group.drain()
    second_group.drain()
    for c in keeps:
        c.wait()


def forward_call(*args):
    def of(*s, t=F32):
        return jax.ShapeDtypeStruct(s, t)
    vm, hbm = pl.BlockSpec(memory_space=pltpu.VMEM), pl.BlockSpec(memory_space=pl.ANY)
    return pl.pallas_call(
        forward_kernel,
        out_shape=[of(4, 4, 2, 4, 8, COLS, t=BF16), of(128, 1024, t=BF16), of(4096, 128, t=BF16),
                   of(128, COLS - FIRST, t=BF16), of(128, 1024), of(128, 1536), of(128, 512), of(1, 1024), of(1, 1024),
                   of(1, 1536), of(4, 1792), of(1, 1536), of(8, 128)] + [of(*s) for _, s in SAVED],
        in_specs=[vm] * 21,
        out_specs=[hbm] + [vm] * 12 + [hbm] * 8,
        scratch_shapes=[pltpu.VMEM(s, F32) for _, s in SAVED] + [
            pltpu.VMEM((1024, COLS), BF16), pltpu.VMEM((128, 1024), F32), pltpu.VMEM((1, 1024), F32),
            pltpu.VMEM((1, 1792), F32), pltpu.VMEM((1024, 128), F32), pltpu.VMEM((8, COLS), BF16), pltpu.VMEM((8, 128), F32),
            pltpu.SemaphoreType.DMA((4,)), pltpu.SemaphoreType.DMA, pltpu.SemaphoreType.DMA((8,)),
            pltpu.SemaphoreType.DMA((2, 3, 3, 6)), pltpu.SemaphoreType.DMA((2, 3, 3, 6)),
            pltpu.SemaphoreType.DMA((2, 3, 7)), pltpu.SemaphoreType.DMA((2, 3, 7)),
        ],
        compiler_params=pltpu.CompilerParams(collective_id=0, has_side_effects=True, vmem_limit_bytes=60 << 20),
        name="forward",
    )(*args)


PIECES_A = (((0, 0, 1280, 256), (0, 1280, 128, 128)), ((0, 1408, 1280, 256), (0, 2688, 128, 128)),
            ((0, 2816, 1280, 256), (0, 4096, 128, 128)))
PIECES_B = (((1, 4224, 2048, 256), (2, 6272, 768, 256)), ((2, 7040, 2688, 384),), ((2, 9728, 640, 128), (3, 10368, 2048, 256)))


def backward_kernel(x_ref, rt, zb, x1_s, dm_s, do_s, gffn_g, gin, gmix, taps, skipx, rows_s, w, *refs):
    kept, (dx, out, head_out), (proj, csum, conv, yfull, dec, soft, qr, misc) = refs[:8], refs[8:11], refs[11:19]
    (wv, z, df_s, dconv, ddt_s, gin_g, gmix_g, taps_g, cbias_g, small, head_g, grad_a, grad_b, zb_sib, za_sib, rt_sib,
     small_sib, wsem, keep_sem, x_send, x_recv, hnow, hbuf, h_send, h_recv, a_sems, b_sems) = refs[19:46]
    bufs_a, bufs_b = refs[46:82], refs[82:118]
    at = places()
    load = pltpu.make_async_copy(w.reshape(1024, COLS).at[:, pl.ds(0, FIRST)], wv, wsem)
    load.start()
    keeps = []
    for k, (src, dst) in enumerate(zip(kept, (proj, csum, conv, yfull, dec, soft, qr, misc))):
        c = pltpu.make_async_copy(src, dst, keep_sem.at[k])
        c.start()
        keeps.append(c)
    greet(at)
    core = at[AC]
    parts_a, parts_b = cut3(FIRST), cut3(COLS - FIRST, FIRST)
    swaps = {}

    def swap(k, src, dst):
        c = pltpu.make_async_remote_copy(src, dst, x_send.at[k], x_recv.at[k], device_id={AC: 1 - core}, device_id_type=MESH)
        c.start()
        swaps[k] = c

    def swap_columns(k, src, dst, part, first):
        c0, lo, hi = part
        cs = pl.ds(c0 - first, lo + hi)
        swap(k, src.at[:, cs], dst.at[:, cs])
    swap(0, rt.at[:, :, 1 - core], rt_sib)
    for part in range(3):
        swap_columns(1 + part, zb, zb_sib, parts_b[part], FIRST)

    def products(pieces, grad, mine, other, first):
        for g, c0, n, width in pieces:
            left = jnp.concatenate([rt[g, :, core].reshape(512, 128), rt_sib[g].reshape(512, 128)], axis=1)

            def one(i, carry, c0=c0, width=width, left=left):
                cs = pl.ds(pl.multiple_of(c0 - first + i * width, 128), width)
                right = jnp.concatenate([mine[:, cs], other[:, cs]], axis=0)
                grad[:, :, :, :, cs] = nn(left, right).reshape(4, 4, 4, 8, width).astype(BF16)
                return carry
            lax.fori_loop(0, n // width, one, 0)

    sum_a = Reduce(at, parts_a, grad_a, 0, out, bufs_a, a_sems.at[0], a_sems.at[1])
    sum_b = Reduce(at, parts_b, grad_b, FIRST, out, bufs_b, b_sems.at[0], b_sems.at[1])
    swaps[0].wait_recv()
    for part in range(3):
        swaps[1 + part].wait_recv()
        products(PIECES_B[part], grad_b, zb, zb_sib, FIRST)
        sum_b.start(0, part)

    axes, head_sent = (AX, AZ, AY), []

    def heads_go(k):
        a = axes[k]
        p = at[a]
        hbuf[k, p] = hnow[k]
        copies = []
        for d in (1, 2, 3):
            c = pltpu.make_async_remote_copy(hnow.at[k], hbuf.at[k, p], h_send.at[k, d - 1], h_recv.at[k, d - 1],
                                             device_id={a: lax.rem(p + d, 4)}, device_id_type=MESH)
            c.start()
            copies.append(c)
        head_sent.extend(copies)
        return copies

    def heads_come(k, copies):
        for c in copies:
            c.wait_recv()
        return ((hbuf[k, 0] + hbuf[k, 1]) + hbuf[k, 2]) + hbuf[k, 3]

    lane = lax.broadcasted_iota(jnp.int32, (128, 128), 1)
    sub = lax.broadcasted_iota(jnp.int32, (128, 128), 0)
    low_lanes = lane < 64
    def halves(v):
        return jnp.where(low_lanes, v, 0.0), jnp.where(low_lanes, 0.0, v)

    def stacked(v):
        lo, hi = halves(v)
        return jnp.concatenate([lo, hi], axis=0).astype(BF16)

    for c in keeps:
        c.wait()
    key_t, val, dt, step, inter, rmix, position, cosine, sine = [misc[k] for k in range(9)]
    rmix = rmix[:, 0:1]
    first = (lane % 64) < 32

    def turn(v, sign):
        side = jnp.where(first, -pltpu.roll(v, 96, axis=1), pltpu.roll(v, 32, axis=1))
        return v * cosine + sign * side * sine

    def dup(v, j):
        other = pltpu.roll(v, 64, axis=1)
        return jnp.where(low_lanes, v, other) if j == 0 else jnp.where(low_lanes, other, v)
    keys = [dup(key_t, j) for j in (0, 1)]
    vals = [dup(val, j) for j in (0, 1)]
    dks, dvs = [], []
    for t in range(4):
        cs = slice(128 * t, 128 * t + 128)
        do2 = stacked(do_s[:, cs])
        dp = nt(do2, vals[t // 2].astype(BF16))
        ds, ws = [], []
        for e in (0, 1):
            w = soft[2 * t + e]
            d = dp[128 * e:128 * e + 128]
            ds.append((w * (d - jnp.sum(d * w, axis=1, keepdims=True)) * 0.125).astype(BF16))
            ws.append(w.astype(BF16))
        dq = nn(jnp.concatenate(ds, axis=1), stacked(keys[t // 2]))
        z[:, 3328 + 128 * t:3456 + 128 * t] = turn(dq, -1.0).astype(BF16)
        dks.append(tn(jnp.concatenate(ds, axis=0), stacked(qr[:, cs])))
        dvs.append(tn(jnp.concatenate(ws, axis=0), do2))

    def fold(parts):
        a, b = parts[0] + parts[1], parts[2] + parts[3]
        return jnp.where(low_lanes, a + pltpu.roll(a, 64, axis=1), b + pltpu.roll(b, 64, axis=1))
    z[:, 3840:3968] = turn(fold(dks), -1.0).astype(BF16)
    z[:, 3968:4096] = fold(dvs).astype(BF16)

    dt_t = dt.T
    rate = -jnp.exp(rows_s[1:2, :])
    b_mat = conv[:, 1536:1664]
    c_mat = conv[:, 1664:1792]
    dots = jnp.zeros((128, 1), F32)
    for t in range(12):
        cs = slice(128 * t, 128 * t + 128)
        gate = proj[:, cs]
        gy = yfull[:, cs] * (gate * sigmoid(gate))
        dm = dm_s[:, cs]
        gmix_g[:, cs] = jnp.sum(dm * gy * rmix, axis=0, keepdims=True)
        dots = dots + jnp.sum(gy * dm * gmix[:, cs], axis=1, keepdims=True)
    pull = rmix * rmix * rmix * dots * (1.0 / 1536)
    ddt_s[...] = jnp.zeros((128, 128), F32)
    dlevel = jnp.zeros((128, 128), F32)
    dskip = jnp.zeros((1, 128), F32)
    lane_row = lane[0:1, :]
    dinter = jnp.zeros((128, 128), F32)
    for t in range(12):
        cs = slice(128 * t, 128 * t + 128)
        gate = proj[:, cs]
        s = sigmoid(gate)
        gs = gate * s
        y = yfull[:, cs]
        dgy = rmix * (gmix[:, cs] * dm_s[:, cs]) - y * gs * pull
        z[:, cs] = (dgy * y * (s + gs * (1.0 - s))).astype(BF16)
        dy = dgy * gs
        xs = conv[:, cs]
        skipped = jnp.sum(dy * xs, axis=0, keepdims=True)
        for e in (0, 1):
            in_head = (lane_row < 64) if e == 0 else (lane_row >= 64)
            dskip = dskip + jnp.where(lane_row == 2 * t + e,
                                      jnp.sum(jnp.where(in_head, skipped, 0.0), axis=1, keepdims=True), 0.0)
        dy2 = stacked(dy)
        dmix = nt(dy2, xs.astype(BF16))
        mixes = []
        for e in (0, 1):
            n = 2 * t + e
            dt_row = dt_t[n:n + 1, :]
            decay = dec[n]
            mixed = decay * inter
            dm = dmix[128 * e:128 * e + 128]
            mixes.append((mixed * dt_row).astype(BF16))
            dd = dm * dt_row
            dinter = dinter + dd * decay
            ddt_s[n:n + 1, :] = jnp.sum(dm * mixed, axis=0, keepdims=True)
            dlevel = dlevel + jnp.where(lane == n, jnp.sum(dd * mixed, axis=1, keepdims=True), 0.0)
        dconv[:, cs] = tn(jnp.concatenate(mixes, axis=0), dy2) + skipx[:, cs] * dy
    sum_b.middle(0)
    dconv[:, 1536:1664] = tn(dinter, c_mat, HIGH)
    dconv[:, 1664:1792] = nn(dinter, b_mat, HIGH)
    ddt = ddt_s[...].T
    dlevel = dlevel - ddt * dt
    upper = (sub <= lane).astype(F32)
    drate = nn(upper, dlevel, HIGH)
    dstep = jnp.where(lane < 24, (ddt + drate * rate) * sigmoid(step), 0.0)
    z[:, 4096:4224] = dstep.astype(BF16)
    head_g[...] = jnp.zeros((8, 128), F32)
    head_g[2:3, :] = dskip
    head_g[0:1, :] = jnp.sum(dstep, axis=0, keepdims=True)
    head_g[1:2, :] = jnp.sum(drate * dt * rate, axis=0, keepdims=True)

    def unconvolve(i, carry):
        cs = cols_of(i, 128)
        total = csum[:, cs]
        s = sigmoid(total)
        d = dconv[:, cs] * (s + total * s * (1.0 - s))
        p = proj[:, cols_of(i, 128, 1536)]
        cbias_g[:, cs] = jnp.sum(d, axis=0, keepdims=True)
        taps_g[3:4, cs] = jnp.sum(d * p, axis=0, keepdims=True)
        back = d * taps[3:4, cs]
        for j in (1, 2, 3):
            masked = jnp.where(position >= float(j), d, 0.0)
            taps_g[3 - j:4 - j, cs] = jnp.sum(masked * pltpu.roll(p, j, axis=0), axis=0, keepdims=True)
            back = back + pltpu.roll(masked, 128 - j, axis=0) * taps[3 - j:4 - j, cs]
        z[:, cols_of(i, 128, 1536)] = back.astype(BF16)
        return carry
    lax.fori_loop(0, 14, unconvolve, 0)

    for part in range(3):
        swap_columns(4 + part, z, za_sib, parts_a[part], 0)
    swap(8, head_g, hnow.at[3])
    load.wait()
    for i in range(4):
        rows = slice(256 * i, 256 * i + 256)
        df_s[:, rows] = nt(z[:, 0:FIRST], wv[rows, 0:FIRST])
    x = x_ref[...].astype(F32)
    part, gain_grad = rms_back(x, row_scale(x), gin[...], df_s[...])
    gin_g[...] = gain_grad
    dx[...] = x1_s[...] + part

    small_rows = small.reshape(1024, 128)
    small_rows[...] = jnp.zeros((1024, 128), F32)
    for r in range(4):
        total = unspread_row(taps_g, AT_TAPS, 14, 1792, r)
        if r == 0:
            for src, (start, n, width) in zip((gin_g, gffn_g, gmix_g, cbias_g), SMALLS):
                total = total + unspread_row(src, start, n, width)
        small_rows[pl.ds(r, 128, stride=8), :] = total


    swap(7, small.at[:, 1 - core], small_sib)
    swaps[8].wait_recv()
    hnow[0] = head_g[...] + hnow[3]
    moving = heads_go(0)
    for part in range(3):
        swaps[4 + part].wait_recv()
        products(PIECES_A[part], grad_a, z, za_sib, 0)
        if part == 2:
            swaps[7].wait_recv()
            tile = grad_a.at[:, :, :, :, pl.ds(4096, 128)]
            extra = small[:, core] + small_sib[...]
            tile[...] = (tile[...].astype(F32) + extra.reshape(4, 4, 4, 8, 128)).astype(BF16)
        sum_a.start(0, part)
    sum_b.finish(0)
    hnow[1] = heads_come(0, moving)
    moving = heads_go(1)
    sum_a.middle(0)
    sum_b.middle(1)
    sum_a.finish(0)
    hnow[2] = heads_come(1, moving)
    moving = heads_go(2)
    sum_b.finish(1)
    sum_a.middle(1)
    sum_b.middle(2)
    sum_a.finish(1)
    sum_b.finish(2)
    head_out[...] = heads_come(2, moving)
    sum_a.middle(2)
    sum_a.finish(2)
    sum_a.drain()
    sum_b.drain()
    for c in list(swaps.values()) + head_sent:
        c.wait_send()


def shapes_of(phase, cols):
    return (4,) * (2 - phase) + (8, cols)


def buffers(parts):
    return [pltpu.VMEM(shapes_of(phase, n), BF16) for c0, lo, hi in parts for phase in range(3)
            for n in (lo, hi, lo + hi, lo + hi)]


def backward_call(*args):
    def of(*s, t=F32):
        return jax.ShapeDtypeStruct(s, t)
    vm, hbm = pl.BlockSpec(memory_space=pltpu.VMEM), pl.BlockSpec(memory_space=pl.ANY)
    second = COLS - FIRST
    return pl.pallas_call(
        backward_kernel,
        out_shape=[of(128, 1024), of(8, COLS), of(8, 128)],
        in_specs=[vm] * 12 + [hbm] * 9,
        out_specs=[vm] * 3,
        scratch_shapes=[pltpu.VMEM(s, F32) for _, s in SAVED] + [
            pltpu.VMEM((1024, FIRST), BF16), pltpu.VMEM((128, FIRST), BF16), pltpu.VMEM((128, 1024), F32),
            pltpu.VMEM((128, 1792), F32), pltpu.VMEM((128, 128), F32), pltpu.VMEM((1, 1024), F32), pltpu.VMEM((1, 1536), F32),
            pltpu.VMEM((4, 1792), F32), pltpu.VMEM((1, 1792), F32), pltpu.VMEM((16, 2, 32, 128), F32),
            pltpu.VMEM((8, 128), F32), pltpu.VMEM((4, 4, 4, 8, FIRST), BF16), pltpu.VMEM((4, 4, 4, 8, second), BF16),
            pltpu.VMEM((128, second), BF16), pltpu.VMEM((128, FIRST), BF16), pltpu.VMEM((4, 16, 32, 128), BF16),
            pltpu.VMEM((16, 32, 128), F32), pltpu.SemaphoreType.DMA, pltpu.SemaphoreType.DMA((8,)),
            pltpu.SemaphoreType.DMA((9,)), pltpu.SemaphoreType.DMA((9,)),
            pltpu.VMEM((4, 8, 128), F32), pltpu.VMEM((3, 4, 8, 128), F32),
            pltpu.SemaphoreType.DMA((3, 3)), pltpu.SemaphoreType.DMA((3, 3)),
            pltpu.SemaphoreType.DMA((2, 3, 3, 6)), pltpu.SemaphoreType.DMA((2, 3, 3, 6)),
        ] + buffers(cut3(FIRST)) + buffers(cut3(second, FIRST)),
        compiler_params=pltpu.CompilerParams(collective_id=1, has_side_effects=True, vmem_limit_bytes=62 << 20),
        name="backward",
    )(*args)


SPLIT = ("gate", "inner", "query", "keyval", "mix", "attn", "gateup", "down")


def split_kernel(grads, head, *outs):
    for name, dst in zip(SPLIT, outs[:8]):
        start, n = OFF[name]
        dst[...] = grads[:, start:start + n]
    step, gin, gffn, gmix, cbias, taps, bias, decay, skip = outs[8:]
    tile = grads[:, 4096:4224]
    step[...] = tile[:, 0:24]
    gin[...] = tile[0:1, AT_IN:AT_IN + 8]
    gffn[...] = tile[0:1, AT_FFN:AT_FFN + 8]
    gmix[...] = tile[0:1, AT_MIX:AT_MIX + 12]
    cbias[...] = tile[0:1, AT_BIAS:AT_BIAS + 14]
    taps[...] = tile[0:4, AT_TAPS:AT_TAPS + 14]
    for r, dst in enumerate((bias, decay, skip)):
        dst[...] = head[r:r + 1, 0:24]


def split_call(grads, head):
    def of(*s):
        return jax.ShapeDtypeStruct(s, F32)
    vm = pl.BlockSpec(memory_space=pltpu.VMEM)
    return pl.pallas_call(
        split_kernel,
        out_shape=[of(8, OFF[k][1]) for k in SPLIT] + [of(8, 24), of(1, 8), of(1, 8), of(1, 12), of(1, 14), of(4, 14),
                                                       of(1, 24), of(1, 24), of(1, 24)],
        in_specs=[vm] * 2,
        out_specs=[vm] * 17,
        name="split",
    )(grads, head)


def body(tokens, seq_lengths, seq_owner, input_norm, gate_proj, inner_proj, step_proj, conv_weight, conv_bias, step_bias,
         decay_log, skip_gain, mixer_norm, mixer_out, query_proj, keyval_proj, attn_out, ffn_norm, gateup_proj, down_proj,
         out_grad):
    made = forward_call(gate_proj[0], inner_proj[0], step_proj[0], conv_weight[0], conv_bias, mixer_norm, mixer_out[0].T,
                        query_proj[0], keyval_proj[0], attn_out[0].T, input_norm, ffn_norm, gateup_proj[0], down_proj[0].T,
                        tokens, out_grad, seq_lengths.reshape(1, 256), seq_owner.reshape(1, 256), step_bias, decay_log,
                        skip_gain)
    weights, result, rt = made[:3]
    dx, grads, heads = backward_call(tokens, rt.reshape(4, 16, 2, 32, 128), *made[3:13], weights, *made[13:])
    (gate, inner, query, keyval, mix, attn, gateup, down, step, gin, gffn, gmix, cbias, taps, bias, decay,
     skip) = split_call(grads, heads)
    return (result, dx, gin, gate[None], inner[None], step[None], taps[None], cbias, bias, decay, skip, gmix, mix.T[None],
            query[None], keyval[None], attn.T[None], gffn, gateup[None], down.T[None])


def solution(mesh):
    split = Mesh(mesh.devices.reshape(4, 4, 2, mesh.shape["fsdp"]), DP_FSDP)
    rows, flat = P(DP_FSDP, None), P(None, DP_FSDP)
    weight, turned = P(None, DP_FSDP, None), P(None, None, DP_FSDP)
    in_specs = (rows, P(), P(), flat, weight, weight, weight, turned, flat, P(), P(), P(), flat, turned, weight, weight,
                turned, flat, weight, turned, rows)
    out_specs = (rows, rows, flat, weight, weight, weight, turned, flat, P(), P(), P(), flat, turned, weight, weight,
                 turned, flat, weight, turned)
    return jax.shard_map(body, mesh=split, in_specs=in_specs, out_specs=out_specs, check_vma=False)
```

time: 185 us -> 162 us (0.88)
  Pallas kernels: 184 us -> 158 us
  local copies, waits for them, and re-layouts: 0 us -> 2.59 us
    pallas_call x3 -> x2, Pallas kernels: 182 us -> 156 us  [the longest x1 85.1 us: forward_call(): pl.pallas_call(forward_kernel, out_shape=[of(4, 4, 2, 4, 8, COLS, t=BF16)...]
    unnamed x0 -> x4, local copies, waits for them, and re-layouts: none -> 2.59 us
where the time goes in v3:
time: 162 us; the launch traced here: 161 us
  Pallas kernels  158 us (98%)
  local copies, waits for them, and re-layouts  2.59 us (2%)
    pallas_call x1, Pallas kernels, forward_call(): pl.pallas_call(forward_kernel, out_shape=[of(4, 4, 2, 4, 8, COLS, t=BF16)...  85.1 us
    pallas_call x1, Pallas kernels, backward_call(): pl.pallas_call(backward_kernel, out_shape=[of(128, 1024), of(8, COLS), of...  70.6 us

profile of v3, /device:TPU:0, one launch (start us, length us, event | category | flops | bytes accessed | tf_op | source)
XLA Modules:
  0.0 160.9 jit_solution(17092556764550800721)
XLA Ops:
  0.7 85.1 %forward.1 = (bf16[4,4,2,4,8,12416]{5,4,3,2,1,0:T(8,128)(2,1)}, bf16[128,1024]{1,0:T(8,128)(2,1)}, bf16[4096,128]{1,0:T(8,128)(2,1)}, bf16[128,8192]{1,0:T(8,128...) custom-call(bf16[8,1536]{1,0:T(8,128)(2,1)} %bitcast.39, ...), custom_call_target="tpu_custom_call" | custom-call | tf_op jit(solution)/shard_map/forward/pallas_call | solution.py:530
  85.8 0.0 copy-start
  85.8 70.6 %backward.1 = (f32[128,1024]{1,0:T(8,128)}, f32[8,12416]{1,0:T(8,128)}, f32[8,128]{1,0:T(8,128)}) custom-call(bf16[128,1024]{1,0:T(8,128)(2,1)} %x_ref.1, bf16[4,16,2,32,128]{4,3,2,1,0:T(8,128)(2,1)} %bitcast.35, bf16[128,8192]{1,0:T(8,128)(2,1)} %get-tuple-element.62.zb, f32[128,1024]{1,0:T(8,128)} %get-tuple-element.63.x1_s, ...), custom_call_target="tpu_custom_call" | custom-call | tf_op jit(solution)/shard_map/backward/pallas_call | solution.py:821
  156.5 1.8 %split.1 = (f32[8,1536]{1,0:T(8,128)}, f32[8,1792]{1,0:T(8,128)}, f32[8,512]{1,0:T(8,128)}, f32[8,256]{1,0:T(8,128)}, f32[8,1536]{1,0:T(8,128)}, /*index=5*/f32[...) custom-call(f32[8,12416]{1,0:T(8,128)} %get-tuple-element.82.grads, ...), custom_call_target="tpu_custom_call" | custom-call | tf_op jit(solution)/shard_map/split/pallas_call | solution.py:866
  158.3 0.0 copy-done
  158.3 0.7 copy.42
  159.0 1.9 %copy.43 = f32[128,1024]{1,0:T(8,128)} copy(f32[128,1024]{1,0:T(8,128)} %get-tuple-element.121) | data formatting | bytes 1048576
Async XLA Ops:
  85.8 72.4 %copy-start = (bf16[128,1024]{1,0:T(8,128)(2,1)S(1)}, bf16[128,1024]{1,0:T(8,128)(2,1)}, u32[]{:S(2)}) copy-start(bf16[128,1024]{1,0:T(8,128)(2,1)} %get-tuple-element.120) | copy-start | bytes 786436

commit v4 on v3

--- a/solution.py
+++ b/solution.py
@@ -13,8 +13,9 @@
 ROPE_BASE = 100000000000.0
 DP_FSDP = ("dp_0", "dp_1", "dp_2", "fsdp")
 OFF = dict(gate=(0, 1536), inner=(1536, 1792), query=(3328, 512), keyval=(3840, 256), step=(4096, 128),
-           mix=(4224, 1536), attn=(5760, 512), gateup=(6272, 4096), down=(10368, 2048))
+           mix=(4224, 1536), attn=(5760, 512), down=(6272, 2048), gateup=(8320, 4096))
 COLS = 12416
+GATEUP = ((0, 8320), (2048, 9344), (1024, 10368), (3072, 11392))
 FIRST = 4224
 F32, BF16 = jnp.float32, jnp.bfloat16
 HIGH = lax.Precision.HIGHEST
@@ -33,13 +34,16 @@
     return {a: lax.axis_index(a) for a in (AX, AZ, AC, AY)}
 
 
-def greet(at):
+def greet_start(at):
     barrier = pltpu.get_barrier_semaphore()
     for a in (AX, AZ, AY):
         for d in (1, 2, 3):
             pl.semaphore_signal(barrier, inc=1, device_id={a: lax.rem(at[a] + d, 4)}, device_id_type=MESH)
     pl.semaphore_signal(barrier, inc=1, device_id={AC: 1 - at[AC]}, device_id_type=MESH)
-    pl.semaphore_wait(barrier, 10)
+
+
+def greet_end():
+    pl.semaphore_wait(pltpu.get_barrier_semaphore(), 10)
 
 
 def cut3(cols, start=0):
@@ -87,6 +91,13 @@
                 src = self.shard.at[:, pl.ds(cc, n)] if (phase == 0 and kind < 4) else dst
                 return pltpu.make_async_remote_copy(src, dst, send.at[part, phase, kind], recv.at[part, phase, kind],
                                                     device_id={a: to}, device_id_type=MESH)
+            if phase == 0:
+                copies = [mk(k, p, c0, lo + hi, to) for k, to in enumerate((nxt, prv, opp))]
+                for c in copies:
+                    c.start()
+                self.sent += copies
+                state.append(copies)
+                continue
             copies = [mk(0, p, c0, lo, nxt), mk(1, p, c0 + lo, hi, prv), mk(2, p, c0 + lo, hi, nxt), mk(3, p, c0, lo, prv)]
             for c in copies:
                 c.start()
@@ -121,6 +132,11 @@
                 self.to_sibling(part, 4, {**base, a: nxt}, c0, lo)
 
     def finish(self, phase):
+        if phase == 0:
+            for copies in self.state[0]:
+                for c in copies:
+                    c.wait_recv()
+            return
         for part, (copies, mk, nxt, prv, opp, base, a, c0, lo, hi) in enumerate(self.state[phase]):
             fr, fl = self.fwd[part]
             fr.wait_recv()
@@ -163,6 +179,13 @@
         def mk(kind, q, cc, n, dst, to):
             return pltpu.make_async_remote_copy(ref(q, cc, n), dst, send.at[part, phase, kind],
                                                 recv.at[part, phase, kind], device_id={a: to}, device_id_type=MESH)
+        if phase == 2:
+            now = [mk(k, q, c0, lo + hi, dst, q) for k, (q, dst) in enumerate(((nxt, el), (prv, er), (opp, fr)))]
+            for c in now:
+                c.start()
+            self.sent += now
+            self.state[2].append((now, ref(p, c0, lo + hi), (el, er, fr)))
+            return
         lead = (WHOLE,) * (3 - phase)
         fr_lo, fr_hi = fr.at[lead + (pl.ds(0, lo),)], fr.at[lead + (pl.ds(lo, hi),)]
         fl_lo, fl_hi = fl.at[lead + (pl.ds(0, lo),)], fl.at[lead + (pl.ds(lo, hi),)]
@@ -175,10 +198,6 @@
         self.state[phase].append((now, later, ref(prv, c0, lo), ref(nxt, c0 + lo, hi), ref(p, c0, lo + hi), el, er, fr, fl))
 
     def each(self, phase, fn):
-        if phase == 2:
-            fn((WHOLE, WHOLE))
-            return
-
         def one(k, carry):
             fn(((k // 4, k % 4) if phase == 0 else (k,)) + (WHOLE, WHOLE))
             return carry
@@ -194,21 +213,25 @@
                 self.each(phase, add)
                 onward.start()
 
-    def finish(self, phase, then=None):
+    def last(self):
+        for (c0, lo, hi), (now, own, come) in zip(self.parts, self.state[2]):
+            for c in now:
+                c.wait_recv()
+            total = own[...].astype(F32)
+            for ref in come:
+                total = total + ref[...].astype(F32)
+            self.out[:, pl.ds(c0, lo + hi)] = total
+
+    def finish(self, phase):
         for part, (now, later, left, right, own, el, er, fr, fl) in enumerate(self.state[phase]):
             for c in (now[2], now[3], later[0], later[1]):
                 c.wait_recv()
-            c0, lo, hi = self.parts[part]
-
-            def total(ix, own=own, fl=fl, fr=fr, c0=c0, n=lo + hi):
+
+            def total(ix, own=own, fl=fl, fr=fr):
                 v = own[ix].astype(F32) + fl[ix].astype(F32) + fr[ix].astype(F32)
-                if phase == 2:
-                    self.out[:, pl.ds(c0, n)] = v
-                else:
-                    own[ix] = v.astype(BF16)
+                own[ix] = v.astype(BF16)
             self.each(phase, total)
-            if phase < 2:
-                self.start(phase + 1, part)
+            self.start(phase + 1, part)
 
     def drain(self):
         for c in self.sent:
@@ -217,8 +240,10 @@
 
 def assemble(pieces, shard, tile):
     gate, inner, step, taps, cbias, mixer, mix, query, keyval, attn, gin, gffn, gateup, down = pieces
+    for src, dst in GATEUP:
+        shard[:, dst:dst + 1024] = gateup[:, src:src + 1024]
     for ref, (c0, n) in ((gate, OFF["gate"]), (inner, OFF["inner"]), (query, OFF["query"]), (keyval, OFF["keyval"]),
-                         (mix, OFF["mix"]), (attn, OFF["attn"]), (gateup, OFF["gateup"]), (down, OFF["down"])):
+                         (mix, OFF["mix"]), (attn, OFF["attn"]), (down, OFF["down"])):
         shard[:, c0:c0 + n] = ref[...]
     tile[...] = jnp.zeros((8, 128), F32)
     tile[:, 0:24] = step[...].astype(F32)
@@ -283,24 +308,28 @@
     return total
 
 
-SAVED = (("proj", (128, FIRST)), ("csum", (128, 1792)), ("conv", (128, 1792)), ("yfull", (128, 1536)), ("dec", (24, 128, 128)),
-         ("soft", (8, 128, 128)), ("qr", (128, 512)), ("misc", (9, 128, 128)))
+GROUPS = ((0, FIRST), (FIRST, 4096), (8320, 2048), (10368, 2048))
+SAVED = ((128, FIRST), (128, 1792), (128, 1792), (128, 1536), (24, 128, 128), (8, 128, 128), (128, 512), (9, 128, 128),
+         (128, 1024), (128, 1024), (128, COLS - FIRST), (4096, 128))
+KINDS = (F32,) * 10 + (BF16,) * 2
 
 
 def forward_kernel(*refs):
     pieces, (x_ref, og_ref, lengths, owners, sbias_ref, dlog_ref, skip_ref) = refs[:14], refs[14:21]
-    w, result, rt, zb, x1_s, dm_s, do_s, gffn_g, gin, gmix, taps, skipx, rows_s = refs[21:34]
-    kept, (proj, csum, conv, yfull, dec, soft, qr, misc) = refs[34:42], refs[42:50]
-    wv, df_s, gffn, cbias, table, shard, tile, wsem, own_sem, keep_sem, a_sems, b_sems, a_sib, b_sib = refs[50:]
+    w, gffn_g, gin, gmix, taps, skipx, rows_s, zb_sib, rt_sib = refs[21:30]
+    kept, (proj, csum, conv, yfull, dec, soft, qr, misc, dx1_s, x1_s, zb, rt) = refs[30:42], refs[42:54]
+    (wv, df_s, da_s, gffn, cbias, table, shard, tile, wsem, own_sem, keep_sem, sems, sib_sems, x_send, x_recv) = refs[54:]
     at = places()
+    greet_start(at)
     assemble(pieces, shard, tile)
-    greet(at)
+    greet_end()
     own = pltpu.make_async_copy(shard, w.at[at[AX], at[AZ], at[AC], at[AY]], own_sem)
     own.start()
-    first_group = Gather(at, cut3(FIRST), shard, w, a_sems.at[0], a_sems.at[1], a_sib.at[0], a_sib.at[1])
-    second_group = Gather(at, cut3(COLS - FIRST, FIRST), shard, w, b_sems.at[0], b_sems.at[1], b_sib.at[0], b_sib.at[1])
-    first_group.start(0)
-    second_group.start(0)
+    groups = [Gather(at, cut3(n, c0), shard, w, sems.at[0, k], sems.at[1, k], sib_sems.at[0, k], sib_sems.at[1, k])
+              for k, (c0, n) in enumerate(GROUPS)]
+    one, two, three, four = groups
+    for g in groups:
+        g.start(0)
     lane = lax.broadcasted_iota(jnp.int32, (128, 128), 1)
     sub = lax.broadcasted_iota(jnp.int32, (128, 128), 0)
     low_lanes = lane < 64
@@ -341,33 +370,47 @@
         lo, hi = halves(v)
         return jnp.concatenate([lo, hi], axis=0).astype(BF16)
 
-    first_group.forward(0)
-    second_group.forward(0)
-    first_group.sides(0)
-    first_group.finish(0)
     own.wait()
-    first_group.start(1)
-    second_group.sides(0)
-    second_group.finish(0)
-    second_group.start(1)
-    first_group.forward(1)
-    first_group.sides(1)
-    second_group.forward(1)
-    first_group.finish(1)
-    first_group.start(2)
-    first_group.forward(2)
-    second_group.sides(1)
-    second_group.finish(1)
-    second_group.start(2)
-    first_group.sides(2)
-    first_group.finish(2)
-    first_group.shared()
+    for g in groups:
+        g.finish(0)
+        g.start(1)
+    for g in groups:
+        g.forward(1)
+    one.sides(1)
+    one.finish(1)
+    one.start(2)
+    one.forward(2)
+    two.sides(1)
+    two.finish(1)
+    two.start(2)
+    one.sides(2)
+    one.finish(2)
+    two.forward(2)
+    for g in (three, four):
+        g.sides(1)
+        g.finish(1)
+        g.start(2)
+    one.shared()
     rows_of_w = w.reshape(1024, COLS)
 
     def load(k, c0, n):
         c = pltpu.make_async_copy(rows_of_w.at[:, pl.ds(c0, n)], wv.at[:, pl.ds(c0, n)], wsem.at[k])
         c.start()
         return c
+    swaps = []
+    rt5 = rt.reshape(4, 16, 2, 32, 128)
+
+    def swap(k, src, dst):
+        c = pltpu.make_async_remote_copy(src, dst, x_send.at[k], x_recv.at[k], device_id={AC: 1 - at[AC]},
+                                         device_id_type=MESH)
+        c.start()
+        swaps.append(c)
+
+    def swap_rows(g):
+        swap(g, rt5.at[g, :, 1 - at[AC]], rt_sib.at[g])
+
+    def swap_columns(k, c0):
+        swap(k, zb.at[:, pl.ds(c0, 2048)], zb_sib.at[:, pl.ds(c0, 2048)])
     load(0, 0, FIRST).wait()
     table[...] = wv[:, 4096:4224].astype(F32)
     tables = [table[pl.ds(r, 128, stride=8), :].astype(BF16) for r in range(4)]
@@ -382,6 +425,8 @@
     g0 = og_ref[...].astype(F32) * active
     glow = g0.astype(BF16)
     rt[3072:4096, :] = glow.T
+    swap_rows(0)
+    swap_rows(3)
     z_h = h
 
     def project(i, carry):
@@ -413,9 +458,25 @@
     c_mat = conv[:, 1664:1792]
     inter = nt(c_mat, b_mat, HIGH)
 
-    second_group.forward(2)
     square = jnp.zeros((128, 1), F32)
-    for t in range(12):
+    for t in range(6):
+        cs = slice(128 * t, 128 * t + 128)
+        mixes = []
+        for n in (2 * t, 2 * t + 1):
+            spread = jnp.where(allowed, level[:, n:n + 1] - level_t[n:n + 1, :], -1e30)
+            decay = jnp.exp(spread)
+            dec[n] = decay
+            mixes.append((decay * inter * dt_t[n:n + 1, :]).astype(BF16))
+        xs = conv[:, cs]
+        y = nn(jnp.concatenate(mixes, axis=1), stacked(xs)) + skipx[:, cs] * xs
+        yfull[:, cs] = y
+        gate = proj[:, cs]
+        gy = y * (gate * sigmoid(gate))
+        square = square + jnp.sum(gy * gy, axis=1, keepdims=True)
+    two.sides(2)
+    two.finish(2)
+    three.forward(2)
+    for t in range(6, 12):
         cs = slice(128 * t, 128 * t + 128)
         mixes = []
         for n in (2 * t, 2 * t + 1):
@@ -439,7 +500,7 @@
         return carry
     lax.fori_loop(0, 12, mixer_norm, 0)
 
-    second_group.sides(2)
+    four.forward(2)
     first = (lane % 64) < 32
 
     def turn(v, sign):
@@ -470,13 +531,18 @@
     for k, v in enumerate((key_t, val, dt, step, inter, jnp.broadcast_to(rmix, (128, 128)), position, cosine, sine)):
         misc[k] = v
     keeps = []
-    for k, (src, dst) in enumerate(zip((proj, csum, conv, yfull, dec, soft, qr, misc), kept)):
-        c = pltpu.make_async_copy(src, dst, keep_sem.at[k])
-        c.start()
-        keeps.append(c)
-    second_group.finish(2)
-    second_group.shared()
-    loads = [load(1, 4224, 2048), load(2, 6272, 4096), load(3, 10368, 2048)]
+
+    def keep(*which):
+        for k in which:
+            c = pltpu.make_async_copy(refs[42 + k], kept[k], keep_sem.at[k])
+            c.start()
+            keeps.append(c)
+    keep(0, 1, 2, 3, 4, 5, 6, 7)
+    swap_columns(4, 0)
+    two.shared()
+    loads = [load(1, 4224, 4096)]
+    three.sides(2)
+    four.sides(2)
     loads[0].wait()
     for i in range(4):
         rows = slice(256 * i, 256 * i + 256)
@@ -485,40 +551,49 @@
     r1 = row_scale(x1)
     f = (x1 * r1 * gffn[...]).astype(BF16)
     rt[2048:3072, :] = f.T
-
-    loads[1].wait()
-    loads[2].wait()
-
-    def feed(i, carry):
-        g = nn(f, wv[:, cols_of(i, 256, 6272)])
-        u = nn(f, wv[:, cols_of(i, 256, 8320)])
-        da = nn(glow, wv[:, cols_of(i, 256, 10368)])
-        s = sigmoid(g)
-        gs = g * s
-        zb[:, cols_of(i, 256, 6144)] = (gs * u).astype(BF16)
-        zb[:, cols_of(i, 256, 2048)] = (da * u * (s + gs * (1.0 - s))).astype(BF16)
-        zb[:, cols_of(i, 256, 4096)] = (da * gs).astype(BF16)
+    swap_rows(2)
+    three.finish(2)
+
+    def back_down(i, carry):
+        da_s[:, cols_of(i, 512)] = nn(glow, wv[:, cols_of(i, 512, 6272)])
         return carry
-    lax.fori_loop(0, 8, feed, 0)
-    for i in range(4):
-        rows = slice(256 * i, 256 * i + 256)
-        result[:, rows] = (x1_s[:, rows] + nt(zb[:, 6144:8192], wv[rows, 10368:12416])).astype(BF16)
-        df_s[:, rows] = nt(zb[:, 2048:6144], wv[rows, 6272:10368])
-    part, gain_grad = rms_back(x1, r1, gffn[...], df_s[...])
+    lax.fori_loop(0, 4, back_down, 0)
+
+    four.finish(2)
+
+    for k, g in enumerate((three, four)):
+        base = 8320 + 2048 * k
+        g.shared()
+        load(2 + k, base, 2048).wait()
+        for i in range(4):
+            gate = nn(f, wv[:, base + 256 * i:base + 256 * i + 256])
+            up = nn(f, wv[:, base + 1024 + 256 * i:base + 1280 + 256 * i])
+            da = da_s[:, 1024 * k + 256 * i:1024 * k + 256 * i + 256]
+            s = sigmoid(gate)
+            gs = gate * s
+            at_a, at_g = 2048 + 1024 * k + 256 * i, 4096 + 2048 * k + 256 * i
+            zb[:, at_a:at_a + 256] = (gs * up).astype(BF16)
+            zb[:, at_g:at_g + 256] = (da * up * (s + gs * (1.0 - s))).astype(BF16)
+            zb[:, at_g + 1024:at_g + 1280] = (da * gs).astype(BF16)
+        swap_columns(5 + k, 4096 + 2048 * k)
+        if k == 1:
+            swap_columns(7, 2048)
+            keep(9, 10)
+        for i in range(4):
+            rows = slice(256 * i, 256 * i + 256)
+            term = nt(zb[:, 4096 + 2048 * k:6144 + 2048 * k], wv[rows, base:base + 2048])
+            df_s[:, rows] = term if k == 0 else df_s[:, rows] + term
+    part, gain_grad = rms_back(x1_s[...], r1, gffn[...], df_s[...])
     gffn_g[...] = gain_grad
     dx1 = g0 + part
-    x1_s[...] = dx1
-    blow = dx1.astype(BF16)
-    rt[1024:2048, :] = blow.T
-
-    def back_branch(i, carry):
-        dm_s[:, cols_of(i, 512)] = nn(blow, wv[:, cols_of(i, 512, 4224)])
-        return carry
-    lax.fori_loop(0, 3, back_branch, 0)
-    do_s[...] = nn(blow, wv[:, 5760:6272])
-
-    first_group.drain()
-    second_group.drain()
+    dx1_s[...] = dx1
+    rt[1024:2048, :] = dx1.astype(BF16).T
+    swap_rows(1)
+    keep(8, 11)
+    for g in groups:
+        g.drain()
+    for c in swaps:
+        c.wait()
     for c in keeps:
         c.wait()
 
@@ -529,17 +604,17 @@
     vm, hbm = pl.BlockSpec(memory_space=pltpu.VMEM), pl.BlockSpec(memory_space=pl.ANY)
     return pl.pallas_call(
         forward_kernel,
-        out_shape=[of(4, 4, 2, 4, 8, COLS, t=BF16), of(128, 1024, t=BF16), of(4096, 128, t=BF16),
-                   of(128, COLS - FIRST, t=BF16), of(128, 1024), of(128, 1536), of(128, 512), of(1, 1024), of(1, 1024),
-                   of(1, 1536), of(4, 1792), of(1, 1536), of(8, 128)] + [of(*s) for _, s in SAVED],
+        out_shape=[of(4, 4, 2, 4, 8, COLS, t=BF16), of(1, 1024), of(1, 1024), of(1, 1536),
+                   of(4, 1792), of(1, 1536), of(8, 128), of(128, COLS - FIRST, t=BF16), of(4, 16, 32, 128, t=BF16)]
+        + [of(*s, t=t) for s, t in zip(SAVED, KINDS)],
         in_specs=[vm] * 21,
-        out_specs=[hbm] + [vm] * 12 + [hbm] * 8,
-        scratch_shapes=[pltpu.VMEM(s, F32) for _, s in SAVED] + [
-            pltpu.VMEM((1024, COLS), BF16), pltpu.VMEM((128, 1024), F32), pltpu.VMEM((1, 1024), F32),
-            pltpu.VMEM((1, 1792), F32), pltpu.VMEM((1024, 128), F32), pltpu.VMEM((8, COLS), BF16), pltpu.VMEM((8, 128), F32),
-            pltpu.SemaphoreType.DMA((4,)), pltpu.SemaphoreType.DMA, pltpu.SemaphoreType.DMA((8,)),
-            pltpu.SemaphoreType.DMA((2, 3, 3, 6)), pltpu.SemaphoreType.DMA((2, 3, 3, 6)),
-            pltpu.SemaphoreType.DMA((2, 3, 7)), pltpu.SemaphoreType.DMA((2, 3, 7)),
+        out_specs=[hbm] + [vm] * 6 + [hbm] * 14,
+        scratch_shapes=[pltpu.VMEM(s, t) for s, t in zip(SAVED, KINDS)] + [
+            pltpu.VMEM((1024, COLS), BF16), pltpu.VMEM((128, 1024), F32), pltpu.VMEM((128, 2048), F32),
+            pltpu.VMEM((1, 1024), F32), pltpu.VMEM((1, 1792), F32), pltpu.VMEM((1024, 128), F32), pltpu.VMEM((8, COLS), BF16),
+            pltpu.VMEM((8, 128), F32), pltpu.SemaphoreType.DMA((10,)), pltpu.SemaphoreType.DMA,
+            pltpu.SemaphoreType.DMA((12,)), pltpu.SemaphoreType.DMA((2, 4, 3, 3, 6)), pltpu.SemaphoreType.DMA((2, 4, 3, 7)),
+            pltpu.SemaphoreType.DMA((8,)), pltpu.SemaphoreType.DMA((8,)),
         ],
         compiler_params=pltpu.CompilerParams(collective_id=0, has_side_effects=True, vmem_limit_bytes=60 << 20),
         name="forward",
@@ -548,25 +623,36 @@
 
 PIECES_A = (((0, 0, 1280, 256), (0, 1280, 128, 128)), ((0, 1408, 1280, 256), (0, 2688, 128, 128)),
             ((0, 2816, 1280, 256), (0, 4096, 128, 128)))
-PIECES_B = (((1, 4224, 2048, 256), (2, 6272, 768, 256)), ((2, 7040, 2688, 384),), ((2, 9728, 640, 128), (3, 10368, 2048, 256)))
-
-
-def backward_kernel(x_ref, rt, zb, x1_s, dm_s, do_s, gffn_g, gin, gmix, taps, skipx, rows_s, w, *refs):
-    kept, (dx, out, head_out), (proj, csum, conv, yfull, dec, soft, qr, misc) = refs[:8], refs[8:11], refs[11:19]
-    (wv, z, df_s, dconv, ddt_s, gin_g, gmix_g, taps_g, cbias_g, small, head_g, grad_a, grad_b, zb_sib, za_sib, rt_sib,
-     small_sib, wsem, keep_sem, x_send, x_recv, hnow, hbuf, h_send, h_recv, a_sems, b_sems) = refs[19:46]
-    bufs_a, bufs_b = refs[46:82], refs[82:118]
+PIECES_B = (((1, 4224, 2048, 256), (3, 6272, 768, 256)), ((3, 7040, 1280, 256), (2, 8320, 1280, 256), (2, 9600, 128, 128)),
+            ((2, 9728, 2688, 384),))
+
+
+def backward_kernel(x_ref, gffn_g, gin, gmix, taps, skipx, rows_s, w, zb_sib_in, rt_sib_in, *refs):
+    kept, (result, dx, out, head_out) = refs[:12], refs[12:16]
+    proj, csum, conv, yfull, dec, soft, qr, misc, dx1_s, x1_s, zb, rt = refs[16:28]
+    (wv, z, df_s, dm_s, do_s, dconv, ddt_s, gin_g, gmix_g, taps_g, cbias_g, small, head_g, grad_a, grad_b, zb_sib, za_sib,
+     rt_sib, small_sib, wsem, keep_sem, x_send, x_recv, hnow, hbuf, h_send, h_recv, a_sems, b_sems) = refs[28:57]
+    bufs_a, bufs_b = refs[57:93], refs[93:129]
     at = places()
-    load = pltpu.make_async_copy(w.reshape(1024, COLS).at[:, pl.ds(0, FIRST)], wv, wsem)
-    load.start()
-    keeps = []
-    for k, (src, dst) in enumerate(zip(kept, (proj, csum, conv, yfull, dec, soft, qr, misc))):
+    greet_start(at)
+
+    def bring(k, src, dst):
         c = pltpu.make_async_copy(src, dst, keep_sem.at[k])
         c.start()
-        keeps.append(c)
-    greet(at)
+        return c
+    sides = [bring(12, kept[11], rt), bring(13, rt_sib_in, rt_sib)]
+    parts_a, parts_b = cut3(FIRST), cut3(COLS - FIRST, FIRST)
+    columns = []
+    for part, (c0, lo, hi) in enumerate(parts_b):
+        cs = pl.ds(c0 - FIRST, lo + hi)
+        columns.append((bring(14 + part, kept[10].at[:, cs], zb.at[:, cs]),
+                        bring(17 + part, zb_sib_in.at[:, cs], zb_sib.at[:, cs])))
+    keeps = [bring(k, kept[k], refs[16 + k]) for k in range(10)]
+    rows_of_w = w.reshape(1024, COLS)
+    load = pltpu.make_async_copy(rows_of_w.at[:, pl.ds(FIRST, 4096)], wv.at[:, pl.ds(0, 4096)], wsem.at[0])
+    load.start()
     core = at[AC]
-    parts_a, parts_b = cut3(FIRST), cut3(COLS - FIRST, FIRST)
+    rt = rt.reshape(4, 16, 2, 32, 128)
     swaps = {}
 
     def swap(k, src, dst):
@@ -578,9 +664,6 @@
         c0, lo, hi = part
         cs = pl.ds(c0 - first, lo + hi)
         swap(k, src.at[:, cs], dst.at[:, cs])
-    swap(0, rt.at[:, :, 1 - core], rt_sib)
-    for part in range(3):
-        swap_columns(1 + part, zb, zb_sib, parts_b[part], FIRST)
 
     def products(pieces, grad, mine, other, first):
         for g, c0, n, width in pieces:
@@ -595,10 +678,14 @@
 
     sum_a = Reduce(at, parts_a, grad_a, 0, out, bufs_a, a_sems.at[0], a_sems.at[1])
     sum_b = Reduce(at, parts_b, grad_b, FIRST, out, bufs_b, b_sems.at[0], b_sems.at[1])
-    swaps[0].wait_recv()
+    for c in sides:
+        c.wait()
     for part in range(3):
-        swaps[1 + part].wait_recv()
+        for c in columns[part]:
+            c.wait()
         products(PIECES_B[part], grad_b, zb, zb_sib, FIRST)
+        if part == 0:
+            greet_end()
         sum_b.start(0, part)
 
     axes, head_sent = (AX, AZ, AY), []
@@ -633,6 +720,19 @@
 
     for c in keeps:
         c.wait()
+    load.wait()
+    blow = dx1_s[...].astype(BF16)
+
+    def back_branch(i, carry):
+        dm_s[:, cols_of(i, 512)] = nn(blow, wv[:, cols_of(i, 512)])
+        return carry
+    lax.fori_loop(0, 3, back_branch, 0)
+    do_s[...] = nn(blow, wv[:, 1536:2048])
+    for i in range(4):
+        rows = slice(256 * i, 256 * i + 256)
+        result[:, rows] = (x1_s[:, rows] + nt(zb[:, 2048:4096], wv[rows, 2048:4096])).astype(BF16)
+    load = pltpu.make_async_copy(rows_of_w.at[:, pl.ds(0, FIRST)], wv, wsem.at[1])
+    load.start()
     key_t, val, dt, step, inter, rmix, position, cosine, sine = [misc[k] for k in range(9)]
     rmix = rmix[:, 0:1]
     first = (lane % 64) < 32
@@ -750,6 +850,13 @@
     for part in range(3):
         swap_columns(4 + part, z, za_sib, parts_a[part], 0)
     swap(8, head_g, hnow.at[3])
+    for part in range(2):
+        swaps[4 + part].wait_recv()
+        products(PIECES_A[part], grad_a, z, za_sib, 0)
+        sum_a.start(0, part)
+    swaps[8].wait_recv()
+    hnow[0] = head_g[...] + hnow[3]
+    moving = heads_go(0)
     load.wait()
     for i in range(4):
         rows = slice(256 * i, 256 * i + 256)
@@ -757,7 +864,7 @@
     x = x_ref[...].astype(F32)
     part, gain_grad = rms_back(x, row_scale(x), gin[...], df_s[...])
     gin_g[...] = gain_grad
-    dx[...] = x1_s[...] + part
+    dx[...] = dx1_s[...] + part
 
     small_rows = small.reshape(1024, 128)
     small_rows[...] = jnp.zeros((1024, 128), F32)
@@ -770,18 +877,13 @@
 
 
     swap(7, small.at[:, 1 - core], small_sib)
-    swaps[8].wait_recv()
-    hnow[0] = head_g[...] + hnow[3]
-    moving = heads_go(0)
-    for part in range(3):
-        swaps[4 + part].wait_recv()
-        products(PIECES_A[part], grad_a, z, za_sib, 0)
-        if part == 2:
-            swaps[7].wait_recv()
-            tile = grad_a.at[:, :, :, :, pl.ds(4096, 128)]
-            extra = small[:, core] + small_sib[...]
-            tile[...] = (tile[...].astype(F32) + extra.reshape(4, 4, 4, 8, 128)).astype(BF16)
-        sum_a.start(0, part)
+    swaps[6].wait_recv()
+    products(PIECES_A[2], grad_a, z, za_sib, 0)
+    swaps[7].wait_recv()
+    tile = grad_a.at[:, :, :, :, pl.ds(4096, 128)]
+    extra = small[:, core] + small_sib[...]
+    tile[...] = (tile[...].astype(F32) + extra.reshape(4, 4, 4, 8, 128)).astype(BF16)
+    sum_a.start(0, 2)
     sum_b.finish(0)
     hnow[1] = heads_come(0, moving)
     moving = heads_go(1)
@@ -792,12 +894,10 @@
     moving = heads_go(2)
     sum_b.finish(1)
     sum_a.middle(1)
-    sum_b.middle(2)
     sum_a.finish(1)
-    sum_b.finish(2)
+    sum_b.last()
     head_out[...] = heads_come(2, moving)
-    sum_a.middle(2)
-    sum_a.finish(2)
+    sum_a.last()
     sum_a.drain()
     sum_b.drain()
     for c in list(swaps.values()) + head_sent:
@@ -810,7 +910,7 @@
 
 def buffers(parts):
     return [pltpu.VMEM(shapes_of(phase, n), BF16) for c0, lo, hi in parts for phase in range(3)
-            for n in (lo, hi, lo + hi, lo + hi)]
+            for n in ((lo, hi, lo + hi, lo + hi) if phase < 2 else (lo + hi, lo + hi, lo + hi, 128))]
 
 
 def backward_call(*args):
@@ -820,16 +920,16 @@
     second = COLS - FIRST
     return pl.pallas_call(
         backward_kernel,
-        out_shape=[of(128, 1024), of(8, COLS), of(8, 128)],
-        in_specs=[vm] * 12 + [hbm] * 9,
-        out_specs=[vm] * 3,
-        scratch_shapes=[pltpu.VMEM(s, F32) for _, s in SAVED] + [
+        out_shape=[of(128, 1024, t=BF16), of(128, 1024), of(8, COLS), of(8, 128)],
+        in_specs=[vm] * 7 + [hbm] * 15,
+        out_specs=[vm] * 4,
+        scratch_shapes=[pltpu.VMEM(s, t) for s, t in zip(SAVED, KINDS)] + [
             pltpu.VMEM((1024, FIRST), BF16), pltpu.VMEM((128, FIRST), BF16), pltpu.VMEM((128, 1024), F32),
-            pltpu.VMEM((128, 1792), F32), pltpu.VMEM((128, 128), F32), pltpu.VMEM((1, 1024), F32), pltpu.VMEM((1, 1536), F32),
+            pltpu.VMEM((128, 1536), F32), pltpu.VMEM((128, 512), F32), pltpu.VMEM((128, 1792), F32), pltpu.VMEM((128, 128), F32), pltpu.VMEM((1, 1024), F32), pltpu.VMEM((1, 1536), F32),
             pltpu.VMEM((4, 1792), F32), pltpu.VMEM((1, 1792), F32), pltpu.VMEM((16, 2, 32, 128), F32),
             pltpu.VMEM((8, 128), F32), pltpu.VMEM((4, 4, 4, 8, FIRST), BF16), pltpu.VMEM((4, 4, 4, 8, second), BF16),
             pltpu.VMEM((128, second), BF16), pltpu.VMEM((128, FIRST), BF16), pltpu.VMEM((4, 16, 32, 128), BF16),
-            pltpu.VMEM((16, 32, 128), F32), pltpu.SemaphoreType.DMA, pltpu.SemaphoreType.DMA((8,)),
+            pltpu.VMEM((16, 32, 128), F32), pltpu.SemaphoreType.DMA((2,)), pltpu.SemaphoreType.DMA((20,)),
             pltpu.SemaphoreType.DMA((9,)), pltpu.SemaphoreType.DMA((9,)),
             pltpu.VMEM((4, 8, 128), F32), pltpu.VMEM((3, 4, 8, 128), F32),
             pltpu.SemaphoreType.DMA((3, 3)), pltpu.SemaphoreType.DMA((3, 3)),
@@ -843,11 +943,17 @@
 SPLIT = ("gate", "inner", "query", "keyval", "mix", "attn", "gateup", "down")
 
 
-def split_kernel(grads, head, *outs):
+def split_kernel(grads, head, result_in, dx_in, *outs):
+    outs[17][...] = result_in[...]
+    outs[18][...] = dx_in[...]
+    for src, dst in GATEUP:
+        outs[6][:, src:src + 1024] = grads[:, dst:dst + 1024]
     for name, dst in zip(SPLIT, outs[:8]):
+        if name == "gateup":
+            continue
         start, n = OFF[name]
         dst[...] = grads[:, start:start + n]
-    step, gin, gffn, gmix, cbias, taps, bias, decay, skip = outs[8:]
+    step, gin, gffn, gmix, cbias, taps, bias, decay, skip = outs[8:17]
     tile = grads[:, 4096:4224]
     step[...] = tile[:, 0:24]
     gin[...] = tile[0:1, AT_IN:AT_IN + 8]
@@ -859,18 +965,19 @@
         dst[...] = head[r:r + 1, 0:24]
 
 
-def split_call(grads, head):
+def split_call(grads, head, result, dx):
     def of(*s):
         return jax.ShapeDtypeStruct(s, F32)
     vm = pl.BlockSpec(memory_space=pltpu.VMEM)
     return pl.pallas_call(
         split_kernel,
         out_shape=[of(8, OFF[k][1]) for k in SPLIT] + [of(8, 24), of(1, 8), of(1, 8), of(1, 12), of(1, 14), of(4, 14),
-                                                       of(1, 24), of(1, 24), of(1, 24)],
-        in_specs=[vm] * 2,
-        out_specs=[vm] * 17,
+                                                       of(1, 24), of(1, 24), of(1, 24),
+                                                       jax.ShapeDtypeStruct((128, 1024), BF16), of(128, 1024)],
+        in_specs=[vm] * 4,
+        out_specs=[vm] * 19,
         name="split",
-    )(grads, head)
+    )(grads, head, result, dx)
 
 
 def body(tokens, seq_lengths, seq_owner, input_norm, gate_proj, inner_proj, step_proj, conv_weight, conv_bias, step_bias,
@@ -880,10 +987,9 @@
                         query_proj[0], keyval_proj[0], attn_out[0].T, input_norm, ffn_norm, gateup_proj[0], down_proj[0].T,
                         tokens, out_grad, seq_lengths.reshape(1, 256), seq_owner.reshape(1, 256), step_bias, decay_log,
                         skip_gain)
-    weights, result, rt = made[:3]
-    dx, grads, heads = backward_call(tokens, rt.reshape(4, 16, 2, 32, 128), *made[3:13], weights, *made[13:])
-    (gate, inner, query, keyval, mix, attn, gateup, down, step, gin, gffn, gmix, cbias, taps, bias, decay,
-     skip) = split_call(grads, heads)
+    result, dx, grads, heads = backward_call(tokens, *made[1:7], made[0], made[7], made[8], *made[9:])
+    (gate, inner, query, keyval, mix, attn, gateup, down, step, gin, gffn, gmix, cbias, taps, bias, decay, skip, result,
+     dx) = split_call(grads, heads, result, dx)
     return (result, dx, gin, gate[None], inner[None], step[None], taps[None], cbias, bias, decay, skip, gmix, mix.T[None],
             query[None], keyval[None], attn.T[None], gffn, gateup[None], down.T[None])
 

time: 162 us -> 152 us (0.938)
  Pallas kernels: 158 us -> 151 us
  local copies, waits for them, and re-layouts: 2.59 us -> 0 us
    pallas_call x1, Pallas kernels: 85.1 us -> 81.7 us  [forward_call(): pl.pallas_call(forward_kernel, out_shape=[of(4, 4, 2, 4, 8, COLS, t=BF16)...]
    pallas_call x1, Pallas kernels: 70.6 us -> 67.2 us  [backward_call(): pl.pallas_call(backward_kernel, out_shape=[of(128, 1024, t=BF16), of(128,...]
    unnamed x4 -> x0, local copies, waits for them, and re-layouts: 2.59 us -> none
where the time goes in v4:
time: 152 us
  Pallas kernels  151 us (99%)
    pallas_call x1, Pallas kernels, forward_call(): pl.pallas_call(forward_kernel, out_shape=[of(4, 4, 2, 4, 8, COLS, t=BF16)...  81.7 us
    pallas_call x1, Pallas kernels, backward_call(): pl.pallas_call(backward_kernel, out_shape=[of(128, 1024, t=BF16), of(128,...  67.2 us

profile of v4, /device:TPU:0, one launch (start us, length us, event | category | flops | bytes accessed | tf_op | source)
XLA Modules:
  0.0 152.1 jit_solution(6398808171162314044)
XLA Ops:
  0.7 81.7 %forward.1 = (bf16[4,4,2,4,8,12416]{5,4,3,2,1,0:T(8,128)(2,1)}, f32[1,1024]{1,0:T(1,128)}, f32[1,1024]{1,0:T(1,128)}, f32[1,1536]{1,0:T(1,128)}, f32[4,1792]{1,0...) custom-call(bf16[8,1536]{1,0:T(8,128)(2,1)} %bitcast.37, ...), custom_call_target="tpu_custom_call" | custom-call | tf_op jit(solution)/shard_map/forward/pallas_call | solution.py:605
  82.4 67.2 %backward.1 = (bf16[128,1024]{1,0:T(8,128)(2,1)}, f32[128,1024]{1,0:T(8,128)}, f32[8,12416]{1,0:T(8,128)}, f32[8,128]{1,0:T(8,128)}) custom-call(bf16[128,1024]{1,0:T(8,128)(2,1)} %x_ref.1, f32[1,1024]{1,0:T(1,128)} %get-tuple-element.63.gffn_g, f32[1,1024]{1,0:T(1,128)} %get-tuple-element.64.gin, f32[1,1536]{1,0:T(1,128)} %get-tuple-element.65.gmix, ...), custom_call_target="tpu_custom_call" | custom-call | tf_op jit(solution)/shard_map/backward/pallas_call | solution.py:921
  149.6 2.3 %split.1 = (f32[8,1536]{1,0:T(8,128)}, f32[8,1792]{1,0:T(8,128)}, f32[8,512]{1,0:T(8,128)}, f32[8,256]{1,0:T(8,128)}, f32[8,1536]{1,0:T(8,128)}, /*index=5*/f32[...) custom-call(f32[8,12416]{1,0:T(8,128)} %get-tuple-element.84.grads, ...), custom_call_target="tpu_custom_call" | custom-call | tf_op jit(solution)/shard_map/split/pallas_call | solution.py:972

commit v5 on v4

--- a/solution.py
+++ b/solution.py
@@ -309,9 +309,10 @@
 
 
 GROUPS = ((0, FIRST), (FIRST, 4096), (8320, 2048), (10368, 2048))
-SAVED = ((128, FIRST), (128, 1792), (128, 1792), (128, 1536), (24, 128, 128), (8, 128, 128), (128, 512), (9, 128, 128),
+SAVED = ((128, FIRST), (128, 1792), (128, 1792), (128, 1536), (8, 128), (8, 128, 128), (128, 512), (10, 128, 128),
          (128, 1024), (128, 1024), (128, COLS - FIRST), (4096, 128))
 KINDS = (F32,) * 10 + (BF16,) * 2
+MADE_AGAIN = (2, 4)
 
 
 def forward_kernel(*refs):
@@ -447,6 +448,15 @@
         return carry
     lax.fori_loop(0, 14, convolve, 0)
 
+    keeps = []
+
+    def keep(*which):
+        for k in which:
+            c = pltpu.make_async_copy(refs[42 + k], kept[k], keep_sem.at[k])
+            c.start()
+            keeps.append(c)
+    keep(0, 1)
+
     step = proj[:, 4096:4224] + sbias
     dt = jnp.maximum(step, 0.0) + jnp.log(1.0 + jnp.exp(-jnp.abs(step)))
     rate = -jnp.exp(dlog)
@@ -465,7 +475,6 @@
         for n in (2 * t, 2 * t + 1):
             spread = jnp.where(allowed, level[:, n:n + 1] - level_t[n:n + 1, :], -1e30)
             decay = jnp.exp(spread)
-            dec[n] = decay
             mixes.append((decay * inter * dt_t[n:n + 1, :]).astype(BF16))
         xs = conv[:, cs]
         y = nn(jnp.concatenate(mixes, axis=1), stacked(xs)) + skipx[:, cs] * xs
@@ -482,7 +491,6 @@
         for n in (2 * t, 2 * t + 1):
             spread = jnp.where(allowed, level[:, n:n + 1] - level_t[n:n + 1, :], -1e30)
             decay = jnp.exp(spread)
-            dec[n] = decay
             mixes.append((decay * inter * dt_t[n:n + 1, :]).astype(BF16))
         xs = conv[:, cs]
         y = nn(jnp.concatenate(mixes, axis=1), stacked(xs)) + skipx[:, cs] * xs
@@ -501,6 +509,8 @@
     lax.fori_loop(0, 12, mixer_norm, 0)
 
     four.forward(2)
+    keep(3)
+
     first = (lane % 64) < 32
 
     def turn(v, sign):
@@ -528,16 +538,9 @@
             weights.append(w.astype(BF16))
         zb[:, 1536 + 128 * t:1664 + 128 * t] = nn(jnp.concatenate(weights, axis=1), stacked(vals[t // 2])).astype(BF16)
 
-    for k, v in enumerate((key_t, val, dt, step, inter, jnp.broadcast_to(rmix, (128, 128)), position, cosine, sine)):
+    for k, v in enumerate((key_t, val, dt, step, inter, jnp.broadcast_to(rmix, (128, 128)), position, cosine, sine, level)):
         misc[k] = v
-    keeps = []
-
-    def keep(*which):
-        for k in which:
-            c = pltpu.make_async_copy(refs[42 + k], kept[k], keep_sem.at[k])
-            c.start()
-            keeps.append(c)
-    keep(0, 1, 2, 3, 4, 5, 6, 7)
+    keep(5, 6, 7)
     swap_columns(4, 0)
     two.shared()
     loads = [load(1, 4224, 4096)]
@@ -564,8 +567,11 @@
     for k, g in enumerate((three, four)):
         base = 8320 + 2048 * k
         g.shared()
-        load(2 + k, base, 2048).wait()
+        pieces_of = [[load(2 + 4 * k + 2 * e + o, base + 512 * e + 1024 * o, 512) for o in (0, 1)] for e in (0, 1)]
         for i in range(4):
+            if i % 2 == 0:
+                for c in pieces_of[i // 2]:
+                    c.wait()
             gate = nn(f, wv[:, base + 256 * i:base + 256 * i + 256])
             up = nn(f, wv[:, base + 1024 + 256 * i:base + 1280 + 256 * i])
             da = da_s[:, 1024 * k + 256 * i:1024 * k + 256 * i + 256]
@@ -606,7 +612,7 @@
         forward_kernel,
         out_shape=[of(4, 4, 2, 4, 8, COLS, t=BF16), of(1, 1024), of(1, 1024), of(1, 1536),
                    of(4, 1792), of(1, 1536), of(8, 128), of(128, COLS - FIRST, t=BF16), of(4, 16, 32, 128, t=BF16)]
-        + [of(*s, t=t) for s, t in zip(SAVED, KINDS)],
+        + [of(*((8, 128) if k in MADE_AGAIN else s), t=t) for k, (s, t) in enumerate(zip(SAVED, KINDS))],
         in_specs=[vm] * 21,
         out_specs=[hbm] + [vm] * 6 + [hbm] * 14,
         scratch_shapes=[pltpu.VMEM(s, t) for s, t in zip(SAVED, KINDS)] + [
@@ -647,7 +653,7 @@
         cs = pl.ds(c0 - FIRST, lo + hi)
         columns.append((bring(14 + part, kept[10].at[:, cs], zb.at[:, cs]),
                         bring(17 + part, zb_sib_in.at[:, cs], zb_sib.at[:, cs])))
-    keeps = [bring(k, kept[k], refs[16 + k]) for k in range(10)]
+    keeps = [bring(k, kept[k], refs[16 + k]) for k in range(10) if k not in MADE_AGAIN]
     rows_of_w = w.reshape(1024, COLS)
     load = pltpu.make_async_copy(rows_of_w.at[:, pl.ds(FIRST, 4096)], wv.at[:, pl.ds(0, 4096)], wsem.at[0])
     load.start()
@@ -733,8 +739,17 @@
         result[:, rows] = (x1_s[:, rows] + nt(zb[:, 2048:4096], wv[rows, 2048:4096])).astype(BF16)
     load = pltpu.make_async_copy(rows_of_w.at[:, pl.ds(0, FIRST)], wv, wsem.at[1])
     load.start()
-    key_t, val, dt, step, inter, rmix, position, cosine, sine = [misc[k] for k in range(9)]
+    key_t, val, dt, step, inter, rmix, position, cosine, sine, level = [misc[k] for k in range(10)]
     rmix = rmix[:, 0:1]
+    level_t = level.T
+    allowed = (sub >= lane) & (lane.astype(F32) >= sub.astype(F32) - position)
+
+    def convolved(i, carry):
+        cs = cols_of(i, 128)
+        total = csum[:, cs]
+        conv[:, cs] = total * sigmoid(total)
+        return carry
+    lax.fori_loop(0, 14, convolved, 0)
     first = (lane % 64) < 32
 
     def turn(v, sign):
@@ -807,7 +822,7 @@
         for e in (0, 1):
             n = 2 * t + e
             dt_row = dt_t[n:n + 1, :]
-            decay = dec[n]
+            decay = jnp.exp(jnp.where(allowed, level[:, n:n + 1] - level_t[n:n + 1, :], -1e30))
             mixed = decay * inter
             dm = dmix[128 * e:128 * e + 128]
             mixes.append((mixed * dt_row).astype(BF16))

time: 152 us -> 152 us (level)
  no operation moved by 1% of the time
where the time goes in v5:
time: 152 us
  Pallas kernels  151 us (99%)
    pallas_call x1, Pallas kernels, forward_call(): pl.pallas_call(forward_kernel, out_shape=[of(4, 4, 2, 4, 8, COLS, t=BF16)...  81.1 us
    pallas_call x1, Pallas kernels, backward_call(): pl.pallas_call(backward_kernel, out_shape=[of(128, 1024, t=BF16), of(128,...  67.3 us

profile of v5, /device:TPU:0, one launch (start us, length us, event | category | flops | bytes accessed | tf_op | source)
XLA Modules:
  0.0 151.5 jit_solution(7111156302041824839)
XLA Ops:
  0.7 81.1 %forward.1 = (bf16[4,4,2,4,8,12416]{5,4,3,2,1,0:T(8,128)(2,1)}, f32[1,1024]{1,0:T(1,128)}, f32[1,1024]{1,0:T(1,128)}, f32[1,1536]{1,0:T(1,128)}, f32[4,1792]{1,0...) custom-call(bf16[8,1536]{1,0:T(8,128)(2,1)} %bitcast.37, ...), custom_call_target="tpu_custom_call" | custom-call | tf_op jit(solution)/shard_map/forward/pallas_call | solution.py:611
  81.8 67.3 %backward.1 = (bf16[128,1024]{1,0:T(8,128)(2,1)}, f32[128,1024]{1,0:T(8,128)}, f32[8,12416]{1,0:T(8,128)}, f32[8,128]{1,0:T(8,128)}) custom-call(bf16[128,1024]{1,0:T(8,128)(2,1)} %x_ref.1, f32[1,1024]{1,0:T(1,128)} %get-tuple-element.63.gffn_g, f32[1,1024]{1,0:T(1,128)} %get-tuple-element.64.gin, f32[1,1536]{1,0:T(1,128)} %get-tuple-element.65.gmix, ...), custom_call_target="tpu_custom_call" | custom-call | tf_op jit(solution)/shard_map/backward/pallas_call | solution.py:936
  149.1 2.3 %split.1 = (f32[8,1536]{1,0:T(8,128)}, f32[8,1792]{1,0:T(8,128)}, f32[8,512]{1,0:T(8,128)}, f32[8,256]{1,0:T(8,128)}, f32[8,1536]{1,0:T(8,128)}, /*index=5*/f32[...) custom-call(f32[8,12416]{1,0:T(8,128)} %get-tuple-element.84.grads, ...), custom_call_target="tpu_custom_call" | custom-call | tf_op jit(solution)/shard_map/split/pallas_call | solution.py:987
